TPU v7x, 32 devices: a whole 2x2x4 slice. The times are simulated.
32 devices in a mesh: pipe: 2 (over core), dp: 16 (over z, y, x).
Axes of the slice: x: 2, y: 2, z: 4, core: 2. Of those that a mesh axis runs over, the one named last changes fastest.
Arguments:
- images: bfloat16 [2, 16, 196, 216], P(None, 'dp'), may hold values from -32 to 32
- codes: int32 [2, 4], replicated, may hold values from 0 to 2, as said below
- cotangent: bfloat16 [2, 16, 196, 216], P(None, 'dp'), may hold values from -5 to 5
- expand_weight: bfloat16 [216, 1296], replicated, may hold values from -0.4375 to 0.4375
- batch_gain: float32 [1296], replicated, may hold values from 0.5 to 1.5
- batch_bias: float32 [1296], replicated, may hold values from -3 to 3
- depth_one: float32 [9, 1296], replicated, may hold values from -2 to 2
- squeeze_weight: bfloat16 [1296, 324], replicated, may hold values from -0.3125 to 0.3125
- squeeze_bias: float32 [324], replicated, may hold values from -3 to 3
- excite_weight: bfloat16 [324, 1296], replicated, may hold values from -0.3125 to 0.3125
- excite_bias: float32 [1296], replicated, may hold values from -3 to 3
- project_weight: bfloat16 [1296, 216], replicated, may hold values from -0.3125 to 0.3125
- norm_gain: float32 [216], replicated, may hold values from 0.5 to 1.5
- norm_bias: float32 [216], replicated, may hold values from -2 to 2
- qkv_weight: bfloat16 [216, 648], replicated, may hold values from -0.4375 to 0.4375
- talk_before: float32 [12, 12], replicated, may hold values from -3 to 3
- talk_after: float32 [12, 12], replicated, may hold values from -3 to 3
- output_weight: bfloat16 [216, 216], replicated, may hold values from -3 to 3
- output_bias: float32 [216], replicated, may hold values from -2 to 2
- mlp_gain: float32 [216], replicated, may hold values from 0.5 to 1.5
- mlp_bias: float32 [216], replicated, may hold values from -2 to 2
- hidden_weight: bfloat16 [216, 864], replicated, may hold values from -0.4375 to 0.4375
- hidden_bias: float32 [864], replicated, may hold values from -2 to 2
- depth_two: float32 [9, 864], replicated, may hold values from -2 to 2
- return_weight: bfloat16 [864, 216], replicated, may hold values from -0.625 to 0.625
- return_bias: float32 [216], replicated, may hold values from -2 to 2
Outputs:
- activations: bfloat16 [2, 2, 16, 196, 216], P('pipe', None, 'dp')
- input_grads: float32 [2, 2, 16, 196, 216], P('pipe', None, 'dp')
- expand_weight_grad: float32 [216, 1296], replicated
- batch_gain_grad: float32 [1296], replicated
- batch_bias_grad: float32 [1296], replicated
- depth_one_grad: float32 [9, 1296], replicated
- squeeze_weight_grad: float32 [1296, 324], replicated
- squeeze_bias_grad: float32 [324], replicated
- excite_weight_grad: float32 [324, 1296], replicated
- excite_bias_grad: float32 [1296], replicated
- project_weight_grad: float32 [1296, 216], replicated
- norm_gain_grad: float32 [216], replicated
- norm_bias_grad: float32 [216], replicated
- qkv_weight_grad: float32 [216, 648], replicated
- talk_before_grad: float32 [12, 12], replicated
- talk_after_grad: float32 [12, 12], replicated
- output_weight_grad: float32 [216, 216], replicated
- output_bias_grad: float32 [216], replicated
- mlp_gain_grad: float32 [216], replicated
- mlp_bias_grad: float32 [216], replicated
- hidden_weight_grad: float32 [216, 864], replicated
- hidden_bias_grad: float32 [864], replicated
- depth_two_grad: float32 [9, 864], replicated
- return_weight_grad: float32 [864, 216], replicated
- return_bias_grad: float32 [216], replicated
Inputs may be any that keep to these rules, and one draw needn't show every extreme that they name: `codes`: each of the four columns holds 2 in at least one micro-batch.
All inputs are finite; a program needn't handle non-finite values.
Results may differ from a plain program's by a relative error of at most 0.017.
The roundings to bfloat16 on the way count: a program that leaves them out, or rounds other values in their place, can miss the bound.
Values may be sent and summed in bfloat16 or wider, within the bound.
No kernel may reach another device: no remote copies, remote signals or barrier semaphores. Data moves between devices by JAX's collectives and lax.ppermute only.
A program may use at most 128 MiB of HBM per device.

v0:
```python
import jax
import jax.numpy as jnp
from jax import lax
from jax.sharding import PartitionSpec as P

D = 216
E = 1296
HEADS = 12
HD = 18
F = 864
MICRO = 2
SIDE = 14
PIX = 196


highest = lax.Precision.HIGHEST
epsilon = 1e-05


def passed_along(value, axis, steps):
    count = lax.axis_size(axis)
    initial, last = (max(0, -steps), min(count, count - steps))
    return lax.ppermute(value, axis, [(source, source + steps) for source in range(initial, last)])


def pixel_mask(image_side):
    positions = jnp.arange(SIDE * SIDE)
    inside = (positions // SIDE < image_side) & (positions % SIDE < image_side)
    return inside.astype(jnp.float32)


def code_masks(subnet_code):
    image_side = SIDE - 4 + 2 * subnet_code[3]
    pixels = pixel_mask(image_side)
    channel_mask = (jnp.arange(E) < E - (2 - subnet_code[0]) * D).astype(jnp.float32)
    head_mask = (jnp.arange(HEADS) < HEADS - 2 * (2 - subnet_code[1])).astype(jnp.float32)
    unit_mask = (jnp.arange(F) < F - (2 - subnet_code[2]) * D).astype(jnp.float32)
    return (image_side, pixels, channel_mask, head_mask, unit_mask)


def depthwise(fields, kernel):
    amount = fields.shape[0]
    channels = fields.shape[-1]
    squares = fields.reshape(amount, SIDE, SIDE, channels)
    padded = jnp.pad(squares, ((0, 0), (1, 1), (1, 1), (0, 0)))
    summed = jnp.zeros(squares.shape, fields.dtype)
    for vertical in range(3):
        for lateral in range(3):
            summed = (
                summed
                + padded[:, vertical : vertical + SIDE, lateral : lateral + SIDE, :]
                * kernel[3 * vertical + lateral]
            )
    return summed.reshape(amount, SIDE * SIDE, channels)


def layer_norm(values, gain_vector, bias_vector):
    centred = values - jnp.mean(values, axis=-1, keepdims=True)
    variance = jnp.mean(centred * centred, axis=-1, keepdims=True)
    return centred * lax.rsqrt(variance + epsilon) * gain_vector + bias_vector


def batch_moments(first_sum, second_sum, token_count):
    average = first_sum / token_count
    variance = second_sum / token_count - average * average
    return (average, lax.rsqrt(variance + epsilon))


def only_where(predicate, action, operands):

    def nothing(*inputs):
        return jax.tree.map(jnp.zeros_like, action(*inputs))

    return lax.cond(predicate, action, nothing, *operands)


def excite_block(
    expanded,
    average,
    inverse,
    gain_vector,
    bias_vector,
    kernel,
    squeeze_matrix,
    squeeze_shift,
    excite_matrix,
    excite_shift,
    pixels,
    channel_mask,
    image_side,
):
    normed = (expanded - average) * inverse * gain_vector + bias_vector
    activated = jax.nn.silu(normed) * channel_mask * pixels[:, None]
    deepened = depthwise(activated, kernel) * pixels[:, None]
    pooled = jnp.sum(deepened, axis=1) / (image_side * image_side).astype(jnp.float32)
    squeezed = jax.nn.silu(jnp.dot(pooled, squeeze_matrix, precision=highest) + squeeze_shift)
    excite = jax.nn.sigmoid(jnp.dot(squeezed, excite_matrix, precision=highest) + excite_shift)
    return deepened * excite[:, None, :]


def mlp_middle(hidden_pre, kernel, pixels, unit_mask):
    hidden = hidden_pre * unit_mask * pixels[:, None]
    return jax.nn.silu(depthwise(hidden, kernel) * pixels[:, None])


def attend_forward(queries, key_rows, value_rows, before_mix, after_mix, live_keys):
    score_scale = HD ** (-0.5)
    scores = (
        jnp.einsum("hpc,hqc->hpq", queries, key_rows, preferred_element_type=jnp.float32)
        * score_scale
    )
    mixture = jnp.einsum("hg,gpq->hpq", before_mix, scores, precision=highest)
    mixture = jnp.where(live_keys, mixture, -1000000000.0)
    top_score = jnp.max(mixture, axis=-1, keepdims=True)
    logsum = top_score + jnp.log(jnp.sum(jnp.exp(mixture - top_score), axis=-1, keepdims=True))
    softmaxed = jnp.exp(mixture - logsum)
    blended = jnp.einsum("hg,gpq->hpq", after_mix, softmaxed, precision=highest).astype(
        jnp.bfloat16
    )
    result = jnp.einsum("hpq,hqc->hpc", blended, value_rows, preferred_element_type=jnp.float32)
    return (result, logsum[..., 0])


def attend_backward(
    queries, key_rows, value_rows, logsum, grad_out, before_mix, after_mix, live_keys
):
    score_scale = HD ** (-0.5)
    scores = (
        jnp.einsum("hpc,hqc->hpq", queries, key_rows, preferred_element_type=jnp.float32)
        * score_scale
    )
    mixture = jnp.einsum("hg,gpq->hpq", before_mix, scores, precision=highest)
    mixture = jnp.where(live_keys, mixture, -1000000000.0)
    softmaxed = jnp.exp(mixture - logsum[..., None])
    blended = jnp.einsum("hg,gpq->hpq", after_mix, softmaxed, precision=highest).astype(
        jnp.bfloat16
    )
    grad_values = jnp.einsum("hpq,hpc->hqc", blended, grad_out, preferred_element_type=jnp.float32)
    grad_blend = jnp.einsum(
        "hpc,hqc->hpq", grad_out, value_rows, preferred_element_type=jnp.float32
    )
    grad_after = jnp.einsum("hpq,gpq->hg", grad_blend, softmaxed, precision=highest)
    grad_soft = jnp.einsum("hg,hpq->gpq", after_mix, grad_blend, precision=highest)
    grad_mixture = softmaxed * (grad_soft - jnp.sum(softmaxed * grad_soft, axis=-1, keepdims=True))
    grad_before = jnp.einsum("hpq,gpq->hg", grad_mixture, scores, precision=highest)
    grad_scores = jnp.einsum("hg,hpq->gpq", before_mix, grad_mixture, precision=highest).astype(
        jnp.bfloat16
    )
    grad_queries = (
        jnp.einsum("hpq,hqc->hpc", grad_scores, key_rows, preferred_element_type=jnp.float32)
        * score_scale
    )
    grad_keys = (
        jnp.einsum("hpq,hpc->hqc", grad_scores, queries, preferred_element_type=jnp.float32)
        * score_scale
    )
    return (grad_queries, grad_keys, grad_values, grad_before, grad_after)


def on_device(
    images,
    codes,
    cotangent,
    expand_weight,
    batch_gain,
    batch_bias,
    depth_one,
    squeeze_weight,
    squeeze_bias,
    excite_weight,
    excite_bias,
    project_weight,
    norm_gain,
    norm_bias,
    qkv_weight,
    talk_before,
    talk_after,
    output_weight,
    output_bias,
    mlp_gain,
    mlp_bias,
    hidden_weight,
    hidden_bias,
    depth_two,
    return_weight,
    return_bias,
):
    leading = lax.axis_index("pipe") == 0
    trailing = jnp.logical_not(leading)
    images_dev = images.shape[1]
    row_count = images_dev * PIX
    devices_dp = lax.axis_size("dp")
    squeeze_full = squeeze_weight.astype(jnp.float32)
    excite_full = excite_weight.astype(jnp.float32)
    one_small = (
        batch_gain,
        batch_bias,
        depth_one,
        squeeze_full,
        squeeze_bias,
        excite_full,
        excite_bias,
    )

    def counted(image_side):
        return (images_dev * devices_dp * image_side * image_side).astype(jnp.float32)

    def one_pre(images_mb, pixels):
        masked = images_mb * pixels[None, :, None].astype(jnp.bfloat16)
        expanded = jnp.dot(
            masked.reshape(row_count, D), expand_weight, preferred_element_type=jnp.float32
        )
        return (masked, expanded, jnp.sum(expanded, axis=0), jnp.sum(expanded * expanded, axis=0))

    def one_post(masked, expanded, first_sum, second_sum, subnet_code):
        image_side, pixels, channel_mask, head_mask, unit_mask = code_masks(subnet_code)
        average, inverse = batch_moments(first_sum, second_sum, counted(image_side))
        scaled = excite_block(
            expanded.reshape(images_dev, PIX, E),
            average,
            inverse,
            *one_small,
            pixels,
            channel_mask,
            image_side
        ).astype(jnp.bfloat16)
        branch = jnp.dot(
            scaled.reshape(row_count, E), project_weight, preferred_element_type=jnp.float32
        )
        handed = masked.reshape(row_count, D).astype(jnp.float32) + branch
        return handed.astype(jnp.bfloat16).reshape(images_dev, PIX, D)

    def split_heads(projected, head_mask):
        pieces = projected.reshape(images_dev, PIX, 3, HEADS, HD).transpose(2, 0, 3, 1, 4)
        values_in = pieces[2] * head_mask[None, :, None, None].astype(jnp.bfloat16)
        return (pieces[0], pieces[1], values_in)

    def two_forward(received, subnet_code):
        image_side, pixels, channel_mask, head_mask, unit_mask = code_masks(subnet_code)
        handed = received.astype(jnp.float32)
        normed_one = layer_norm(handed, norm_gain, norm_bias).astype(jnp.bfloat16)
        projected = jnp.dot(
            normed_one.reshape(row_count, D), qkv_weight, preferred_element_type=jnp.float32
        ).astype(jnp.bfloat16)
        queries, key_rows, values_in = split_heads(projected, head_mask)
        before_mix = talk_before * head_mask
        after_mix = talk_after * head_mask
        live_keys = pixels > 0.5
        outcomes, logsums = lax.map(
            lambda triple: attend_forward(
                triple[0], triple[1], triple[2], before_mix, after_mix, live_keys
            ),
            (queries, key_rows, values_in),
        )
        heads_out = outcomes.transpose(0, 2, 1, 3).reshape(row_count, D).astype(jnp.bfloat16)
        attended = (
            jnp.dot(heads_out, output_weight, preferred_element_type=jnp.float32) + output_bias
        ).reshape(images_dev, PIX, D) * pixels[:, None]
        middle = handed + attended
        normed_two = layer_norm(middle, mlp_gain, mlp_bias).astype(jnp.bfloat16)
        hidden_pre = (
            jnp.dot(
                normed_two.reshape(row_count, D), hidden_weight, preferred_element_type=jnp.float32
            )
            + hidden_bias
        )
        activated = mlp_middle(
            hidden_pre.reshape(images_dev, PIX, F), depth_two, pixels, unit_mask
        ).astype(jnp.bfloat16)
        output = (
            jnp.dot(
                activated.reshape(row_count, F), return_weight, preferred_element_type=jnp.float32
            )
            + return_bias
        )
        final_out = (middle + output.reshape(images_dev, PIX, D)) * pixels[:, None]
        return (
            final_out.astype(jnp.bfloat16),
            (projected, heads_out, logsums, middle, hidden_pre, activated),
        )

    def two_backward(received, kept_state, cotangent_mb, subnet_code):
        projected, heads_out, logsums, middle, hidden_pre, activated = kept_state
        image_side, pixels, channel_mask, head_mask, unit_mask = code_masks(subnet_code)
        handed = received.astype(jnp.float32)
        upstream = (cotangent_mb.astype(jnp.float32) * pixels[:, None]).reshape(row_count, D)
        grad_return_bias = jnp.sum(upstream, axis=0)
        upstream_low = upstream.astype(jnp.bfloat16)
        grad_return_weight = jnp.einsum(
            "rf,rd->fd",
            activated.reshape(row_count, F),
            upstream_low,
            preferred_element_type=jnp.float32,
        )
        grad_activated = jnp.einsum(
            "rd,fd->rf", upstream_low, return_weight, preferred_element_type=jnp.float32
        )
        ignored, middle_pull = jax.vjp(
            lambda pre_values, kernel: mlp_middle(pre_values, kernel, pixels, unit_mask),
            hidden_pre.reshape(images_dev, PIX, F),
            depth_two,
        )
        grad_hidden_pre, grad_depth_two = middle_pull(grad_activated.reshape(images_dev, PIX, F))
        grad_hidden_pre = grad_hidden_pre.reshape(row_count, F)
        grad_hidden_bias = jnp.sum(grad_hidden_pre, axis=0)
        hidden_low = grad_hidden_pre.astype(jnp.bfloat16)
        normed_two, norm_two_pull = jax.vjp(layer_norm, middle, mlp_gain, mlp_bias)
        normed_two_low = normed_two.astype(jnp.bfloat16).reshape(row_count, D)
        grad_hidden_weight = jnp.einsum(
            "rd,rf->df", normed_two_low, hidden_low, preferred_element_type=jnp.float32
        )
        grad_normed_two = jnp.einsum(
            "rf,df->rd", hidden_low, hidden_weight, preferred_element_type=jnp.float32
        )
        grad_middle_part, grad_mlp_gain, grad_mlp_bias = norm_two_pull(
            grad_normed_two.reshape(images_dev, PIX, D)
        )
        grad_middle = upstream.reshape(images_dev, PIX, D) + grad_middle_part
        attend_up = (grad_middle * pixels[:, None]).reshape(row_count, D)
        grad_output_bias = jnp.sum(attend_up, axis=0)
        attend_low = attend_up.astype(jnp.bfloat16)
        grad_output_weight = jnp.einsum(
            "rd,re->de", heads_out, attend_low, preferred_element_type=jnp.float32
        )
        grad_heads = jnp.einsum(
            "re,de->rd", attend_low, output_weight, preferred_element_type=jnp.float32
        ).astype(jnp.bfloat16)
        grad_heads_split = grad_heads.reshape(images_dev, PIX, HEADS, HD).transpose(0, 2, 1, 3)
        queries, key_rows, values_in = split_heads(projected, head_mask)
        before_mix = talk_before * head_mask
        after_mix = talk_after * head_mask
        live_keys = pixels > 0.5

        def image_back(running, sample):
            grad_queries, grad_keys, grad_values, grad_before, grad_after = attend_backward(
                sample[0],
                sample[1],
                sample[2],
                sample[3],
                sample[4],
                before_mix,
                after_mix,
                live_keys,
            )
            return (
                (running[0] + grad_before, running[1] + grad_after),
                (grad_queries, grad_keys, grad_values),
            )

        empty_mix = jnp.zeros((HEADS, HEADS), jnp.float32)
        mix_grads, qkv_grads = lax.scan(
            image_back,
            (empty_mix, empty_mix),
            (queries, key_rows, values_in, logsums, grad_heads_split),
        )
        grad_values_masked = qkv_grads[2] * head_mask[None, :, None, None]
        grad_projected = (
            jnp.stack([qkv_grads[0], qkv_grads[1], grad_values_masked])
            .transpose(1, 3, 0, 2, 4)
            .reshape(row_count, 3 * D)
            .astype(jnp.bfloat16)
        )
        normed_one, norm_one_pull = jax.vjp(layer_norm, handed, norm_gain, norm_bias)
        normed_one_low = normed_one.astype(jnp.bfloat16).reshape(row_count, D)
        grad_qkv_weight = jnp.einsum(
            "rd,re->de", normed_one_low, grad_projected, preferred_element_type=jnp.float32
        )
        grad_normed_one = jnp.einsum(
            "re,de->rd", grad_projected, qkv_weight, preferred_element_type=jnp.float32
        )
        grad_handed_part, grad_norm_gain, grad_norm_bias = norm_one_pull(
            grad_normed_one.reshape(images_dev, PIX, D)
        )
        grad_handed = grad_middle + grad_handed_part
        gradients = (
            grad_norm_gain,
            grad_norm_bias,
            grad_qkv_weight,
            mix_grads[0] * head_mask,
            mix_grads[1] * head_mask,
            grad_output_weight,
            grad_output_bias,
            grad_mlp_gain,
            grad_mlp_bias,
            grad_hidden_weight,
            grad_hidden_bias,
            grad_depth_two,
            grad_return_weight,
            grad_return_bias,
        )
        return (grad_handed, gradients)

    def one_back_first(masked, expanded, first_sum, second_sum, grad_in, subnet_code):
        image_side, pixels, channel_mask, head_mask, unit_mask = code_masks(subnet_code)
        average, inverse = batch_moments(first_sum, second_sum, counted(image_side))

        def excite_piece(
            expanded_in,
            average_in,
            inverse_in,
            gain_in,
            bias_in,
            kernel_in,
            squeeze_in,
            squeeze_shift,
            excite_in,
            excite_shift,
        ):
            return excite_block(
                expanded_in,
                average_in,
                inverse_in,
                gain_in,
                bias_in,
                kernel_in,
                squeeze_in,
                squeeze_shift,
                excite_in,
                excite_shift,
                pixels,
                channel_mask,
                image_side,
            )

        scaled, excite_pull = jax.vjp(
            excite_piece, expanded.reshape(images_dev, PIX, E), average, inverse, *one_small
        )
        scaled_low = scaled.astype(jnp.bfloat16).reshape(row_count, E)
        grad_low = grad_in.reshape(row_count, D)
        grad_project_weight = jnp.einsum(
            "re,rd->ed", scaled_low, grad_low, preferred_element_type=jnp.float32
        )
        grad_scaled = jnp.einsum(
            "rd,ed->re", grad_low, project_weight, preferred_element_type=jnp.float32
        )
        pulled = excite_pull(grad_scaled.reshape(images_dev, PIX, E))
        return tuple(pulled) + (grad_project_weight,)

    def one_back_second(
        masked,
        expanded,
        first_sum,
        second_sum,
        grad_in,
        grad_expanded_part,
        grad_average,
        grad_inverse,
        subnet_code,
    ):
        image_side, pixels, channel_mask, head_mask, unit_mask = code_masks(subnet_code)
        token_count = counted(image_side)
        ignored, moment_pull = jax.vjp(
            lambda one_sum, two_sum: batch_moments(one_sum, two_sum, token_count),
            first_sum,
            second_sum,
        )
        grad_first, grad_second = moment_pull((grad_average, grad_inverse))
        grad_expanded = (
            grad_expanded_part.reshape(row_count, E) + grad_first + 2.0 * expanded * grad_second
        ).astype(jnp.bfloat16)
        grad_expand_weight = jnp.einsum(
            "rd,re->de",
            masked.reshape(row_count, D),
            grad_expanded,
            preferred_element_type=jnp.float32,
        )
        grad_masked = jnp.einsum(
            "re,de->rd", grad_expanded, expand_weight, preferred_element_type=jnp.float32
        )
        grad_images = (grad_in.reshape(row_count, D).astype(jnp.float32) + grad_masked).reshape(
            images_dev, PIX, D
        ) * pixels[:, None]
        return (grad_images, grad_expand_weight)

    one_kept = []
    two_kept = []
    first_acts = []
    final_acts = []
    for timestep in range(MICRO + 1):
        if timestep < MICRO:
            pixels_now = code_masks(codes[timestep])[1]
            masked, expanded, first_sum, second_sum = only_where(
                leading, one_pre, (images[timestep], pixels_now)
            )
            first_sum, second_sum = lax.psum((first_sum, second_sum), "dp")
            handed_out = only_where(
                leading, one_post, (masked, expanded, first_sum, second_sum, codes[timestep])
            )
            one_kept.append((masked, expanded, first_sum, second_sum))
            first_acts.append(handed_out)
        if timestep >= 1:
            final_out, kept_state = only_where(
                trailing, two_forward, (received, codes[timestep - 1])
            )
            two_kept.append((received, kept_state))
            final_acts.append(final_out)
        if timestep < MICRO:
            received = passed_along(handed_out, "pipe", 1)
    grads_one = None
    grads_two = None
    grads_back = []
    grads_images = []
    for timestep in range(MICRO + 1):
        if timestep < MICRO:
            grad_handed, step_two = only_where(
                trailing,
                two_backward,
                (
                    two_kept[timestep][0],
                    two_kept[timestep][1],
                    cotangent[timestep],
                    codes[timestep],
                ),
            )
            grads_two = (
                step_two if grads_two is None else jax.tree.map(jnp.add, grads_two, step_two)
            )
            grads_back.append(grad_handed)
        if timestep >= 1:
            earlier = timestep - 1
            masked, expanded, first_sum, second_sum = one_kept[earlier]
            pulled = only_where(
                leading,
                one_back_first,
                (masked, expanded, first_sum, second_sum, back_received, codes[earlier]),
            )
            grad_average, grad_inverse = lax.psum((pulled[1], pulled[2]), "dp")
            grad_images, grad_expand_weight = only_where(
                leading,
                one_back_second,
                (
                    masked,
                    expanded,
                    first_sum,
                    second_sum,
                    back_received,
                    pulled[0],
                    grad_average,
                    grad_inverse,
                    codes[earlier],
                ),
            )
            step_one = (grad_expand_weight,) + tuple(pulled[3:10]) + (pulled[10],)
            grads_one = (
                step_one if grads_one is None else jax.tree.map(jnp.add, grads_one, step_one)
            )
            grads_images.append(grad_images)
        if timestep < MICRO:
            back_received = passed_along(grad_handed.astype(jnp.bfloat16), "pipe", -1)
    activations = jnp.where(leading, jnp.stack(first_acts), jnp.stack(final_acts))[None]
    input_grads = jnp.where(leading, jnp.stack(grads_images), jnp.stack(grads_back))[None]
    grads_all = grads_one + grads_two
    summed = lax.psum(
        (
            grads_all[0],
            grads_all[1],
            grads_all[2],
            grads_all[3],
            grads_all[4],
            grads_all[5],
            grads_all[6],
            grads_all[7],
            grads_all[8],
            grads_all[9],
            grads_all[10],
            grads_all[11],
            grads_all[12],
            grads_all[13],
            grads_all[14],
            grads_all[15],
            grads_all[16],
            grads_all[17],
            grads_all[18],
            grads_all[19],
            grads_all[20],
            grads_all[21],
            grads_all[22],
        ),
        ("pipe", "dp"),
    )
    return (activations, input_grads, *summed)


def solution(mesh):
    in_specs = (
        P(None, "dp", None, None),
        P(),
        P(None, "dp", None, None),
        P(),
        P(),
        P(),
        P(),
        P(),
        P(),
        P(),
        P(),
        P(),
        P(),
        P(),
        P(),
        P(),
        P(),
        P(),
        P(),
        P(),
        P(),
        P(),
        P(),
        P(),
        P(),
        P(),
    )
    out_specs = (
        P("pipe", None, "dp", None, None),
        P("pipe", None, "dp", None, None),
        P(),
        P(),
        P(),
        P(),
        P(),
        P(),
        P(),
        P(),
        P(),
        P(),
        P(),
        P(),
        P(),
        P(),
        P(),
        P(),
        P(),
        P(),
        P(),
        P(),
        P(),
        P(),
        P(),
    )
    return jax.shard_map(
        on_device, mesh=mesh, in_specs=in_specs, out_specs=out_specs, check_vma=False
    )
```

profile of v0, /device:TPU:0, one launch (start us, length us, event | category | flops | bytes accessed | tf_op | source)
XLA Modules:
  0.0 847.7 jit_solution(8544704404122777579)
XLA Ops:
  17.6 4.9 conditional.14
  22.5 79.1 %all-reduce.83 = (f32[1296]{0:T(1024)}, f32[1296]{0:T(1024)}, f32[1296]{0:T(1024)}, f32[1296]{0:T(1024)}) all-reduce(f32[1296]{0:T(1024)} %get-tuple-element.717, f32[1296]{0:T(1024)} %get-tuple-element.719, f32[1296]{0:T(1024)} %copy-done.157, f32[1296]{0:T(1024)} %copy-done.158), channel_id=1, replica_groups=mesh['pipe'=2,'dp'=16] {'dp'}, use_global_device_ids=true, to_apply=%region_13.14 | all-reduce | flops 5184 | bytes 41472 | tf_op jit(solution)/shard_map/psum | solution.py:485
  101.6 22.1 %conditional.13 = (bf16[1,196,216]{2,1,0:T(8,128)(2,1)}, bf16[1,1,1,196,216]{4,3,2,1,0:T(8,128)(2,1)S(1)}) conditional(s32[]{:T(128)} %convert_element_type.670, () %tuple.133, (bf16[1,196,216]{2,1,0:T(8,128)(2,1)S(1)}, s32[4]{0:T(128)S(1)}, f32[1296]{0:T(1024)}, f32[196,1296]{1,0:T(8,128)S(1)}, f32[1296]{0:T(1024)}, /*index=5*/f32[1296]{0:T(1024)S(1)}, ...), branch_computations={%region_6.7_spmd, %region_7.9_spmd} | conditional | flops 128090680 | bytes 26878512 | solution.py:74
  108.4 8.4 multiply_reduce_fusion.2
  125.8 24.6 %conditional.15 = (bf16[1,196,216]{2,1,0:T(8,128)(2,1)}, bf16[1,1,1,196,216]{4,3,2,1,0:T(8,128)(2,1)S(1)}) conditional(s32[]{:T(128)} %convert_element_type.670, () %tuple.137, (bf16[1,196,216]{2,1,0:T(8,128)(2,1)S(1)}, s32[4]{0:T(128)}, f32[1296]{0:T(1024)}, f32[196,1296]{1,0:T(8,128)}, f32[1296]{0:T(1024)}, /*index=5*/f32[1296]{0:T(1024)S(1)}, ...), branch_computations={%region_15.16_spmd, %region_16.18_spmd} | conditional | flops 128090680 | bytes 26899276 | solution.py:74
  134.9 8.4 multiply_reduce_fusion.3
  152.3 4.2 conditional.16
  156.5 14.3 %conditional.18 = (f32[1,196,216]{2,1,0:T(8,128)}, f32[216]{0:T(256)}, f32[216]{0:T(256)}, f32[216,648]{1,0:T(8,128)}, f32[12,12]{1,0:T(8,128)}, /*index=5*/f32[...) conditional(s32[]{:T(128)} %convert_element_type.675, ...), branch_computations={%region_34.35_spmd, %region_35.61_spmd} | conditional | flops 941713216 | bytes 82464720 | solution.py:74
  173.7 6.8 conditional.17
  180.5 16.8 %conditional.21 = (f32[1,196,216]{2,1,0:T(8,128)}, f32[216]{0:T(256)}, f32[216]{0:T(256)}, f32[216,648]{1,0:T(8,128)}, f32[12,12]{1,0:T(8,128)}, /*index=5*/f32[...) conditional(s32[]{:T(128)} %convert_element_type.675, ...), branch_computations={%region_82.83_spmd, %region_83.109_spmd} | conditional | flops 941713216 | bytes 82629824 | solution.py:74
  213.1 66.1 %collective-permute-done.2 = bf16[1,196,216]{2,1,0:T(8,128)(2,1)} collective-permute-done((bf16[1,196,216]{2,1,0:T(8,128)(2,1)}, bf16[1,196,216]{2,1,0:T(8,128)(2,1)}, u32[]{:S(2)}, u32[]{:S(2)}) %collective-permute-start.2) | collective-permute-done | bytes 84704 | tf_op jit(solution)/shard_map/ppermute | solution.py:23
  279.2 62.1 %conditional.19 = (f32[1,196,1296]{2,1,0:T(8,128)}, f32[1296]{0:T(1024)S(1)}, f32[1296]{0:T(1024)S(1)}, f32[1296]{0:T(1024)S(1)}, f32[1296]{0:T(1024)S(1)}, /*in...) conditional(s32[]{:T(128)} %convert_element_type.670, ...), branch_computations={%region_61.62_spmd, %region_62.78_spmd} | conditional | flops 268161392 | bytes 82831104 | solution.py:74
  287.3 8.4 multiply_reduce_fusion.26
  312.3 7.5 multiply_reduce_fusion.25
  341.4 93.5 %collective-permute-done.3 = bf16[1,196,216]{2,1,0:T(8,128)(2,1)S(1)} collective-permute-done((bf16[1,196,216]{2,1,0:T(8,128)(2,1)}, bf16[1,196,216]{2,1,0:T(8,128)(2,1)S(1)}, u32[]{:S(2)}, u32[]{:S(2)}) %collective-permute-start.3) | collective-permute-done | bytes 84704 | tf_op jit(solution)/shard_map/ppermute | solution.py:23
  435.0 56.1 %conditional.22 = (f32[1,196,1296]{2,1,0:T(8,128)}, f32[1296]{0:T(1024)S(1)}, f32[1296]{0:T(1024)S(1)}, f32[1296]{0:T(1024)S(1)}, f32[1296]{0:T(1024)S(1)}, /*in...) conditional(s32[]{:T(128)} %convert_element_type.670, ...), branch_computations={%region_109.110_spmd, %region_110.126_spmd} | conditional | flops 268161392 | bytes 91031472 | solution.py:74
  442.9 8.5 %multiply_reduce_fusion.52 = (f32[1296]{0:T(1024)S(1)}, f32[1,14,14,1296]{3,2,1,0:T(8,128)}) fusion(f32[14,14]{1,0:T(8,128)S(1)} %fusion.535, f32[1296]{0:T(1024)S(1)} %get-tuple-element.1393, f32[1296]{0:T(1024)S(1)} %get-tuple-element.1386, f32[1296]{0:T(1024)S(1)} %get-tuple-element.1387, f32[1296]{0:T(1024)S(1)} %get-tuple-element.1388, ...), kind=kLoop, calls=%fused_computation.961 | loop fusion | flops 4825008 | bytes 2084752 | tf_op jit(solution)/shard_map/cond/branch_1_fun/jvp()/reduce_sum | solution.py:95
  469.4 3.6 multiply_reduce_fusion.51
  477.9 3.1 multiply_reduce_fusion.54
  512.5 71.8 %all-reduce.82 = (f32[1296]{0:T(1024)S(1)}, f32[1296]{0:T(1024)S(1)}, f32[1296]{0:T(1024)S(1)}, f32[1296]{0:T(1024)S(1)}) all-reduce(f32[1296]{0:T(1024)S(1)} %get-tuple-element.744, f32[1296]{0:T(1024)S(1)} %get-tuple-element.745, f32[1296]{0:T(1024)S(1)} %copy-done.155, ...), channel_id=1, replica_groups=mesh['pipe'=2,'dp'=16] {'dp'}, use_global_device_ids=true, to_apply=%region_126.127 | all-reduce | flops 5184 | bytes 41472 | tf_op jit(solution)/shard_map/psum | solution.py:527
  584.4 6.1 conditional.20
  590.5 3.8 conditional.23
  601.8 26.2 %all-reduce.87.cloned.1.call-done = (f32[1296]{0:T(1024)}, f32[1296]{0:T(1024)}, f32[9,1296]{1,0:T(8,128)}, f32[324]{0:T(512)}, f32[1296]{0:T(1024)}, /*index=5*...) async-done(((f32[1296]{0:T(1024)}, f32[1296]{0:T(1024)}, ...) | async-done | bytes 104416 | tf_op jit(solution)/shard_map/psum | solution.py:553
  628.1 193.8 %all-reduce.89.cloned.1.call-done = (f32[216,1296]{1,0:T(8,128)}, f32[1296,324]{0,1:T(8,128)}, f32[324,1296]{1,0:T(8,128)}, f32[1296,216]{0,1:T(8,128)}, f32[216...) async-done(((f32[216,1296]{1,0:T(8,128)}, f32[1296,324]{0,1:T(8,128)}, f32[324,1296]{1,0:T(8,128)}, f32[1296,216]{0,1:T(8,128)}, ...) | async-done | bytes 7838224 | tf_op jit(solution)/shard_map/psum | solution.py:553
  (463 shorter events, 228.7 us)
Async XLA Ops:
  7.2 620.9 %all-reduce.87.cloned.1.call-start = ((), (), s32[]{:S(2)}) async-start(), calls=%async_computation | async-start | bytes 401408 | tf_op jit(solution)/shard_map/psum | solution.py:553
  9.9 91.8 %copy-start.110 = (s32[4]{0:T(128)}, s32[4]{0:T(128)S(1)}, u32[]{:S(2)}) copy-start(s32[4]{0:T(128)S(1)} %get-tuple-element.1579) | copy-start | bytes 52
  17.0 84.6 %copy-start.54 = (bf16[1,196,216]{2,1,0:T(8,128)(2,1)}, bf16[1,196,216]{2,1,0:T(8,128)(2,1)S(1)}, u32[]{:S(2)}) copy-start(bf16[1,196,216]{2,1,0:T(8,128)(2,1)S(1)} %get-tuple-element.711) | copy-start | bytes 254020
  17.0 84.6 %copy-start.58 = (f32[1296]{0:T(1024)S(1)}, f32[1296]{0:T(1024)}, u32[]{:S(2)}) copy-start(f32[1296]{0:T(1024)} %param.54) | copy-start | bytes 15556
  17.0 84.6 %copy-start.66 = (f32[1296]{0:T(1024)S(1)}, f32[1296]{0:T(1024)}, u32[]{:S(2)}) copy-start(f32[1296]{0:T(1024)} %param.55) | copy-start | bytes 15556
  17.0 84.6 %copy-start.86 = (f32[1296]{0:T(1024)S(1)}, f32[1296]{0:T(1024)}, u32[]{:S(2)}) copy-start(f32[1296]{0:T(1024)} %param.60) | copy-start | bytes 15556
  22.5 103.3 %copy-start.56 = (bf16[1,196,216]{2,1,0:T(8,128)(2,1)}, bf16[1,196,216]{2,1,0:T(8,128)(2,1)S(1)}, u32[]{:S(2)}) copy-start(bf16[1,196,216]{2,1,0:T(8,128)(2,1)S(1)} %get-tuple-element.716) | copy-start | bytes 254020
  124.4 27.9 %collective-permute-start = (bf16[1,196,216]{2,1,0:T(8,128)(2,1)}, bf16[1,196,216]{2,1,0:T(8,128)(2,1)S(1)}, u32[]{:S(2)}, u32[]{:S(2)}) collective-permute-start(bf16[1,196,216]{2,1,0:T(8,128)(2,1)} %get-tuple-element.721), channel_id=1, source_target_pairs={{0,16},{1,17},{2,18},{3,19},{4,20},{5,21},{6,22},{7,23},{8,24},{9,... | collective-permute-start | bytes 254024 | tf_op jit(solution)/shard_map/ppermute | solution.py:23
  151.0 22.7 %collective-permute-start.1 = (bf16[1,196,216]{2,1,0:T(8,128)(2,1)}, bf16[1,196,216]{2,1,0:T(8,128)(2,1)S(1)}, u32[]{:S(2)}, u32[]{:S(2)}) collective-permute-start(bf16[1,196,216]{2,1,0:T(8,128)(2,1)} %get-tuple-element.723), channel_id=1, source_target_pairs={{0,16},{1,17},{2,18},{3,19},{4,20},{5,21},{6,22},{7,23},{8,24},{9,... | collective-permute-start | bytes 254024 | tf_op jit(solution)/shard_map/ppermute | solution.py:23
  172.4 106.8 %collective-permute-start.2 = (bf16[1,196,216]{2,1,0:T(8,128)(2,1)}, bf16[1,196,216]{2,1,0:T(8,128)(2,1)}, u32[]{:S(2)}, u32[]{:S(2)}) collective-permute-start(bf16[1,196,216]{2,1,0:T(8,128)(2,1)} %convert_element_type.676), channel_id=1, source_target_pairs={{16,0},{17,1},{18,2},{19,3},{20,4},{21,5},{22,6},{23,7},{24,8},{25... | collective-permute-start | bytes 254024 | tf_op jit(solution)/shard_map/ppermute | solution.py:23
  198.9 236.0 %collective-permute-start.3 = (bf16[1,196,216]{2,1,0:T(8,128)(2,1)}, bf16[1,196,216]{2,1,0:T(8,128)(2,1)S(1)}, u32[]{:S(2)}, u32[]{:S(2)}) collective-permute-start(bf16[1,196,216]{2,1,0:T(8,128)(2,1)} %convert_element_type.677), channel_id=1, source_target_pairs={{16,0},{17,1},{18,2},{19,3},{20,4},{21,5},{22,6},{23,7},{24,8},{25... | collective-permute-start | bytes 254024 | tf_op jit(solution)/shard_map/ppermute | solution.py:23
  279.2 155.7 %copy-start.94 = (f32[1296]{0:T(1024)S(1)}, f32[1296]{0:T(1024)}, u32[]{:S(2)}) copy-start(f32[1296]{0:T(1024)} %get-tuple-element.1421) | copy-start | bytes 15556
  279.2 155.7 %copy-start.108 = (s32[4]{0:T(128)S(1)}, s32[4]{0:T(128)}, u32[]{:S(2)}) copy-start(s32[4]{0:T(128)} %get-tuple-element.1580) | copy-start | bytes 52
  341.3 93.6 %copy-start.15 = (f32[1296,324]{0,1:T(8,128)}, f32[1296,324]{0,1:T(8,128)S(1)}, u32[]{:S(2)}) copy-start(f32[1296,324]{0,1:T(8,128)S(1)} %get-tuple-element.1259) | copy-start | bytes 5038852
  341.4 93.6 %copy-start.17 = (f32[324,1296]{1,0:T(8,128)}, f32[324,1296]{1,0:T(8,128)S(1)}, u32[]{:S(2)}) copy-start(f32[324,1296]{1,0:T(8,128)S(1)} %get-tuple-element.759) | copy-start | bytes 5038852
  341.4 93.6 %copy-start.144 = (f32[1296]{0:T(1024)}, f32[1296]{0:T(1024)S(1)}, u32[]{:S(2)}) copy-start(f32[1296]{0:T(1024)S(1)} %get-tuple-element.749) | copy-start | bytes 15556
  341.4 93.6 %copy-start.145 = (f32[1296]{0:T(1024)}, f32[1296]{0:T(1024)S(1)}, u32[]{:S(2)}) copy-start(f32[1296]{0:T(1024)S(1)} %get-tuple-element.751) | copy-start | bytes 15556
  341.4 93.6 %copy-start.152 = (f32[1296]{0:T(1024)}, f32[1296]{0:T(1024)S(1)}, u32[]{:S(2)}) copy-start(f32[1296]{0:T(1024)S(1)} %get-tuple-element.734) | copy-start | bytes 15556
  341.4 93.6 %copy-start.154 = (f32[1296]{0:T(1024)}, f32[1296]{0:T(1024)S(1)}, u32[]{:S(2)}) copy-start(f32[1296]{0:T(1024)S(1)} %get-tuple-element.733) | copy-start | bytes 15556
  496.3 325.6 %all-reduce.89.cloned.1.call-start = ((), (), s32[]{:S(2)}) async-start(), calls=%async_computation.1 | async-start | bytes 17121280 | tf_op jit(solution)/shard_map/psum | solution.py:553
  511.0 73.3 %copy-start.13 = (bf16[216,1296]{1,0:T(8,128)(2,1)S(1)}, bf16[216,1296]{1,0:T(8,128)(2,1)}, u32[]{:S(2)}) copy-start(bf16[216,1296]{1,0:T(8,128)(2,1)} %param.53) | copy-start | bytes 1679620
  628.1 196.3 %copy-start.186 = (f32[1296]{0:T(1024)S(1)}, f32[1296]{0:T(1024)}, u32[]{:S(2)}) copy-start(f32[1296]{0:T(1024)} %get-tuple-element.1750) | copy-start | bytes 15556
  628.1 196.9 %copy-start.185 = (f32[1296]{0:T(1024)S(1)}, f32[1296]{0:T(1024)}, u32[]{:S(2)}) copy-start(f32[1296]{0:T(1024)} %get-tuple-element.1751) | copy-start | bytes 15556
  628.1 197.5 %copy-start.90 = (f32[9,1296]{1,0:T(8,128)S(1)}, f32[9,1296]{1,0:T(8,128)}, u32[]{:S(2)}) copy-start(f32[9,1296]{1,0:T(8,128)} %get-tuple-element.1752) | copy-start | bytes 139972
  (82 other events, 443.6 us)
Sparse Core Ops, SparseCore 0:
  496.4 131.5 all-reduce.86
  636.2 185.6 all-reduce.88
where the time goes:
time: 852 us; the launch traced here: 848 us
  waiting for transfers between devices  380 us (45%)
  blocking collectives  151 us (18%)
  other arithmetic  132 us (15%)
  local copies, waits for them, and re-layouts  106 us (12%)
  matrix products  33.4 us (4%)
  loops' own time  24.6 us (3%)
  between operations  16.2 us (2%)
    psum x2, waiting for transfers between devices, on_device(): lax.psum((grads_all[0], grads_all[1], grads_all[2], grads_all[3], grads_a...  220 us
    ppermute x4, waiting for transfers between devices, passed_along(): lax.ppermute(value, axis, [(source, source + steps) for source in range(i...  160 us
    psum x1, blocking collectives, on_device(): first_sum, second_sum = lax.psum((first_sum, second_sum), 'dp')  79.1 us
    psum x1, blocking collectives, on_device(): grad_average, grad_inverse = lax.psum((pulled[1], pulled[2]), 'dp')  71.8 us
    reduce_sum x4, other arithmetic, excite_block(): jnp.sum(deepened, axis=1) / (image_side * image_side).astype(jnp.float32)  33.8 us
    unnamed x148, local copies, waits for them, and re-layouts  26.8 us
    another operation x44, local copies, waits for them, and re-layouts  25.8 us
    another operation x12, loops' own time, only_where(): return lax.cond(predicate, action, nothing, *operands)  24.6 us
  transfers between devices with their start and end apart: 6, of which 4 were waited for; matrix products, arithmetic and copies ran while one was open for 18% of the time, Pallas kernels for 0%

commit v1 on v0

v1 whole, which is shorter than its diff:
```python
import functools
import math

import jax
import jax.numpy as jnp
from jax import lax
from jax.experimental import pallas as pl
from jax.experimental.pallas import tpu as pltpu
from jax.sharding import PartitionSpec as P

D = 216
E = 1296
SQ = 324
HEADS = 12
HD = 18
F = 864
SIDE = 14
PIX = 196
EPSILON = 1e-05
LOG2E = 1.4426950408889634

WIDE = 16
ROWS = SIDE * WIDE
LANES = 128
EB = -(-E // LANES)
FB = -(-F // LANES)
DB = -(-D // LANES)
EP = EB * LANES
FP = FB * LANES
DP = DB * LANES
QB = -(-3 * D // LANES)
QP = QB * LANES

PROJECT = 0
HIDDEN = PROJECT + EB
RETURN = HIDDEN + FB
QKV = RETURN + FB
OUTPUT = QKV + QB
COVARIANCE = OUTPUT + DB
EXPAND = COVARIANCE + DB
BLOCKS = EXPAND + EB - 1
TILES = ROWS // 16
ALL_TILES = BLOCKS * TILES
SHARED = QKV + QB - 1
HALF = LANES // 2
PARTS = 2
FACTOR_ROWS = 32
WEIGHTS = 18
UNPACKED = 26

f32 = jnp.float32
bf16 = jnp.bfloat16
HIGHEST = lax.Precision.HIGHEST
MIB = 1 << 20


def dot(a, b, contract=((1,), (0,)), precision=None):
    return lax.dot_general(a, b, (contract, ((), ())), preferred_element_type=f32, precision=precision)


NT = ((1,), (1,))


def iota(shape, dim):
    return lax.broadcasted_iota(jnp.int32, shape, dim)


def sigmoid(v):
    return 0.5 * jnp.tanh(0.5 * v) + 0.5


def grid_mask(shape, side):
    row = iota(shape, 0)
    return jnp.where(((row >> 4) < side) & ((row & 15) < side), 1.0, 0.0)


def widen(tokens, side):
    row = iota((ROWS, PIX), 0)
    hit = iota((ROWS, PIX), 1) == (row >> 4) * SIDE + (row & 15)
    pick = jnp.where(hit & ((row >> 4) < side) & ((row & 15) < side), 1.0, 0.0).astype(bf16)
    return dot(pick, tokens)


def narrow(tokens):
    column = iota((PIX, ROWS), 1)
    hit = iota((PIX, ROWS), 0) == (column >> 4) * SIDE + (column & 15)
    pick = jnp.where(hit & ((column & 15) < SIDE), 1.0, 0.0).astype(bf16)
    return dot(pick, tokens)


def narrow_into(ref, tokens):
    for i in range(SIDE):
        ref[i * SIDE : (i + 1) * SIDE, :] = tokens[i * WIDE : i * WIDE + SIDE, :]


def grid(v):
    return v.reshape(SIDE, WIDE, v.shape[-1])


def flat(v):
    return v.reshape(ROWS, v.shape[-1])


def depthwise(v, kernel):
    zero = jnp.zeros((1, WIDE, v.shape[-1]), f32)
    v3 = grid(v)
    above = flat(jnp.concatenate([zero, v3[:-1]], axis=0))
    below = flat(jnp.concatenate([v3[1:], zero], axis=0))
    left, middle, right = (kernel[b] * above + kernel[3 + b] * v + kernel[6 + b] * below for b in range(3))
    return middle + pltpu.roll(left, 1, 0) + pltpu.roll(right, ROWS - 1, 0)


def depthwise_kernel_grad(grad, v):
    g3 = grid(grad)
    shifted = [grid(pltpu.roll(v, 1, 0)), grid(v), grid(pltpu.roll(v, ROWS - 1, 0))]
    taps = []
    for a in (-1, 0, 1):
        for b in range(3):
            if a < 0:
                product = g3[1:] * shifted[b][:-1]
            elif a > 0:
                product = g3[:-1] * shifted[b][1:]
            else:
                product = g3 * shifted[b]
            taps.append(jnp.sum(jnp.sum(product, axis=0), axis=0, keepdims=True))
    return taps


def norm_forward(v):
    centred = v - jnp.sum(v, axis=-1, keepdims=True) * (1.0 / D)
    rs = lax.rsqrt(jnp.sum(centred * centred, axis=-1, keepdims=True) * (1.0 / D) + EPSILON)
    return centred * rs, rs


def norm_backward(grad, hat, rs, gain):
    scaled = grad * gain
    first = jnp.sum(scaled, axis=-1, keepdims=True) * (1.0 / D)
    second = jnp.sum(scaled * hat, axis=-1, keepdims=True) * (1.0 / D)
    return rs * (scaled - first - hat * second)


def row_sum(v):
    return jnp.sum(v, axis=0, keepdims=True)


def vector_times(row, matrix, contract):
    high = row.astype(bf16).astype(f32)
    rest = row - high
    mid = rest.astype(bf16).astype(f32)
    low = rest - mid
    which = iota((16, row.shape[-1]), 0)
    stack = jnp.where(which == 0, high, jnp.where(which == 1, mid, jnp.where(which == 2, low, 0.0)))
    return row_sum(dot(stack.astype(bf16), matrix, contract))


def moments(sums, count):
    average = sums[0:1] / count
    variance = sums[1:2] / count - average * average
    return average, lax.rsqrt(variance + EPSILON)


def put_block(tiles_ref, block, grad, smalls):
    tiles_ref[block * TILES : (block + 1) * TILES] = (
        jnp.concatenate([grad, smalls], axis=0).astype(bf16).reshape(TILES, 16, LANES)
    )


def block_of(v, b):
    return v[:, b * LANES : (b + 1) * LANES]


def code_of(codes):
    mine = lax.axis_index("pipe")
    return SIDE - 4 + 2 * codes[mine, 3], codes[mine, 0], codes[mine, 1], codes[mine, 2]


def home_of(order):
    spot = lax.axis_index("dp")
    home = lax.axis_index("pipe")
    for b in order:
        home = home * 2 + ((spot >> b) & 1)
    return home


def fetch(sources, targets, sems):
    copies = [pltpu.make_async_copy(a, b, sems.at[i]) for i, (a, b) in enumerate(zip(sources, targets))]
    for copy in copies:
        copy.start()
    return copies


def sums_kernel(codes, image, expand_hbm, sums_out, expand, sems):
    (expand_copy,) = fetch([expand_hbm], [expand], sems)
    side = code_of(codes)[0]
    tokens = widen(image[...], side).astype(bf16)
    expand_copy.wait()
    expanded = dot(tokens, expand[...])
    sums_out[0:1, :] = row_sum(expanded)
    sums_out[1:2, :] = row_sum(expanded * expanded)
    sums_out[2:3, :] = jnp.zeros((1, E), f32)
    sums_out[2:3, :D] = row_sum(tokens.astype(f32))


def middle_kernel(
    images_total,
    pieces,
    orders,
    codes,
    image,
    cotangent,
    sums,
    gain,
    bias,
    squeeze_bias,
    excite_bias,
    hidden_bias,
    *refs,
):
    (
        first_out,
        second_out,
        handed_grad_out,
        handed_low_out,
        tokens_out,
        expanded_grad_out,
        batch_out,
        kept_out,
        sent_out,
        factors_out,
        tiles_out,
        wide_e,
        wide_f,
        live,
        expanded_s,
        deep_s,
        scaled_s,
        soft_s,
        all_soft,
        all_grad,
        all_keys,
        all_values,
        hidden_s,
        conv_s,
        active_s,
        hidden_low_s,
        up_s,
        smalls_e,
        tail_e,
        smalls_f,
        grad_k,
        grad_v,
        talk_s,
        projected_s,
    ) = refs[WEIGHTS:]
    (
        expand,
        depth_one,
        squeeze_t,
        excite,
        project_t,
        norm_gain,
        norm_bias,
        qkv,
        talk_before,
        talk_after,
        output,
        output_bias,
        mlp_gain,
        mlp_bias,
        hidden,
        depth_two,
        return_t,
        return_bias,
    ) = refs[:WEIGHTS]
    side, code_channels, code_heads, code_units = code_of(codes)
    pixels = (side * side).astype(f32)
    count = images_total * pixels
    live[...] = grid_mask((ROWS, LANES), side)
    live_d = grid_mask((ROWS, D), side)

    average, inverse = moments(sums[...], count)
    wide_e[...] = jnp.zeros_like(wide_e)
    channel_mask = jnp.where(iota((1, E), 1) < E - (2 - code_channels) * D, 1.0, 0.0)
    wide_e[0:1, :E] = average
    wide_e[1:2, :E] = inverse * gain[...]
    wide_e[2:3, :E] = bias[...]
    wide_e[3:4, :E] = channel_mask
    wide_e[4:13, :E] = depth_one[...]
    wide_e[15:16, :E] = inverse
    tokens = widen(image[...], side).astype(bf16)
    tokens_out[...] = tokens
    token_mean = sums[2:3, :D] / count
    centred_tokens = (tokens.astype(f32) - token_mean) * live_d
    expanded_s[:, E - E % LANES :] = jnp.zeros((ROWS, EP - E + E % LANES), f32)
    expanded_s[:, :E] = dot(tokens, expand[...])

    def activate(at):
        centred = expanded_s[:, at] - wide_e[0:1, at]
        normed = centred * wide_e[1:2, at] + wide_e[2:3, at]
        gate = sigmoid(normed)
        return centred, normed, gate

    def forward_one(c, carry):
        at = pl.ds(pl.multiple_of(c * LANES, LANES), LANES)
        centred, normed, gate = activate(at)
        active = normed * gate * (live[...] * wide_e[3:4, at])
        deep = depthwise(active, [wide_e[4 + t : 5 + t, at] for t in range(9)]) * live[...]
        deep_s[:, at] = deep
        wide_e[14:15, at] = row_sum(deep) / pixels
        return carry

    lax.fori_loop(0, EB, forward_one, 0)
    pooled = wide_e[14:15, :E]
    squeeze_pre = vector_times(pooled, squeeze_t[...], NT) + squeeze_bias[...]
    squeeze_gate = sigmoid(squeeze_pre)
    squeezed = squeeze_pre * squeeze_gate
    excited = sigmoid(vector_times(squeezed, excite[...], ((1,), (0,))) + excite_bias[...])
    wide_e[13:14, :E] = excited
    scaled_s[...] = (deep_s[...] * wide_e[13:14, :]).astype(bf16)
    branch = dot(scaled_s[:, :E], project_t[...], NT)
    handed_low = (tokens.astype(f32) + branch).astype(bf16)
    first_out[...] = narrow(handed_low).astype(bf16)
    handed = handed_low.astype(f32)

    hat_one, rs_one = norm_forward(handed)
    normed_one = (hat_one * norm_gain[...] + norm_bias[...]).astype(bf16)
    projected = dot(normed_one, qkv[...]).astype(bf16).astype(f32)
    queries = projected[:, :D]
    key_rows_f = projected[:, D : 2 * D]
    live_heads = HEADS - 2 * (2 - code_heads)
    head_columns = iota((HEADS, D), 1)
    head_rows = iota((HEADS, D), 0) * HD
    own = jnp.where((head_columns >= head_rows) & (head_columns < head_rows + HD), 1.0, 0.0)
    own_rows = iota((D, HEADS), 0)
    own_columns = iota((D, HEADS), 1) * HD
    own_t = jnp.where((own_rows >= own_columns) & (own_rows < own_columns + HD), 1.0, 0.0)
    head_row = jnp.where(iota((1, HEADS), 1) < live_heads, 1.0, 0.0)
    head_column = jnp.where(iota((HEADS, 1), 0) < live_heads, 1.0, 0.0)
    value_mask = jnp.where(iota((1, D), 1) < live_heads * HD, 1.0, 0.0)
    before = talk_before[...] * head_row * HD ** (-0.5)
    after = talk_after[...] * head_row
    before_rows = dot(before, own, precision=HIGHEST)
    before_columns = dot(own_t, before, NT, precision=HIGHEST)
    after_rows = dot(after, own, ((0,), (0,)), precision=HIGHEST)
    after_columns = dot(own_t, after, precision=HIGHEST)
    value_rows_f = projected[:, 2 * D :] * value_mask
    queries_low = queries.astype(bf16)
    spare = iota((ROWS, DP), 1) == D
    row_place = iota((ROWS, DP), 0)
    dead = ((row_place >> 4) >= side) | ((row_place & 15) >= side)
    no_columns = jnp.zeros((ROWS, DP - D), f32)
    keys_wide = jnp.concatenate([key_rows_f, no_columns], axis=1)
    keys_wide = jnp.where(spare & dead, -1000000000.0, keys_wide)
    queries_wide = jnp.where(spare, 1.0, jnp.concatenate([queries, no_columns], axis=1))
    queries_t = queries_wide.T.astype(bf16)
    queries_twice = jnp.concatenate([queries_t, queries_t], axis=0)
    before_wide = jnp.concatenate([before_rows * LOG2E, jnp.zeros((HEADS, DP - D), f32)], axis=1)
    before_wide = jnp.where(iota((HEADS, DP), 1) == D, 1.0, before_wide)
    keys_t = key_rows_f.T
    values_t = value_rows_f.T
    all_soft[...] = jnp.zeros_like(all_soft)
    all_grad[...] = jnp.zeros_like(all_grad)
    all_keys[...] = jnp.zeros_like(all_keys)
    all_values[...] = jnp.zeros_like(all_values)
    for h in range(HEADS):
        weighted = keys_wide * before_wide[h : h + 1]
        high = weighted.astype(bf16)
        low = (weighted - high.astype(f32)).astype(bf16)
        scores = dot(jnp.concatenate([high, low], axis=1), queries_twice)
        grown = jnp.exp2(scores - jnp.max(scores, axis=0, keepdims=True))
        soft = grown * (1.0 / row_sum(grown))
        soft_s[h] = soft
        all_soft[h, 0:ROWS] = soft.astype(bf16)
        all_values[:, h * DP : h * DP + ROWS] = (values_t * after_columns[:, h : h + 1]).astype(bf16)
        all_keys[:, h * DP : h * DP + ROWS] = (keys_t * before_columns[:, h : h + 1]).astype(bf16)
    heads_out_t = dot(all_values[...], all_soft[...].reshape(HEADS * DP, ROWS)).astype(bf16)
    heads_out = heads_out_t.astype(f32).T.astype(bf16)
    attended = dot(heads_out, output[...]) + output_bias[...]
    middle = handed + attended * live_d

    hat_two, rs_two = norm_forward(middle)
    normed_two_f = hat_two * mlp_gain[...] + mlp_bias[...]
    normed_two = normed_two_f.astype(bf16)
    wide_f[...] = jnp.zeros_like(wide_f)
    wide_f[0:1, :F] = hidden_bias[...]
    wide_f[1:2, :F] = jnp.where(iota((1, F), 1) < F - (2 - code_units) * D, 1.0, 0.0)
    wide_f[2:11, :F] = depth_two[...]
    hidden_s[:, F - F % LANES :] = jnp.zeros((ROWS, FP - F + F % LANES), f32)
    hidden_s[:, :F] = dot(normed_two, hidden[...])

    def forward_two(c, carry):
        at = pl.ds(pl.multiple_of(c * LANES, LANES), LANES)
        units = (hidden_s[:, at] + wide_f[0:1, at]) * (live[...] * wide_f[1:2, at])
        hidden_s[:, at] = units
        conv = depthwise(units, [wide_f[2 + t : 3 + t, at] for t in range(9)]) * live[...]
        conv_s[:, at] = conv
        active_s[:, at] = (conv * sigmoid(conv)).astype(bf16)
        return carry

    lax.fori_loop(0, FB, forward_two, 0)
    final = middle + dot(active_s[:, :F], return_t[...], NT) + return_bias[...]
    second_out[...] = narrow((final * live_d).astype(bf16)).astype(bf16)

    upstream = widen(cotangent[...], side)
    grad_return_bias = row_sum(upstream)
    up_s[:, F - F % LANES :] = jnp.zeros((ROWS, FP - F + F % LANES), f32)
    up_s[:, :F] = dot(upstream.astype(bf16), return_t[...])
    smalls_f[...] = jnp.zeros_like(smalls_f)

    def backward_two(c, carry):
        at = pl.ds(pl.multiple_of(c * LANES, LANES), LANES)
        conv = conv_s[:, at]
        gate = sigmoid(conv)
        grad_conv = up_s[:, at] * (gate * (1.0 + conv * (1.0 - gate))) * live[...]
        taps = depthwise_kernel_grad(grad_conv, hidden_s[:, at])
        for t in range(9):
            smalls_f[t : t + 1, at] = taps[t]
        flipped = [wide_f[10 - t : 11 - t, at] for t in range(9)]
        grad_units = depthwise(grad_conv, flipped) * (live[...] * wide_f[1:2, at])
        smalls_f[9:10, at] = row_sum(grad_units)
        hidden_low_s[:, at] = grad_units.astype(bf16)
        return carry

    lax.fori_loop(0, FB, backward_two, 0)
    grad_return = dot(upstream.T.astype(bf16), active_s[...])
    for b in range(FB):
        put_block(tiles_out, RETURN + b, block_of(grad_return, b), smalls_f[8:16, b * LANES : (b + 1) * LANES])
    grad_hidden = dot(normed_two_f.T.astype(bf16), hidden_low_s[...])
    for b in range(FB):
        put_block(tiles_out, HIDDEN + b, block_of(grad_hidden, b), smalls_f[0:8, b * LANES : (b + 1) * LANES])
    grad_normed_two = dot(hidden_low_s[:, :F], hidden[...], NT)
    grad_mlp_gain = row_sum(grad_normed_two * hat_two)
    grad_mlp_bias = row_sum(grad_normed_two)
    grad_middle = upstream + norm_backward(grad_normed_two, hat_two, rs_two, mlp_gain[...])

    attend_up = grad_middle * live_d
    grad_output_bias = row_sum(attend_up)
    attend_low = attend_up.astype(bf16)
    grad_output = dot(heads_out_t, attend_low)
    grad_heads_low = dot(attend_low, output[...], NT).astype(bf16)
    grad_heads_t = grad_heads_low.astype(f32).T.astype(bf16)
    grad_k[...] = jnp.zeros_like(grad_k)
    grad_v[...] = jnp.zeros_like(grad_v)
    for h in range(HEADS):
        soft = soft_s[h]
        grad_soft = dot((value_rows_f * after_rows[h : h + 1]).astype(bf16), grad_heads_t)
        grad_scores = (soft * (grad_soft - row_sum(soft * grad_soft))).astype(bf16)
        all_grad[h, 0:ROWS] = grad_scores
        back = dot(grad_scores, queries_low)
        grad_k[...] += back * before_rows[h : h + 1]
        talk_s[h : h + 1, :] = row_sum(back * key_rows_f)
        back = dot(all_soft[h, 0:ROWS], grad_heads_low)
        grad_v[...] += back * after_rows[h : h + 1]
        talk_s[16 + h : 17 + h, :] = row_sum(back * value_rows_f)
    grad_q = dot(all_keys[...], all_grad[...].reshape(HEADS * DP, ROWS)).T
    talk_before_grad = dot(talk_s[0:12, :], own_t, precision=HIGHEST) * (head_row * HD ** (-0.5))
    talk_after_grad = dot(own_t, talk_s[16:28, :], ((0,), (1,)), precision=HIGHEST) * head_row
    projected_s[:, :D] = grad_q
    projected_s[:, D : 2 * D] = grad_k[...]
    projected_s[:, 2 * D :] = grad_v[...] * value_mask
    grad_projected = projected_s[...].astype(bf16)
    grad_normed_one = dot(grad_projected, qkv[...], NT)
    normed_one_t = (hat_one * norm_gain[...] + norm_bias[...]).T.astype(bf16)
    grad_norm_gain = row_sum(grad_normed_one * hat_one)
    grad_norm_bias = row_sum(grad_normed_one)
    handed_grad = grad_middle + norm_backward(grad_normed_one, hat_one, rs_one, norm_gain[...])
    narrow_into(handed_grad_out, handed_grad)

    talk_s[...] = jnp.zeros_like(talk_s)
    talk_s[0:12, 0:HEADS] = talk_before_grad
    talk_s[16:28, 0:HEADS] = talk_after_grad
    grad_qkv = jnp.concatenate([dot(normed_one_t, grad_projected), jnp.zeros((D, QP - 3 * D), f32)], axis=1)
    for b in range(QB - 1):
        extra = talk_s[8 * b : 8 * b + 8, 0:LANES] if b < 4 else jnp.zeros((8, LANES), f32)
        put_block(tiles_out, QKV + b, block_of(grad_qkv, b), extra)
    talk_s[0:8, :] = jnp.zeros((8, D), f32)
    talk_s[0:1, :] = grad_norm_gain
    talk_s[1:2, :] = grad_norm_bias
    talk_s[2:3, :] = grad_output_bias
    talk_s[3:4, :] = grad_mlp_gain
    talk_s[4:5, :] = grad_mlp_bias
    talk_s[5:6, :] = grad_return_bias
    leading = lax.axis_index("pipe") == 0
    centred_low = centred_tokens.astype(bf16)
    centred_t = centred_tokens.T.astype(bf16)
    covariance = dot(centred_t, centred_low)
    over = iota((D, D), 0) - iota((D, D), 1)
    over = jnp.where(leading, over, -over)
    talk_s[6:7, :] = jnp.where(leading, 0.0, row_sum(jnp.where(over == 0, covariance, 0.0)))
    wanted = (over < 0) | ((over == 0) & leading)
    covariance = jnp.concatenate([jnp.where(wanted, covariance, 0.0), jnp.zeros((D, DP - D), f32)], axis=1)
    for b in range(DB):
        put_block(tiles_out, COVARIANCE + b, block_of(covariance, b), jnp.zeros((8, LANES), f32))
    for b in range(DB):
        piece = jnp.concatenate([grad_output, jnp.zeros((D, DP - D), f32)], axis=1)
        extra = jnp.concatenate([talk_s[0:8, :], jnp.zeros((8, DP - D), f32)], axis=1)
        put_block(tiles_out, OUTPUT + b, block_of(piece, b), block_of(extra, b))

    back_low = handed_grad.astype(bf16)
    handed_low_out[...] = back_low
    expanded_grad_out[:, E - E % LANES :] = jnp.zeros((ROWS, EP - E + E % LANES), f32)
    expanded_grad_out[:, :E] = dot(back_low, project_t[...])

    excited = wide_e[13:14, :E]
    grad_excited = row_sum(expanded_grad_out[:, :E] * deep_s[:, :E])
    grad_excite_pre = grad_excited * excited * (1.0 - excited)
    grad_squeezed = vector_times(grad_excite_pre, excite[...], NT)
    grad_squeeze_pre = grad_squeezed * (squeeze_gate * (1.0 + squeeze_pre * (1.0 - squeeze_gate)))
    grad_pooled = vector_times(grad_squeeze_pre, squeeze_t[...], ((1,), (0,)))
    factors_out[...] = jnp.zeros_like(factors_out)

    def put_factor(start, row):
        width = row.shape[-1]
        for b in range(-(-width // LANES)):
            end = min(width, (b + 1) * LANES)
            factors_out[start + b : start + b + 1, 0 : end - b * LANES] = row[:, b * LANES : end]

    put_factor(0, wide_e[14:15, :E])
    put_factor(EB, grad_excite_pre)
    put_factor(2 * EB, squeezed)
    put_factor(2 * EB + 3, grad_squeeze_pre)
    wide_e[14:15, :E] = grad_pooled / pixels
    tail_e[...] = jnp.zeros_like(tail_e)
    batch_out[...] = jnp.zeros_like(batch_out)

    def backward_one(c, carry):
        at = pl.ds(pl.multiple_of(c * LANES, LANES), LANES)
        centred, normed, gate = activate(at)
        mask = live[...] * wide_e[3:4, at]
        active = normed * gate * mask
        grad_deep = (expanded_grad_out[:, at] * wide_e[13:14, at] + wide_e[14:15, at]) * live[...]
        taps = depthwise_kernel_grad(grad_deep, active)
        for t in range(8):
            smalls_e[t : t + 1, at] = taps[t]
        flipped = [wide_e[12 - t : 13 - t, at] for t in range(9)]
        grad_active = depthwise(grad_deep, flipped) * mask
        grad_normed = grad_active * (gate * (1.0 + normed * (1.0 - gate)))
        grad_gain = row_sum(grad_normed * centred) * wide_e[15:16, at]
        grad_bias = row_sum(grad_normed)
        batch_out[pl.ds(c, 1), :] = grad_gain
        batch_out[pl.ds(c + 16, 1), :] = grad_bias
        tail_e[0:1, at] = grad_gain
        tail_e[1:2, at] = grad_bias
        tail_e[2:3, at] = taps[8]
        grad_second = grad_gain * wide_e[15:16, at] * wide_e[1:2, at] * (-1.0 / count)
        tail_e[3:4, at] = jnp.where(leading, grad_second, 0.0)
        tail_e[4:5, at] = jnp.where(leading, 0.0, grad_second)
        expanded_grad_out[:, at] = grad_normed * wide_e[1:2, at]
        return carry

    lax.fori_loop(0, EB, backward_one, 0)
    grad_project = dot(handed_grad.T.astype(bf16), scaled_s[...])
    for b in range(EB):
        put_block(tiles_out, PROJECT + b, block_of(grad_project, b), smalls_e[:, b * LANES : (b + 1) * LANES])
    grad_expand = dot(centred_t, expanded_grad_out[...].astype(bf16))
    for b in range(EB - 1):
        put_block(tiles_out, EXPAND + b, block_of(grad_expand, b), tail_e[:, b * LANES : (b + 1) * LANES])
    last = jnp.concatenate([block_of(grad_expand, EB - 1), tail_e[:, EP - LANES :]], axis=0)
    shared = jnp.concatenate([block_of(grad_qkv, QB - 1), jnp.zeros((8, LANES), f32)], axis=0)
    shared = shared + pltpu.roll(last, HALF, 1)
    put_block(tiles_out, SHARED, shared[:D], shared[D:])
    spare = tiles_out.shape[0] - ALL_TILES
    if spare:
        tiles_out[ALL_TILES:] = jnp.zeros((spare, 16, LANES), bf16)

    half = pieces // 2
    per_piece = kept_out.shape[2]
    for part, order in enumerate(orders):
        me = home_of(order) & (half - 1)
        for piece in range(half):
            first = (part * pieces + piece) * per_piece
            second = first + half * per_piece
            low = tiles_out[first : first + per_piece]
            high = tiles_out[second : second + per_piece]
            kept_out[piece ^ me, part] = jnp.where(leading, low, high)
            sent_out[piece ^ me, part] = jnp.where(leading, high, low)


def last_kernel(
    images_total, codes, sums, total, gain, tokens, handed_low, expanded_grad, expand, grad_out, wide
):
    side = code_of(codes)[0]
    count = images_total * (side * side).astype(f32)
    average, inverse = moments(sums[...], count)
    scale = inverse * gain[...]
    for b in range(EB):
        wide[0:1, b * LANES : (b + 1) * LANES] = total[b : b + 1, :]
        wide[1:2, b * LANES : (b + 1) * LANES] = total[16 + b : 17 + b, :]
    grad_variance = -0.5 * inverse * scale * wide[0:1, :E]
    grad_second = grad_variance / count
    grad_first = (-scale * wide[1:2, :E] - 2.0 * average * grad_variance) / count
    expanded = dot(tokens[...], expand[...])
    grad = (expanded_grad[:, :E] + grad_first + 2.0 * expanded * grad_second).astype(bf16)
    grad_tokens = (handed_low[...].astype(f32) + dot(grad, expand[...], NT)) * grid_mask((ROWS, D), side)
    narrow_into(grad_out, grad_tokens)


def unpack_kernel(pieces, per_piece, orders, merged, *refs):
    expand, *refs = refs
    single = (len(refs) - UNPACKED - merged) // PARTS
    inputs = refs[: merged + PARTS * single]
    (
        expand_out,
        gain_out,
        bias_out,
        depth_one_out,
        squeeze_out,
        squeeze_bias_out,
        excite_out,
        excite_bias_out,
        project_out,
        norm_gain_out,
        norm_bias_out,
        qkv_out,
        talk_before_out,
        talk_after_out,
        output_out,
        output_bias_out,
        mlp_gain_out,
        mlp_bias_out,
        hidden_out,
        hidden_bias_out,
        depth_two_out,
        return_out,
        return_bias_out,
        tiles,
        factors,
        wide,
    ) = refs[merged + PARTS * single :]
    for part, order in enumerate(orders):
        me = home_of(order)
        at = 0
        own = inputs[merged + part * single : merged + (part + 1) * single]
        for number, ref in enumerate(inputs[:merged] + own):
            skipped = part * (per_piece + FACTOR_ROWS // 16) if number < merged else 0
            for inner in range(ref.shape[0]):
                home = at ^ me
                tiles[pl.ds((part * pieces + home) * per_piece, per_piece)] = ref[inner, skipped : skipped + per_piece]
                if part == 0:
                    factor = ref[inner, per_piece : per_piece + FACTOR_ROWS // 16]
                    factors[home] = factor.reshape(FACTOR_ROWS, LANES).astype(f32)
                at += 1

    def block(b):
        return tiles[b * TILES : (b + 1) * TILES].reshape(ROWS, LANES).astype(f32)

    def spread(first, count, width, out, take):
        for b in range(count):
            value = block(first + b)
            start, stop = b * LANES, min(width, (b + 1) * LANES)
            out[:, start:stop] = value[0:D, 0 : stop - start]
            for ref, top, row, rows in take:
                if len(ref.shape) == 1:
                    ref[start:stop] = value[D + row, 0 : stop - start]
                else:
                    ref[top : top + rows, start:stop] = value[D + row : D + row + rows, 0 : stop - start]

    spread(PROJECT, EB, E, project_out, [(depth_one_out, 0, 0, 8)])
    shared = pltpu.roll(block(SHARED), HALF, 1)
    for b in range(EB):
        value = block(EXPAND + b) if b < EB - 1 else shared
        wide[:, b * LANES : (b + 1) * LANES] = value
    gain_out[...] = wide[D, 0:E]
    bias_out[...] = wide[D + 1, 0:E]
    depth_one_out[8:9, :] = wide[D + 2 : D + 3, 0:E]
    both = jnp.concatenate([block(COVARIANCE), block(COVARIANCE + 1)], axis=1)[0:D, 0:D]
    turned = both.T
    over = iota((D, D), 0) - iota((D, D), 1)
    diagonal = jnp.concatenate([block(OUTPUT)[D + 6 : D + 7], block(OUTPUT + 1)[D + 6 : D + 7]], axis=1)[:, 0:D]
    first = jnp.where(over <= 0, both, turned).astype(bf16)
    second = jnp.where(over > 0, both, jnp.where(over < 0, turned, diagonal)).astype(bf16)
    added = dot(first, expand[...]) * wide[D + 3 : D + 4, 0:E] + dot(second, expand[...]) * wide[D + 4 : D + 5, 0:E]
    expand_out[...] = wide[0:D, 0:E] + added
    spread(HIDDEN, FB, F, hidden_out, [(depth_two_out, 0, 0, 8)])
    spread(RETURN, FB, F, return_out, [(depth_two_out, 8, 0, 1), (hidden_bias_out, 0, 1, 1)])
    vectors = (norm_gain_out, norm_bias_out, output_bias_out, mlp_gain_out, mlp_bias_out, return_bias_out)
    spread(OUTPUT, DB, D, output_out, [(ref, 0, row, 1) for row, ref in enumerate(vectors)])
    spread(QKV, QB, 3 * D, qkv_out, [])
    talk_before_out[0:8] = block(QKV)[D : D + 8, 0:HEADS]
    talk_before_out[8:12] = block(QKV + 1)[D : D + 4, 0:HEADS]
    talk_after_out[0:8] = block(QKV + 2)[D : D + 8, 0:HEADS]
    talk_after_out[8:12] = block(QKV + 3)[D : D + 4, 0:HEADS]

    def gathered(start, width):
        columns = [factors[:, start + b, :] for b in range(-(-width // LANES))]
        return jnp.concatenate(columns, axis=1)[:, 0:width]

    pooled = gathered(0, E)
    grad_excite_pre = gathered(EB, E)
    squeezed = gathered(2 * EB, SQ)
    grad_squeeze_pre = gathered(2 * EB + 3, SQ)
    squeeze_bias_out[...] = jnp.sum(grad_squeeze_pre, axis=0)
    excite_bias_out[...] = jnp.sum(grad_excite_pre, axis=0)
    squeeze_out[...] = dot(grad_squeeze_pre.T.astype(bf16), pooled.astype(bf16))
    excite_out[...] = dot(squeezed.T.astype(bf16), grad_excite_pre.astype(bf16))


def kernel_call(body, name, shapes, scratch, operands, fetched, limit, flops):
    in_specs = [pl.BlockSpec(memory_space=pltpu.VMEM)] * len(operands)
    if fetched is not None:
        in_specs[0] = pl.BlockSpec(memory_space=pltpu.SMEM)
        in_specs += [pl.BlockSpec(memory_space=pltpu.HBM)] * len(fetched)
    return pl.pallas_call(
        body,
        out_shape=[jax.ShapeDtypeStruct(shape, kind) for shape, kind in shapes],
        in_specs=in_specs,
        out_specs=[pl.BlockSpec(memory_space=pltpu.VMEM)] * len(shapes),
        scratch_shapes=scratch,
        compiler_params=pltpu.CompilerParams(vmem_limit_bytes=limit * MIB),
        cost_estimate=pl.CostEstimate(flops=flops, bytes_accessed=8 * MIB, transcendentals=0),
        name=name,
    )(*operands, *(fetched or ()))


def swapped(value, axis, mask):
    size = lax.axis_size(axis)
    return lax.ppermute(value, axis, [(i, i ^ mask) for i in range(size)])


def summed_over_dp(value, bits):
    for first in range(0, bits, 2):
        here = [1 << b for b in range(first, min(first + 2, bits))]
        masks = here + ([here[0] | here[1]] if len(here) == 2 else [])
        others = [swapped(value, "dp", mask) for mask in masks]
        value = value + functools.reduce(jnp.add, others)
    return value


def on_device(
    images,
    codes,
    cotangent,
    expand_weight,
    batch_gain,
    batch_bias,
    depth_one,
    squeeze_weight,
    squeeze_bias,
    excite_weight,
    excite_bias,
    project_weight,
    norm_gain,
    norm_bias,
    qkv_weight,
    talk_before,
    talk_after,
    output_weight,
    output_bias,
    mlp_gain,
    mlp_bias,
    hidden_weight,
    hidden_bias,
    depth_two,
    return_weight,
    return_bias,
):
    devices_dp = lax.axis_size("dp")
    bits = devices_dp.bit_length() - 1
    pieces = 2 * devices_dp
    half = pieces // 2
    images_total = float(images.shape[1] * devices_dp)
    per_piece = -(-ALL_TILES // (PARTS * pieces))
    factor_tiles = FACTOR_ROWS // 16
    pipe = lax.axis_index("pipe")

    rest = list(range(2, bits))
    groups = [rest[g : g + 2] for g in range(0, len(rest), 2)]
    orders = [[0, 1] + rest, [1, 0] + rest]
    image = lax.dynamic_index_in_dim(images, pipe, 0, keepdims=False)[0]
    upstream = lax.dynamic_index_in_dim(cotangent, pipe, 0, keepdims=False)[0]

    def row(vector):
        return vector.reshape(1, -1)

    def buffers(arrays):
        return [pltpu.VMEM(a.shape, a.dtype) for a in arrays]

    squeeze_t = squeeze_weight.T
    project_t = project_weight.T
    return_t = return_weight.T
    gain = row(batch_gain)

    (sums,) = kernel_call(
        sums_kernel,
        "sums",
        [((3, E), f32)],
        buffers([expand_weight]) + [pltpu.SemaphoreType.DMA((1,))],
        (codes, image),
        (expand_weight,),
        16,
        1 << 33,
    )
    sums = summed_over_dp(sums, bits)

    operands = (
        codes,
        image,
        upstream,
        sums,
        gain,
        row(batch_bias),
        row(squeeze_bias),
        row(excite_bias),
        row(hidden_bias),
        expand_weight,
        depth_one,
        squeeze_t,
        excite_weight,
        project_t,
        row(norm_gain),
        row(norm_bias),
        qkv_weight,
        talk_before,
        talk_after,
        output_weight,
        row(output_bias),
        row(mlp_gain),
        row(mlp_bias),
        hidden_weight,
        depth_two,
        return_t,
        row(return_bias),
    )
    shapes = [
        ((PIX, D), bf16),
        ((PIX, D), bf16),
        ((PIX, D), f32),
        ((ROWS, D), bf16),
        ((ROWS, D), bf16),
        ((ROWS, EP), f32),
        ((32, LANES), f32),
        ((half, PARTS, per_piece, 16, LANES), bf16),
        ((half, PARTS, per_piece, 16, LANES), bf16),
        ((FACTOR_ROWS, LANES), f32),
    ]
    scratch = [
        pltpu.VMEM((PARTS * pieces * per_piece, 16, LANES), bf16),
        pltpu.VMEM((16, EP), f32),
        pltpu.VMEM((16, FP), f32),
        pltpu.VMEM((ROWS, LANES), f32),
        pltpu.VMEM((ROWS, EP), f32),
        pltpu.VMEM((ROWS, EP), f32),
        pltpu.VMEM((ROWS, EP), bf16),
        pltpu.VMEM((HEADS, ROWS, ROWS), f32),
        pltpu.VMEM((HEADS, DP, ROWS), bf16),
        pltpu.VMEM((HEADS, DP, ROWS), bf16),
        pltpu.VMEM((D, HEADS * DP), bf16),
        pltpu.VMEM((D, HEADS * DP), bf16),
        pltpu.VMEM((ROWS, FP), f32),
        pltpu.VMEM((ROWS, FP), f32),
        pltpu.VMEM((ROWS, FP), bf16),
        pltpu.VMEM((ROWS, FP), bf16),
        pltpu.VMEM((ROWS, FP), f32),
        pltpu.VMEM((8, EP), f32),
        pltpu.VMEM((8, EP), f32),
        pltpu.VMEM((16, FP), f32),
        pltpu.VMEM((ROWS, D), f32),
        pltpu.VMEM((ROWS, D), f32),
        pltpu.VMEM((32, D), f32),
        pltpu.VMEM((ROWS, 3 * D), f32),
    ]
    first, second, handed_grad, handed_low, tokens, expanded_grad, batch, kept, sent, factors = kernel_call(
        functools.partial(middle_kernel, images_total, pieces, orders),
        "middle",
        shapes,
        scratch,
        operands,
        (),
        40,
        1 << 32,
    )

    def plus(value, *others):
        return functools.reduce(jnp.add, [v.astype(f32) for v in (value, *others)]).astype(bf16)

    def masks_of(group):
        return [sum(1 << b for i, b in enumerate(group) if (j >> (len(group) - 1 - i)) & 1) for j in range(1 << len(group))]

    def as_tiles(value):
        high = lax.reduce_precision(value, exponent_bits=8, mantissa_bits=7)
        return jnp.concatenate([high, value - high]).astype(bf16).reshape(-1, 16, LANES)

    def with_batch(value):
        return jnp.concatenate([value.reshape(-1, 16, LANES), as_tiles(batch)])

    def from_batch(value, like):
        count = math.prod(like.shape[:-2])
        rest_of = value[count:].astype(f32).reshape(2, -1, LANES)
        return value[:count].reshape(like.shape), rest_of[0] + rest_of[1]

    held = plus(kept, swapped(sent, "pipe", 1))
    held = [held[:, part] for part in range(PARTS)]
    for step in range(2):
        sending = [value[value.shape[0] // 2 :] for value in held]
        arrived = [swapped(with_batch(sending[0]), "dp", 1 << orders[0][step])]
        arrived += [swapped(value, "dp", 1 << order[step]) for value, order in zip(sending[1:], orders[1:])]
        arrived[0], other_batch = from_batch(arrived[0], sending[0])
        batch = batch + other_batch
        held = [plus(value[: value.shape[0] // 2], other) for value, other in zip(held, arrived)]
    held = jnp.concatenate(held, axis=1)
    for group in groups:
        masks = masks_of(group)
        quarters = held.reshape((len(masks), -1) + held.shape[1:])
        arrived = [swapped(with_batch(quarters[j]), "dp", masks[j]) for j in range(1, len(masks))]
        arrived = [from_batch(value, quarters[0]) for value in arrived]
        batch = batch + functools.reduce(jnp.add, [other for _, other in arrived])
        held = plus(quarters[0], *[value for value, _ in arrived])
    (images_grad,) = kernel_call(
        functools.partial(last_kernel, images_total),
        "last",
        [((PIX, D), f32)],
        [pltpu.VMEM((2, EP), f32)],
        (codes, sums, batch, gain, tokens, handed_low, expanded_grad, expand_weight),
        (),
        16,
        1 << 31,
    )

    held = jnp.concatenate(
        [held[:, :per_piece], factors.astype(bf16).reshape(1, factor_tiles, 16, LANES), held[:, per_piece:]], axis=1
    )
    merged = [held]
    for group in reversed(groups):
        merged += [swapped(held, "dp", mask) for mask in masks_of(group)[1:]]
        held = jnp.concatenate(merged, axis=0)
    widths = per_piece + factor_tiles
    held = [held[:, :widths], held[:, widths:]]
    collected = [[], []]
    for step in (1, 0):
        arrived = [swapped(value, "dp", 1 << order[step]) for value, order in zip(held, orders)]
        for part in range(PARTS):
            collected[part].append(arrived[part])
        held = [jnp.concatenate([value, other], axis=0) for value, other in zip(held, arrived)]
    for part in range(PARTS):
        collected[part].append(swapped(held[part], "pipe", 1))
    grads = kernel_call(
        functools.partial(unpack_kernel, pieces, per_piece, orders, len(merged)),
        "unpack",
        [
            ((D, E), f32),
            ((E,), f32),
            ((E,), f32),
            ((9, E), f32),
            ((SQ, E), f32),
            ((SQ,), f32),
            ((SQ, E), f32),
            ((E,), f32),
            ((D, E), f32),
            ((D,), f32),
            ((D,), f32),
            ((D, 3 * D), f32),
            ((HEADS, HEADS), f32),
            ((HEADS, HEADS), f32),
            ((D, D), f32),
            ((D,), f32),
            ((D,), f32),
            ((D,), f32),
            ((D, F), f32),
            ((F,), f32),
            ((9, F), f32),
            ((D, F), f32),
            ((D,), f32),
        ],
        [
            pltpu.VMEM((PARTS * pieces * per_piece, 16, LANES), bf16),
            pltpu.VMEM((pieces, FACTOR_ROWS, LANES), f32),
            pltpu.VMEM((ROWS, EP), f32),
        ],
        (expand_weight, *merged, *collected[0], *collected[1]),
        None,
        40,
        1 << 26,
    )
    grads = list(grads)
    for transposed in (4, 8, 21):
        grads[transposed] = grads[transposed].T

    leading = pipe == 0

    def both_layers(one, two):
        other = swapped(jnp.where(leading, two, one), "pipe", 1)
        return jnp.where(leading, jnp.stack([one, other]), jnp.stack([other, two]))[None, :, None]

    activations = both_layers(first, second)
    input_grads = both_layers(images_grad, handed_grad)
    return (activations, input_grads, *grads)


def solution(mesh):
    in_specs = (P(None, "dp", None, None), P(), P(None, "dp", None, None)) + (P(),) * 23
    out_specs = (P("pipe", None, "dp", None, None), P("pipe", None, "dp", None, None)) + (P(),) * 23
    return jax.shard_map(on_device, mesh=mesh, in_specs=in_specs, out_specs=out_specs, check_vma=False)
```

time: 852 us -> 112 us (0.13)
  waiting for transfers between devices: 380 us -> 40.2 us
  blocking collectives: 151 us -> 0 us
  other arithmetic: 132 us -> 2.47 us
  local copies, waits for them, and re-layouts: 106 us -> 7.48 us
  matrix products: 33.4 us -> 0 us
  Pallas kernels: 0 us -> 29.8 us
  starting transfers between devices: 5.2 us -> 30.5 us
  loops' own time: 24.6 us -> 0 us
  between operations: 16.2 us -> 1.51 us
    psum x2 -> x0, waiting for transfers between devices: 220 us -> none  [on_device(): lax.psum((grads_all[0], grads_all[1], grads_all[2], grads_all[3], grads_a...]
    psum x2 -> x0, blocking collectives: 151 us -> none  [the longest x1 79.1 us: on_device(): first_sum, second_sum = lax.psum((first_sum, second_sum), 'dp')]
    ppermute x4 -> x25, waiting for transfers between devices: 160 us -> 40.2 us  [swapped(): return lax.ppermute(value, axis, [(i, i ^ mask) for i in range(size)])]
    reduce_sum x10 -> x0, other arithmetic: 54.7 us -> none  [the longest x4 33.8 us: excite_block(): jnp.sum(deepened, axis=1) / (image_side * image_side).astype(jnp.float32)]
    add x23 -> x6, other arithmetic: 36.6 us -> 0.05 us  [the longest x2 0.02 us: summed_over_dp(): value = value + functools.reduce(jnp.add, others)]
    dot_general x24 -> x0, matrix products: 33.4 us -> none  [the longest x6 7.83 us: excite_block(): jnp.dot(pooled, squeeze_matrix, precision=highest) + squeeze_shift]
    pallas_call x0 -> x4, Pallas kernels: none -> 29.8 us  [kernel_call(): pl.pallas_call(body, out_shape=[jax.ShapeDtypeStruct(shape, kind) for sha...]
    reshape x12 -> x5, local copies, waits for them, and re-layouts: 29.3 us -> 0.02 us  [row(): return vector.reshape(1, -1)]
  transfers between devices with their start and end apart: 6 -> 25, of which waited for: 4 -> 18; matrix products, arithmetic and copies ran while one was open for 18% -> 3% of each run, Pallas kernels for 0% -> 1%
where the time goes in v1:
time: 112 us
  waiting for transfers between devices  40.2 us (36%)
  starting transfers between devices  30.5 us (27%)
  Pallas kernels  29.8 us (27%)
  local copies, waits for them, and re-layouts  7.48 us (7%)
  other arithmetic  2.47 us (2%)
  between operations  1.51 us (1%)
    ppermute x25, waiting for transfers between devices, swapped(): return lax.ppermute(value, axis, [(i, i ^ mask) for i in range(size)])  40.2 us
    ppermute x25, starting transfers between devices, swapped(): return lax.ppermute(value, axis, [(i, i ^ mask) for i in range(size)])  30.5 us
    pallas_call x4, Pallas kernels, kernel_call(): pl.pallas_call(body, out_shape=[jax.ShapeDtypeStruct(shape, kind) for sha...  29.8 us
    unnamed x62, local copies, waits for them, and re-layouts  5.89 us
  transfers between devices with their start and end apart: 25, of which 18 were waited for; matrix products, arithmetic and copies ran while one was open for 3% of the time, Pallas kernels for 1%

profile of v1, /device:TPU:0, one launch (start us, length us, event | category | flops | bytes accessed | tf_op | source)
XLA Modules:
  0.0 111.9 jit_solution(1530932346908167205)
XLA Ops:
  5.1 4.0 %collective-permute-start.2 = (f32[3,1296]{1,0:T(4,128)S(1)}, f32[3,1296]{1,0:T(4,128)S(1)}, u32[]{:S(2)}, u32[]{:S(2)}) collective-permute-start(f32[3,1296]{1,0:T(4,128)S(1)} %sums.1), channel_id=1, source_target_pairs={{0,3},{1,2},{2,1},{3,0},{4,7},{5,6},{6,5},{7,4},{8,11},{9,10},{10,... | collective-permute-start | bytes 46664 | tf_op jit(solution)/shard_map/ppermute | solution.py:717
  10.8 2.0 %collective-permute-done.1 = f32[3,1296]{1,0:T(4,128)S(1)} collective-permute-done((f32[3,1296]{1,0:T(4,128)S(1)}, f32[3,1296]{1,0:T(4,128)S(1)}, u32[]{:S(2)}, u32[]{:S(2)}) %collective-permute-start.1) | collective-permute-done | bytes 15584 | tf_op jit(solution)/shard_map/ppermute | solution.py:717
  13.4 3.7 %collective-permute-start.5 = (f32[3,1296]{1,0:T(4,128)S(1)}, f32[3,1296]{1,0:T(4,128)S(1)}, u32[]{:S(2)}, u32[]{:S(2)}) collective-permute-start(f32[3,1296]{1,0:T(4,128)S(1)} %add_add_fusion.1), channel_id=1, source_target_pairs={{0,12},{1,13},{2,14},{3,15},{4,8},{5,9},{6,10},{7,11},{8,4},{9,5},... | collective-permute-start | bytes 46664 | tf_op jit(solution)/shard_map/ppermute | solution.py:717
  19.1 2.7 %collective-permute-done.4 = f32[3,1296]{1,0:T(4,128)S(1)} collective-permute-done((f32[3,1296]{1,0:T(4,128)S(1)}, f32[3,1296]{1,0:T(4,128)S(1)}, u32[]{:S(2)}, u32[]{:S(2)}) %collective-permute-start.4) | collective-permute-done | bytes 15584 | tf_op jit(solution)/shard_map/ppermute | solution.py:717
  22.0 22.9 %middle.1 = (bf16[196,216]{1,0:T(8,128)(2,1)S(1)}, bf16[196,216]{1,0:T(8,128)(2,1)S(1)}, f32[196,216]{1,0:T(8,128)S(1)}, bf16[224,216]{1,0:T(8,128)(2,1)S(1)}, b...) custom-call(s32[2,4]{1,0:T(2,128)S(1)} %copy-done.21, ...), custom_call_target="tpu_custom_call" | custom-call | flops 4294967296 | bytes 8388608 | tf_op jit(solution)/shard_map/middle/pallas_call | solution.py:703
  45.2 3.0 %collective-permute-done.7 = bf16[16,2,10,16,128]{4,3,2,0,1:T(8,128)(2,1)S(1)} collective-permute-done((bf16[16,2,10,16,128]{4,3,2,0,1:T(8,128)(2,1)S(1)}, bf16[16,2,10,16,128]{4,3,2,0,1:T(8,128)(2,1)S(1)}, u32[]{:S(2)}, u32[]{:S(2)}) %collective-permute-start.7) | collective-permute-done | bytes 1310752 | tf_op jit(solution)/shard_map/ppermute | solution.py:717
  51.1 1.5 %collective-permute-start.10 = (bf16[8,10,16,128]{3,2,1,0:T(8,128)(2,1)}, bf16[8,10,16,128]{3,2,1,0:T(8,128)(2,1)S(1)}, u32[]{:S(2)}, u32[]{:S(2)}) collective-permute-start(bf16[8,10,16,128]{3,2,1,0:T(8,128)(2,1)} %get-tuple-element.145), channel_id=1, source_target_pairs={{0,2},{1,3},{2,0},{3,1},{4,6},{5,7},{6,4},{7,5},{8,10},{9,11},{10,... | collective-permute-start | bytes 983048 | tf_op jit(solution)/shard_map/ppermute | solution.py:717
  52.6 8.0 %collective-permute-done.8 = bf16[84,16,128]{2,1,0:T(8,128)(2,1)S(1)} collective-permute-done((bf16[84,16,128]{2,1,0:T(8,128)(2,1)S(1)}, bf16[84,16,128]{2,1,0:T(8,128)(2,1)S(1)}, u32[]{:S(2)}, u32[]{:S(2)}) %collective-permute-start.8) | collective-permute-done | bytes 344096 | tf_op jit(solution)/shard_map/ppermute | solution.py:717
  62.1 1.5 %collective-permute-start.11 = (bf16[4,10,16,128]{3,2,1,0:T(8,128)(2,1)S(1)}, bf16[4,10,16,128]{3,2,1,0:T(8,128)(2,1)S(1)}, u32[]{:S(2)}, u32[]{:S(2)}) collective-permute-start(bf16[4,10,16,128]{3,2,1,0:T(8,128)(2,1)S(1)} %slice.186), channel_id=1, source_target_pairs={{0,1},{1,0},{2,3},{3,2},{4,5},{5,4},{6,7},{7,6},{8,9},{9,8},{10,11... | collective-permute-start | bytes 491528 | tf_op jit(solution)/shard_map/ppermute | solution.py:717
  63.7 1.6 %collective-permute-start.9 = (bf16[44,16,128]{2,1,0:T(8,128)(2,1)S(1)}, bf16[44,16,128]{2,1,0:T(8,128)(2,1)S(1)}, u32[]{:S(2)}, u32[]{:S(2)}) collective-permute-start(bf16[44,16,128]{2,1,0:T(8,128)(2,1)S(1)} %pad_maximum_fusion.6), channel_id=1, source_target_pairs={{0,2},{1,3},{2,0},{3,1},{4,6},{5,7},{6,4},{7,5},{8,10},{9,11},{10,... | collective-permute-start | bytes 540680 | tf_op jit(solution)/shard_map/ppermute | solution.py:717
  65.3 2.2 %collective-permute-done.11 = bf16[4,10,16,128]{3,2,1,0:T(8,128)(2,1)S(1)} collective-permute-done((bf16[4,10,16,128]{3,2,1,0:T(8,128)(2,1)S(1)}, bf16[4,10,16,128]{3,2,1,0:T(8,128)(2,1)S(1)}, u32[]{:S(2)}, u32[]{:S(2)}) %collective-permute-start.11) | collective-permute-done | bytes 163872 | tf_op jit(solution)/shard_map/ppermute | solution.py:717
  67.6 1.7 %collective-permute-done.9 = bf16[44,16,128]{2,1,0:T(8,128)(2,1)S(1)} collective-permute-done((bf16[44,16,128]{2,1,0:T(8,128)(2,1)S(1)}, bf16[44,16,128]{2,1,0:T(8,128)(2,1)S(1)}, u32[]{:S(2)}, u32[]{:S(2)}) %collective-permute-start.9) | collective-permute-done | bytes 180256 | tf_op jit(solution)/shard_map/ppermute | solution.py:717
  69.4 2.1 %collective-permute-start.12 = (bf16[24,16,128]{2,1,0:T(8,128)(2,1)S(1)}, bf16[24,16,128]{2,1,0:T(8,128)(2,1)S(1)}, u32[]{:S(2)}, u32[]{:S(2)}) collective-permute-start(bf16[24,16,128]{2,1,0:T(8,128)(2,1)S(1)} %get-tuple-element.154), channel_id=1, source_target_pairs={{0,8},{1,9},{2,10},{3,11},{4,12},{5,13},{6,14},{7,15},{8,0},{9,1},... | collective-permute-start | bytes 294920 | tf_op jit(solution)/shard_map/ppermute | solution.py:717
  71.5 2.4 %collective-permute-start.14 = (bf16[24,16,128]{2,1,0:T(8,128)(2,1)S(1)}, bf16[24,16,128]{2,1,0:T(8,128)(2,1)S(1)}, u32[]{:S(2)}, u32[]{:S(2)}) collective-permute-start(bf16[24,16,128]{2,1,0:T(8,128)(2,1)S(1)} %get-tuple-element.156), channel_id=1, source_target_pairs={{0,12},{1,13},{2,14},{3,15},{4,8},{5,9},{6,10},{7,11},{8,4},{9,5},... | collective-permute-start | bytes 294920 | tf_op jit(solution)/shard_map/ppermute | solution.py:717
  74.0 4.2 %collective-permute-done.12 = bf16[24,16,128]{2,1,0:T(8,128)(2,1)S(1)} collective-permute-done((bf16[24,16,128]{2,1,0:T(8,128)(2,1)S(1)}, bf16[24,16,128]{2,1,0:T(8,128)(2,1)S(1)}, u32[]{:S(2)}, u32[]{:S(2)}) %collective-permute-start.12) | collective-permute-done | bytes 98336 | tf_op jit(solution)/shard_map/ppermute | solution.py:717
  78.6 1.9 %collective-permute-start.18 = (bf16[1,22,16,128]{3,2,1,0:T(8,128)(2,1)S(1)}, bf16[1,22,16,128]{3,2,1,0:T(8,128)(2,1)S(1)}, u32[]{:S(2)}, u32[]{:S(2)}) collective-permute-start(bf16[1,22,16,128]{3,2,1,0:T(8,128)(2,1)S(1)} %pad_maximum_fusion.11.refs_1_), channel_id=1, source_target_pairs={{0,12},{1,13},{2,14},{3,15},{4,8},{5,9},{6,10},{7,11},{8,4},{9,5},... | collective-permute-start | bytes 270344 | tf_op jit(solution)/shard_map/ppermute | solution.py:717
  81.1 2.0 %collective-permute-start.16 = (bf16[1,22,16,128]{3,2,1,0:T(8,128)(2,1)S(1)}, bf16[1,22,16,128]{3,2,1,0:T(8,128)(2,1)S(1)}, u32[]{:S(2)}, u32[]{:S(2)}) collective-permute-start(bf16[1,22,16,128]{3,2,1,0:T(8,128)(2,1)S(1)} %pad_maximum_fusion.11.refs_1_), channel_id=1, source_target_pairs={{0,8},{1,9},{2,10},{3,11},{4,12},{5,13},{6,14},{7,15},{8,0},{9,1},... | collective-permute-start | bytes 270344 | tf_op jit(solution)/shard_map/ppermute | solution.py:717
  83.1 2.1 %collective-permute-done.18.refs_4_ = bf16[1,22,16,128]{3,2,1,0:T(8,128)(2,1)S(1)} collective-permute-done((bf16[1,22,16,128]{3,2,1,0:T(8,128)(2,1)S(1)}, bf16[1,22,16,128]{3,2,1,0:T(8,128)(2,1)S(1)}, u32[]{:S(2)}, u32[]{:S(2)}) %collective-permute-start.18) | collective-permute-done | bytes 90144 | tf_op jit(solution)/shard_map/ppermute | solution.py:717
  85.2 1.8 %collective-permute-done.17.refs_3_ = bf16[1,22,16,128]{3,2,1,0:T(8,128)(2,1)S(1)} collective-permute-done((bf16[1,22,16,128]{3,2,1,0:T(8,128)(2,1)S(1)}, bf16[1,22,16,128]{3,2,1,0:T(8,128)(2,1)S(1)}, u32[]{:S(2)}, u32[]{:S(2)}) %collective-permute-start.17) | collective-permute-done | bytes 90144 | tf_op jit(solution)/shard_map/ppermute | solution.py:717
  87.1 1.6 %collective-permute-start.19 = (bf16[4,12,16,128]{3,2,1,0:T(8,128)(2,1)S(1)}, bf16[4,12,16,128]{3,2,1,0:T(8,128)(2,1)S(1)}, u32[]{:S(2)}, u32[]{:S(2)}) collective-permute-start(bf16[4,12,16,128]{3,2,1,0:T(8,128)(2,1)S(1)} %slice.207), channel_id=1, source_target_pairs={{0,2},{1,3},{2,0},{3,1},{4,6},{5,7},{6,4},{7,5},{8,10},{9,11},{10,... | collective-permute-start | bytes 589832 | tf_op jit(solution)/shard_map/ppermute | solution.py:717
  90.1 3.8 %collective-permute-done.19.refs_5_ = bf16[4,12,16,128]{3,2,1,0:T(8,128)(2,1)S(1)} collective-permute-done((bf16[4,12,16,128]{3,2,1,0:T(8,128)(2,1)S(1)}, bf16[4,12,16,128]{3,2,1,0:T(8,128)(2,1)S(1)}, u32[]{:S(2)}, u32[]{:S(2)}) %collective-permute-start.19) | collective-permute-done | bytes 196640 | tf_op jit(solution)/shard_map/ppermute | solution.py:717
  94.0 1.9 %collective-permute-start.20 = (bf16[8,12,16,128]{3,2,1,0:T(8,128)(2,1)S(1)}, bf16[8,12,16,128]{3,2,1,0:T(8,128)(2,1)S(1)}, u32[]{:S(2)}, u32[]{:S(2)}) collective-permute-start(bf16[8,12,16,128]{3,2,1,0:T(8,128)(2,1)S(1)} %pad_maximum_fusion.2), channel_id=1, source_target_pairs={{0,1},{1,0},{2,3},{3,2},{4,5},{5,4},{6,7},{7,6},{8,9},{9,8},{10,11... | collective-permute-start | bytes 1179656 | tf_op jit(solution)/shard_map/ppermute | solution.py:717
  97.5 4.3 %collective-permute-done.20.refs_6_ = bf16[8,12,16,128]{3,2,1,0:T(8,128)(2,1)S(1)} collective-permute-done((bf16[8,12,16,128]{3,2,1,0:T(8,128)(2,1)S(1)}, bf16[8,12,16,128]{3,2,1,0:T(8,128)(2,1)S(1)}, u32[]{:S(2)}, u32[]{:S(2)}) %collective-permute-start.20) | collective-permute-done | bytes 393248 | tf_op jit(solution)/shard_map/ppermute | solution.py:717
  107.4 4.4 %unpack.1 = (f32[216,1296]{1,0:T(8,128)}, f32[1296]{0:T(1024)}, f32[1296]{0:T(1024)}, f32[9,1296]{1,0:T(8,128)}, f32[324,1296]{1,0:T(8,128)}, /*index=5*/f32[324...) custom-call(bf16[216,1296]{1,0:T(8,128)(2,1)S(1)} %copy-done.2, ...), custom_call_target="tpu_custom_call" | custom-call | flops 67108864 | bytes 8388608 | tf_op jit(solution)/shard_map/unpack/pallas_call | solution.py:703
  (146 shorter events, 23.0 us)
Async XLA Ops:
  5.1 5.7 %collective-permute-start.2 = (f32[3,1296]{1,0:T(4,128)S(1)}, f32[3,1296]{1,0:T(4,128)S(1)}, u32[]{:S(2)}, u32[]{:S(2)}) collective-permute-start(f32[3,1296]{1,0:T(4,128)S(1)} %sums.1), channel_id=1, source_target_pairs={{0,3},{1,2},{2,1},{3,0},{4,7},{5,6},{6,5},{7,4},{8,11},{9,10},{10,... | collective-permute-start | bytes 46664 | tf_op jit(solution)/shard_map/ppermute | solution.py:717
  9.1 3.8 %collective-permute-start.1 = (f32[3,1296]{1,0:T(4,128)S(1)}, f32[3,1296]{1,0:T(4,128)S(1)}, u32[]{:S(2)}, u32[]{:S(2)}) collective-permute-start(f32[3,1296]{1,0:T(4,128)S(1)} %sums.1), channel_id=1, source_target_pairs={{0,2},{1,3},{2,0},{3,1},{4,6},{5,7},{6,4},{7,5},{8,10},{9,11},{10,... | collective-permute-start | bytes 46664 | tf_op jit(solution)/shard_map/ppermute | solution.py:717
  9.6 3.8 %collective-permute-start = (f32[3,1296]{1,0:T(4,128)S(1)}, f32[3,1296]{1,0:T(4,128)S(1)}, u32[]{:S(2)}, u32[]{:S(2)}) collective-permute-start(f32[3,1296]{1,0:T(4,128)S(1)} %sums.1), channel_id=1, source_target_pairs={{0,1},{1,0},{2,3},{3,2},{4,5},{5,4},{6,7},{7,6},{8,9},{9,8},{10,11... | collective-permute-start | bytes 46664 | tf_op jit(solution)/shard_map/ppermute | solution.py:717
  13.4 5.7 %collective-permute-start.5 = (f32[3,1296]{1,0:T(4,128)S(1)}, f32[3,1296]{1,0:T(4,128)S(1)}, u32[]{:S(2)}, u32[]{:S(2)}) collective-permute-start(f32[3,1296]{1,0:T(4,128)S(1)} %add_add_fusion.1), channel_id=1, source_target_pairs={{0,12},{1,13},{2,14},{3,15},{4,8},{5,9},{6,10},{7,11},{8,4},{9,5},... | collective-permute-start | bytes 46664 | tf_op jit(solution)/shard_map/ppermute | solution.py:717
  17.1 4.7 %collective-permute-start.4 = (f32[3,1296]{1,0:T(4,128)S(1)}, f32[3,1296]{1,0:T(4,128)S(1)}, u32[]{:S(2)}, u32[]{:S(2)}) collective-permute-start(f32[3,1296]{1,0:T(4,128)S(1)} %add_add_fusion.1), channel_id=1, source_target_pairs={{0,8},{1,9},{2,10},{3,11},{4,12},{5,13},{6,14},{7,15},{8,0},{9,1},... | collective-permute-start | bytes 46664 | tf_op jit(solution)/shard_map/ppermute | solution.py:717
  17.1 4.7 %collective-permute-start.3 = (f32[3,1296]{1,0:T(4,128)S(1)}, f32[3,1296]{1,0:T(4,128)S(1)}, u32[]{:S(2)}, u32[]{:S(2)}) collective-permute-start(f32[3,1296]{1,0:T(4,128)S(1)} %add_add_fusion.1), channel_id=1, source_target_pairs={{0,4},{1,5},{2,6},{3,7},{4,0},{5,1},{6,2},{7,3},{8,12},{9,13},{10,... | collective-permute-start | bytes 46664 | tf_op jit(solution)/shard_map/ppermute | solution.py:717
  45.1 3.1 %collective-permute-start.7 = (bf16[16,2,10,16,128]{4,3,2,0,1:T(8,128)(2,1)S(1)}, bf16[16,2,10,16,128]{4,3,2,0,1:T(8,128)(2,1)S(1)}, u32[]{:S(2)}, u32[]{:S(2)}) collective-permute-start(bf16[16,2,10,16,128]{4,3,2,0,1:T(8,128)(2,1)S(1)} %copy.58), channel_id=1, source_target_pairs={{0,16},{16,0},{1,17},{17,1},{2,18},{18,2},{3,19},{19,3},{4,20},{20... | collective-permute-start | bytes 3932168 | tf_op jit(solution)/shard_map/ppermute | solution.py:717
  50.5 10.2 %collective-permute-start.8 = (bf16[84,16,128]{2,1,0:T(8,128)(2,1)S(1)}, bf16[84,16,128]{2,1,0:T(8,128)(2,1)S(1)}, u32[]{:S(2)}, u32[]{:S(2)}) collective-permute-start(bf16[84,16,128]{2,1,0:T(8,128)(2,1)S(1)} %pad_maximum_fusion.4), channel_id=1, source_target_pairs={{0,1},{1,0},{2,3},{3,2},{4,5},{5,4},{6,7},{7,6},{8,9},{9,8},{10,11... | collective-permute-start | bytes 1032200 | tf_op jit(solution)/shard_map/ppermute | solution.py:717
  51.1 9.7 %collective-permute-start.10 = (bf16[8,10,16,128]{3,2,1,0:T(8,128)(2,1)}, bf16[8,10,16,128]{3,2,1,0:T(8,128)(2,1)S(1)}, u32[]{:S(2)}, u32[]{:S(2)}) collective-permute-start(bf16[8,10,16,128]{3,2,1,0:T(8,128)(2,1)} %get-tuple-element.145), channel_id=1, source_target_pairs={{0,2},{1,3},{2,0},{3,1},{4,6},{5,7},{6,4},{7,5},{8,10},{9,11},{10,... | collective-permute-start | bytes 983048 | tf_op jit(solution)/shard_map/ppermute | solution.py:717
  62.1 5.4 %collective-permute-start.11 = (bf16[4,10,16,128]{3,2,1,0:T(8,128)(2,1)S(1)}, bf16[4,10,16,128]{3,2,1,0:T(8,128)(2,1)S(1)}, u32[]{:S(2)}, u32[]{:S(2)}) collective-permute-start(bf16[4,10,16,128]{3,2,1,0:T(8,128)(2,1)S(1)} %slice.186), channel_id=1, source_target_pairs={{0,1},{1,0},{2,3},{3,2},{4,5},{5,4},{6,7},{7,6},{8,9},{9,8},{10,11... | collective-permute-start | bytes 491528 | tf_op jit(solution)/shard_map/ppermute | solution.py:717
  63.7 5.6 %collective-permute-start.9 = (bf16[44,16,128]{2,1,0:T(8,128)(2,1)S(1)}, bf16[44,16,128]{2,1,0:T(8,128)(2,1)S(1)}, u32[]{:S(2)}, u32[]{:S(2)}) collective-permute-start(bf16[44,16,128]{2,1,0:T(8,128)(2,1)S(1)} %pad_maximum_fusion.6), channel_id=1, source_target_pairs={{0,2},{1,3},{2,0},{3,1},{4,6},{5,7},{6,4},{7,5},{8,10},{9,11},{10,... | collective-permute-start | bytes 540680 | tf_op jit(solution)/shard_map/ppermute | solution.py:717
  69.4 8.8 %collective-permute-start.12 = (bf16[24,16,128]{2,1,0:T(8,128)(2,1)S(1)}, bf16[24,16,128]{2,1,0:T(8,128)(2,1)S(1)}, u32[]{:S(2)}, u32[]{:S(2)}) collective-permute-start(bf16[24,16,128]{2,1,0:T(8,128)(2,1)S(1)} %get-tuple-element.154), channel_id=1, source_target_pairs={{0,8},{1,9},{2,10},{3,11},{4,12},{5,13},{6,14},{7,15},{8,0},{9,1},... | collective-permute-start | bytes 294920 | tf_op jit(solution)/shard_map/ppermute | solution.py:717
  71.5 7.0 %collective-permute-start.13 = (bf16[24,16,128]{2,1,0:T(8,128)(2,1)S(1)}, bf16[24,16,128]{2,1,0:T(8,128)(2,1)S(1)}, u32[]{:S(2)}, u32[]{:S(2)}) collective-permute-start(bf16[24,16,128]{2,1,0:T(8,128)(2,1)S(1)} %get-tuple-element.155), channel_id=1, source_target_pairs={{0,4},{1,5},{2,6},{3,7},{4,0},{5,1},{6,2},{7,3},{8,12},{9,13},{10,... | collective-permute-start | bytes 294920 | tf_op jit(solution)/shard_map/ppermute | solution.py:717
  71.5 7.0 %collective-permute-start.14 = (bf16[24,16,128]{2,1,0:T(8,128)(2,1)S(1)}, bf16[24,16,128]{2,1,0:T(8,128)(2,1)S(1)}, u32[]{:S(2)}, u32[]{:S(2)}) collective-permute-start(bf16[24,16,128]{2,1,0:T(8,128)(2,1)S(1)} %get-tuple-element.156), channel_id=1, source_target_pairs={{0,12},{1,13},{2,14},{3,15},{4,8},{5,9},{6,10},{7,11},{8,4},{9,5},... | collective-permute-start | bytes 294920 | tf_op jit(solution)/shard_map/ppermute | solution.py:717
  73.9 31.2 %collective-permute-start.6 = (bf16[196,216]{1,0:T(8,128)(2,1)S(1)}, bf16[196,216]{1,0:T(8,128)(2,1)S(1)}, u32[]{:S(2)}, u32[]{:S(2)}) collective-permute-start(bf16[196,216]{1,0:T(8,128)(2,1)S(1)} %broadcast_select_fusion.1), channel_id=1, source_target_pairs={{0,16},{16,0},{1,17},{17,1},{2,18},{18,2},{3,19},{19,3},{4,20},{20... | collective-permute-start | bytes 254024 | tf_op jit(solution)/shard_map/ppermute | solution.py:717
  78.6 6.6 %collective-permute-start.18 = (bf16[1,22,16,128]{3,2,1,0:T(8,128)(2,1)S(1)}, bf16[1,22,16,128]{3,2,1,0:T(8,128)(2,1)S(1)}, u32[]{:S(2)}, u32[]{:S(2)}) collective-permute-start(bf16[1,22,16,128]{3,2,1,0:T(8,128)(2,1)S(1)} %pad_maximum_fusion.11.refs_1_), channel_id=1, source_target_pairs={{0,12},{1,13},{2,14},{3,15},{4,8},{5,9},{6,10},{7,11},{8,4},{9,5},... | collective-permute-start | bytes 270344 | tf_op jit(solution)/shard_map/ppermute | solution.py:717
  80.6 6.4 %collective-permute-start.17 = (bf16[1,22,16,128]{3,2,1,0:T(8,128)(2,1)S(1)}, bf16[1,22,16,128]{3,2,1,0:T(8,128)(2,1)S(1)}, u32[]{:S(2)}, u32[]{:S(2)}) collective-permute-start(bf16[1,22,16,128]{3,2,1,0:T(8,128)(2,1)S(1)} %pad_maximum_fusion.11.refs_1_), channel_id=1, source_target_pairs={{0,4},{1,5},{2,6},{3,7},{4,0},{5,1},{6,2},{7,3},{8,12},{9,13},{10,... | collective-permute-start | bytes 270344 | tf_op jit(solution)/shard_map/ppermute | solution.py:717
  81.1 5.9 %collective-permute-start.16 = (bf16[1,22,16,128]{3,2,1,0:T(8,128)(2,1)S(1)}, bf16[1,22,16,128]{3,2,1,0:T(8,128)(2,1)S(1)}, u32[]{:S(2)}, u32[]{:S(2)}) collective-permute-start(bf16[1,22,16,128]{3,2,1,0:T(8,128)(2,1)S(1)} %pad_maximum_fusion.11.refs_1_), channel_id=1, source_target_pairs={{0,8},{1,9},{2,10},{3,11},{4,12},{5,13},{6,14},{7,15},{8,0},{9,1},... | collective-permute-start | bytes 270344 | tf_op jit(solution)/shard_map/ppermute | solution.py:717
  87.1 6.8 %collective-permute-start.19 = (bf16[4,12,16,128]{3,2,1,0:T(8,128)(2,1)S(1)}, bf16[4,12,16,128]{3,2,1,0:T(8,128)(2,1)S(1)}, u32[]{:S(2)}, u32[]{:S(2)}) collective-permute-start(bf16[4,12,16,128]{3,2,1,0:T(8,128)(2,1)S(1)} %slice.207), channel_id=1, source_target_pairs={{0,2},{1,3},{2,0},{3,1},{4,6},{5,7},{6,4},{7,5},{8,10},{9,11},{10,... | collective-permute-start | bytes 589832 | tf_op jit(solution)/shard_map/ppermute | solution.py:717
  88.7 7.2 %collective-permute-start.22 = (bf16[4,10,16,128]{3,2,1,0:T(8,128)(2,1)S(1)}, bf16[4,10,16,128]{3,2,1,0:T(8,128)(2,1)S(1)}, u32[]{:S(2)}, u32[]{:S(2)}) collective-permute-start(bf16[4,10,16,128]{3,2,1,0:T(8,128)(2,1)S(1)} %pad_maximum_fusion.7), channel_id=1, source_target_pairs={{0,1},{1,0},{2,3},{3,2},{4,5},{5,4},{6,7},{7,6},{8,9},{9,8},{10,11... | collective-permute-start | bytes 491528 | tf_op jit(solution)/shard_map/ppermute | solution.py:717
  94.0 7.8 %collective-permute-start.20 = (bf16[8,12,16,128]{3,2,1,0:T(8,128)(2,1)S(1)}, bf16[8,12,16,128]{3,2,1,0:T(8,128)(2,1)S(1)}, u32[]{:S(2)}, u32[]{:S(2)}) collective-permute-start(bf16[8,12,16,128]{3,2,1,0:T(8,128)(2,1)S(1)} %pad_maximum_fusion.2), channel_id=1, source_target_pairs={{0,1},{1,0},{2,3},{3,2},{4,5},{5,4},{6,7},{7,6},{8,9},{9,8},{10,11... | collective-permute-start | bytes 1179656 | tf_op jit(solution)/shard_map/ppermute | solution.py:717
  96.0 7.1 %collective-permute-start.23 = (bf16[8,10,16,128]{3,2,1,0:T(8,128)(2,1)S(1)}, bf16[8,10,16,128]{3,2,1,0:T(8,128)(2,1)S(1)}, u32[]{:S(2)}, u32[]{:S(2)}) collective-permute-start(bf16[8,10,16,128]{3,2,1,0:T(8,128)(2,1)S(1)} %pad_maximum_fusion.5), channel_id=1, source_target_pairs={{0,2},{1,3},{2,0},{3,1},{4,6},{5,7},{6,4},{7,5},{8,10},{9,11},{10,... | collective-permute-start | bytes 983048 | tf_op jit(solution)/shard_map/ppermute | solution.py:717
  101.9 5.5 %collective-permute-start.21 = (bf16[16,12,16,128]{3,2,1,0:T(8,128)(2,1)S(1)}, bf16[16,12,16,128]{3,2,1,0:T(8,128)(2,1)S(1)}, u32[]{:S(2)}, u32[]{:S(2)}) collective-permute-start(bf16[16,12,16,128]{3,2,1,0:T(8,128)(2,1)S(1)} %pad_maximum_fusion), channel_id=1, source_target_pairs={{0,16},{16,0},{1,17},{17,1},{2,18},{18,2},{3,19},{19,3},{4,20},{20... | collective-permute-start | bytes 2359304 | tf_op jit(solution)/shard_map/ppermute | solution.py:717
  103.2 4.2 %collective-permute-start.24 = (bf16[16,10,16,128]{3,2,1,0:T(8,128)(2,1)S(1)}, bf16[16,10,16,128]{3,2,1,0:T(8,128)(2,1)S(1)}, u32[]{:S(2)}, u32[]{:S(2)}) collective-permute-start(bf16[16,10,16,128]{3,2,1,0:T(8,128)(2,1)S(1)} %pad_maximum_fusion.1), channel_id=1, source_target_pairs={{0,16},{16,0},{1,17},{17,1},{2,18},{18,2},{3,19},{19,3},{4,20},{20... | collective-permute-start | bytes 1966088 | tf_op jit(solution)/shard_map/ppermute | solution.py:717
  (30 other events, 436.7 us)

commit v2 on v1

v2 whole, which is shorter than its diff:
```python
import functools
import math

import jax
import jax.numpy as jnp
from jax import lax
from jax.experimental import pallas as pl
from jax.experimental.pallas import tpu as pltpu
from jax.sharding import PartitionSpec as P

D = 216
E = 1296
SQ = 324
HEADS = 12
HD = 18
F = 864
SIDE = 14
PIX = 196
EPSILON = 1e-05
LOG2E = 1.4426950408889634

WIDE = 16
ROWS = SIDE * WIDE
LANES = 128
EB = -(-E // LANES)
FB = -(-F // LANES)
DB = -(-D // LANES)
EP = EB * LANES
FP = FB * LANES
DP = DB * LANES
QB = -(-3 * D // LANES)
QP = QB * LANES

PROJECT = 0
HIDDEN = PROJECT + EB - 1
RETURN = HIDDEN + FB
QKV = RETURN + FB
OUTPUT = QKV + QB - 1
COVARIANCE = OUTPUT + DB
EXPAND = COVARIANCE + DB
BLOCKS = EXPAND + EB - 1
PROJECT_TAIL = HIDDEN + FB - 1
EXPAND_TAIL = RETURN + FB - 1
QKV_TAIL = OUTPUT + DB - 1
TAIL_LANE = 96
TILES = ROWS // 16
ALL_TILES = BLOCKS * TILES
PARTS = 2
RIDDEN = 1
FACTOR_ROWS = 32
WEIGHTS = 18
UNPACKED = 26

f32 = jnp.float32
bf16 = jnp.bfloat16
HIGHEST = lax.Precision.HIGHEST
MIB = 1 << 20


def dot(a, b, contract=((1,), (0,)), precision=None):
    return lax.dot_general(a, b, (contract, ((), ())), preferred_element_type=f32, precision=precision)


NT = ((1,), (1,))


def iota(shape, dim):
    return lax.broadcasted_iota(jnp.int32, shape, dim)


def sigmoid(v):
    return 0.5 * jnp.tanh(0.5 * v) + 0.5


def silu_and_slope(half, live):
    turn = jnp.tanh(half)
    more = 1.0 + turn
    return half * more, (more * (1.0 + half * (1.0 - turn))) * live


def grid_mask(shape, side):
    row = iota(shape, 0)
    return jnp.where(((row >> 4) < side) & ((row & 15) < side), 1.0, 0.0)


def widen(tokens, side):
    row = iota((ROWS, PIX), 0)
    hit = iota((ROWS, PIX), 1) == (row >> 4) * SIDE + (row & 15)
    pick = jnp.where(hit & ((row >> 4) < side) & ((row & 15) < side), 1.0, 0.0).astype(bf16)
    return dot(pick, tokens)


def narrow(tokens):
    column = iota((PIX, ROWS), 1)
    hit = iota((PIX, ROWS), 0) == (column >> 4) * SIDE + (column & 15)
    pick = jnp.where(hit & ((column & 15) < SIDE), 1.0, 0.0).astype(bf16)
    return dot(pick, tokens)


def narrow_into(ref, tokens):
    for i in range(SIDE):
        ref[i * SIDE : (i + 1) * SIDE, :] = tokens[i * WIDE : i * WIDE + SIDE, :]


def grid(v):
    return v.reshape(SIDE, WIDE, v.shape[-1])


def flat(v):
    return v.reshape(ROWS, v.shape[-1])


def sideways(ref, v):
    ref[8 : 8 + ROWS] = v
    return [ref[7 : 7 + ROWS], v, ref[9 : 9 + ROWS]]


def depthwise(three, kernel):
    rows = [sum(kernel[3 * a + b] * three[b] for b in range(3)) for a in range(3)]
    zero = jnp.zeros((1, WIDE, LANES), f32)
    above = flat(jnp.concatenate([zero, grid(rows[0])[:-1]], axis=0))
    below = flat(jnp.concatenate([grid(rows[2])[1:], zero], axis=0))
    return rows[1] + above + below


def depthwise_kernel_grad(three, v):
    v3 = grid(v)
    taps = []
    for a in (-1, 0, 1):
        for b in (-1, 0, 1):
            g3 = grid(three[1 - b])
            if a < 0:
                product = v3[:-1] * g3[1:]
            elif a > 0:
                product = v3[1:] * g3[:-1]
            else:
                product = v3 * g3
            taps.append(jnp.sum(jnp.sum(product, axis=0), axis=0, keepdims=True))
    return taps


def norm_forward(v):
    centred = v - jnp.sum(v, axis=-1, keepdims=True) * (1.0 / D)
    rs = lax.rsqrt(jnp.sum(centred * centred, axis=-1, keepdims=True) * (1.0 / D) + EPSILON)
    return centred * rs, rs


def norm_backward(grad, hat, rs, gain):
    scaled = grad * gain
    first = jnp.sum(scaled, axis=-1, keepdims=True) * (1.0 / D)
    second = jnp.sum(scaled * hat, axis=-1, keepdims=True) * (1.0 / D)
    return rs * (scaled - first - hat * second)


def row_sum(v):
    return jnp.sum(v, axis=0, keepdims=True)


def vector_times(row, matrix, contract):
    high = row.astype(bf16).astype(f32)
    rest = row - high
    mid = rest.astype(bf16).astype(f32)
    low = rest - mid
    which = iota((16, row.shape[-1]), 0)
    stack = jnp.where(which == 0, high, jnp.where(which == 1, mid, jnp.where(which == 2, low, 0.0)))
    return row_sum(dot(stack.astype(bf16), matrix, contract))


def moments(sums, count):
    average = sums[0:1] / count
    variance = sums[1:2] / count - average * average
    return average, lax.rsqrt(variance + EPSILON)


def put_block(tiles_ref, block, grad, smalls):
    tiles_ref[block * TILES : (block + 1) * TILES] = (
        jnp.concatenate([grad, smalls], axis=0).astype(bf16).reshape(TILES, 16, LANES)
    )


def add_tail(tiles_ref, block, grad, smalls):
    at = slice(block * TILES, (block + 1) * TILES)
    tail = pltpu.roll(jnp.concatenate([grad, smalls], axis=0), TAIL_LANE, 1)
    held = tiles_ref[at].reshape(ROWS, LANES).astype(f32)
    tiles_ref[at] = (held + tail).astype(bf16).reshape(TILES, 16, LANES)


def block_of(v, b):
    return v[:, b * LANES : (b + 1) * LANES]


def code_of(codes):
    mine = lax.axis_index("pipe")
    return SIDE - 4 + 2 * codes[mine, 3], codes[mine, 0], codes[mine, 1], codes[mine, 2]


def home_of(order):
    spot = lax.axis_index("dp")
    home = lax.axis_index("pipe")
    for b in order:
        home = home * 2 + ((spot >> b) & 1)
    return home


def fetch(sources, targets, sems):
    copies = [pltpu.make_async_copy(a, b, sems.at[i]) for i, (a, b) in enumerate(zip(sources, targets))]
    for copy in copies:
        copy.start()
    return copies


def sums_kernel(codes, image, expand_hbm, sums_out, expand, sems):
    (expand_copy,) = fetch([expand_hbm], [expand], sems)
    side = code_of(codes)[0]
    tokens = widen(image[...], side).astype(bf16)
    expand_copy.wait()
    expanded = dot(tokens, expand[...])
    sums_out[0:1, :] = row_sum(expanded)
    sums_out[1:2, :] = row_sum(expanded * expanded)
    sums_out[2:3, :] = jnp.zeros((1, E), f32)
    sums_out[2:3, :D] = row_sum(tokens.astype(f32))


def middle_kernel(
    images_total,
    pieces,
    per_piece,
    orders,
    codes,
    image,
    cotangent,
    sums,
    gain,
    bias,
    squeeze_bias,
    excite_bias,
    hidden_bias,
    *refs,
):
    (
        first_out,
        second_out,
        handed_grad_out,
        handed_low_out,
        tokens_out,
        expanded_grad_out,
        batch_out,
        kept_out,
        sent_out,
        factors_out,
        tiles_out,
        wide_e,
        wide_f,
        live,
        half_live,
        beside,
        half_scale,
        expanded_s,
        deep_grad,
        active_e,
        slope_e,
        deep_s,
        scaled_s,
        mixes,
        three_s,
        keys_wide,
        soft_s,
        all_soft,
        all_grad,
        all_keys,
        all_values,
        hidden_s,
        slope_s,
        active_s,
        hidden_low_s,
        up_s,
        smalls_e,
        tail_e,
        smalls_f,
        grad_k,
        grad_v,
        talk_s,
        projected_s,
    ) = refs[WEIGHTS:]
    (
        expand,
        depth_one,
        squeeze_t,
        excite,
        project_t,
        norm_gain,
        norm_bias,
        qkv,
        talk_before,
        talk_after,
        output,
        output_bias,
        mlp_gain,
        mlp_bias,
        hidden,
        depth_two,
        return_t,
        return_bias,
    ) = refs[:WEIGHTS]
    side, code_channels, code_heads, code_units = code_of(codes)
    pixels = (side * side).astype(f32)
    count = images_total * pixels
    live[...] = grid_mask((ROWS, LANES), side)
    half_live[...] = 0.5 * live[...]
    live_d = grid_mask((ROWS, D), side)

    average, inverse = moments(sums[...], count)
    wide_e[...] = jnp.zeros_like(wide_e)
    channel_mask = jnp.where(iota((1, E), 1) < E - (2 - code_channels) * D, 1.0, 0.0)
    wide_e[0:1, :E] = average
    wide_e[1:2, :E] = inverse * gain[...]
    wide_e[2:3, :E] = bias[...]
    wide_e[3:4, :E] = channel_mask
    wide_e[4:13, :E] = depth_one[...] * channel_mask
    wide_e[15:16, :E] = inverse
    tokens = widen(image[...], side).astype(bf16)
    tokens_out[...] = tokens
    token_mean = sums[2:3, :D] / count
    centred_tokens = (tokens.astype(f32) - token_mean) * live_d
    expanded_s[:, E - E % LANES :] = jnp.zeros((ROWS, EP - E + E % LANES), f32)
    expanded_s[:, :E] = dot(tokens, expand[...])

    beside[...] = jnp.zeros_like(beside)
    half_scale[0:1, :] = 0.5 * wide_e[1:2, :]
    half_scale[1:2, :] = 0.5 * (wide_e[2:3, :] - wide_e[0:1, :] * wide_e[1:2, :])

    def forward_one(c, carry):
        at = pl.ds(c * LANES, LANES)
        silu, slope = silu_and_slope(expanded_s[:, at] * half_scale[0:1, at] + half_scale[1:2, at], half_live[...])
        active = silu * live[...]
        active_e[:, at] = active
        slope_e[:, at] = slope
        deep = depthwise(sideways(beside.at[c % 3], active), [wide_e[4 + t : 5 + t, at] for t in range(9)]) * live[...]
        deep_s[:, at] = deep
        wide_e[14:15, at] = row_sum(deep) / pixels
        return carry

    for c in range(EB):
        forward_one(c, 0)
    pooled = wide_e[14:15, :E]
    squeeze_pre = vector_times(pooled, squeeze_t[...], NT) + squeeze_bias[...]
    squeeze_gate = sigmoid(squeeze_pre)
    squeezed = squeeze_pre * squeeze_gate
    excited = sigmoid(vector_times(squeezed, excite[...], ((1,), (0,))) + excite_bias[...])
    wide_e[13:14, :E] = excited
    scaled_s[...] = (deep_s[...] * wide_e[13:14, :]).astype(bf16)
    branch = dot(scaled_s[:, :E], project_t[...], NT)
    handed_low = (tokens.astype(f32) + branch).astype(bf16)
    first_out[...] = narrow(handed_low).astype(bf16)
    handed = handed_low.astype(f32)

    hat_one, rs_one = norm_forward(handed)
    normed_one = (hat_one * norm_gain[...] + norm_bias[...]).astype(bf16)
    projected = dot(normed_one, qkv[...]).astype(bf16).astype(f32)
    live_heads = HEADS - 2 * (2 - code_heads)
    own = jnp.where((iota((HEADS, DP), 1) >= iota((HEADS, DP), 0) * HD), 1.0, 0.0)
    own = jnp.where((iota((HEADS, DP), 1) < iota((HEADS, DP), 0) * HD + HD), own, 0.0)
    own_t = jnp.where((iota((DP, HEADS), 0) >= iota((DP, HEADS), 1) * HD), 1.0, 0.0)
    own_t = jnp.where((iota((DP, HEADS), 0) < iota((DP, HEADS), 1) * HD + HD), own_t, 0.0)
    head_row = jnp.where(iota((1, HEADS), 1) < live_heads, 1.0, 0.0)
    value_mask = jnp.where(iota((1, DP), 1) < live_heads * HD, 1.0, 0.0)
    before = talk_before[...] * head_row * HD ** (-0.5)
    after = talk_after[...] * head_row
    mixes[...] = jnp.zeros_like(mixes)
    mixes[0:HEADS] = dot(before, own, precision=HIGHEST)
    mixes[16 : 16 + HEADS] = dot(after, own, ((0,), (0,)), precision=HIGHEST)
    columns = mixes[...].T
    before_columns = columns[:, 0:16]
    after_columns = columns[:, 16:32]

    three_s[...] = jnp.zeros_like(three_s)
    for which in range(3):
        three_s[which, 0:ROWS, 0:D] = projected[:, which * D : (which + 1) * D]
    three_s[2, 0:ROWS] = three_s[2, 0:ROWS] * value_mask

    spare = iota((ROWS, DP), 1) == D
    row_place = iota((ROWS, DP), 0)
    dead = ((row_place >> 4) >= side) | ((row_place & 15) >= side)
    keys_wide[...] = jnp.where(spare & dead, -1000000000.0, three_s[1, 0:ROWS])
    queries_t = jnp.where(iota((DP, DP), 1) == D, 1.0, three_s[0]).T.astype(bf16)
    queries_twice = jnp.concatenate([queries_t, queries_t], axis=0)
    queries_low = three_s[0].astype(bf16)
    keys_t = three_s[1].T[0:D]
    values_t = three_s[2].T[0:D]
    before_wide = jnp.where(iota((HEADS, DP), 1) == D, 1.0, mixes[0:HEADS] * LOG2E)
    all_soft[:, ROWS:] = jnp.zeros((HEADS, DP - ROWS, DP), bf16)
    all_grad[:, ROWS:] = jnp.zeros((HEADS, DP - ROWS, DP), bf16)
    for h in range(HEADS):
        weighted = keys_wide[...] * before_wide[h : h + 1]
        high = weighted.astype(bf16)
        low = (weighted - high.astype(f32)).astype(bf16)
        scores = dot(jnp.concatenate([high, low], axis=1), queries_twice)
        grown = jnp.exp2(scores - jnp.max(scores, axis=0, keepdims=True))
        soft = grown * (1.0 / row_sum(grown))
        soft_s[h] = soft
        all_soft[h, 0:ROWS] = soft.astype(bf16)
    for h in range(HEADS):
        all_values[:, h * DP : (h + 1) * DP] = (values_t * after_columns[0:D, h : h + 1]).astype(bf16)
    for h in range(HEADS):
        all_keys[:, h * DP : (h + 1) * DP] = (keys_t * before_columns[0:D, h : h + 1]).astype(bf16)
    heads_out_t = dot(all_values[...], all_soft[...].reshape(HEADS * DP, DP))
    heads_out_low = heads_out_t[:, 0:ROWS].astype(bf16)
    heads_out = heads_out_t.T[0:ROWS].astype(bf16)
    attended = dot(heads_out, output[...]) + output_bias[...]
    middle = handed + attended * live_d

    hat_two, rs_two = norm_forward(middle)
    normed_two_f = hat_two * mlp_gain[...] + mlp_bias[...]
    normed_two = normed_two_f.astype(bf16)
    wide_f[...] = jnp.zeros_like(wide_f)
    wide_f[0:1, :F] = hidden_bias[...]
    unit_mask = jnp.where(iota((1, F), 1) < F - (2 - code_units) * D, 1.0, 0.0)
    wide_f[1:2, :F] = unit_mask
    wide_f[2:11, :F] = depth_two[...] * unit_mask
    hidden_s[:, F - F % LANES :] = jnp.zeros((ROWS, FP - F + F % LANES), f32)
    hidden_s[:, :F] = dot(normed_two, hidden[...])

    def forward_two(c, carry):
        at = pl.ds(c * LANES, LANES)
        units = (hidden_s[:, at] + wide_f[0:1, at]) * live[...]
        hidden_s[:, at] = units
        conv = depthwise(sideways(beside.at[c % 3], units), [wide_f[2 + t : 3 + t, at] for t in range(9)]) * live[...]
        silu, slope = silu_and_slope(0.5 * conv, half_live[...])
        slope_s[:, at] = slope
        active_s[:, at] = silu.astype(bf16)
        return carry

    for c in range(FB):
        forward_two(c, 0)
    final = middle + dot(active_s[:, :F], return_t[...], NT) + return_bias[...]
    second_out[...] = narrow((final * live_d).astype(bf16)).astype(bf16)

    upstream = widen(cotangent[...], side)
    grad_return_bias = row_sum(upstream)
    up_s[:, F - F % LANES :] = jnp.zeros((ROWS, FP - F + F % LANES), f32)
    up_s[:, :F] = dot(upstream.astype(bf16), return_t[...])
    smalls_f[...] = jnp.zeros_like(smalls_f)

    def backward_two(c, carry):
        at = pl.ds(c * LANES, LANES)
        three = sideways(beside.at[c % 3], up_s[:, at] * slope_s[:, at])
        taps = depthwise_kernel_grad(three, hidden_s[:, at])
        for t in range(9):
            smalls_f[t : t + 1, at] = taps[t] * wide_f[1:2, at]
        flipped = [wide_f[10 - t : 11 - t, at] for t in range(9)]
        grad_units = depthwise(three, flipped) * live[...]
        smalls_f[9:10, at] = row_sum(grad_units)
        hidden_low_s[:, at] = grad_units.astype(bf16)
        return carry

    for c in range(FB):
        backward_two(c, 0)
    grad_return = dot(upstream.T.astype(bf16), active_s[...])
    for b in range(FB):
        put_block(tiles_out, RETURN + b, block_of(grad_return, b), smalls_f[8:16, b * LANES : (b + 1) * LANES])
    grad_hidden = dot(normed_two_f.T.astype(bf16), hidden_low_s[...])
    for b in range(FB):
        put_block(tiles_out, HIDDEN + b, block_of(grad_hidden, b), smalls_f[0:8, b * LANES : (b + 1) * LANES])
    grad_normed_two = dot(hidden_low_s[:, :F], hidden[...], NT)
    grad_mlp_gain = row_sum(grad_normed_two * hat_two)
    grad_mlp_bias = row_sum(grad_normed_two)
    grad_middle = upstream + norm_backward(grad_normed_two, hat_two, rs_two, mlp_gain[...])

    attend_up = grad_middle * live_d
    grad_output_bias = row_sum(attend_up)
    attend_low = attend_up.astype(bf16)
    grad_output = dot(heads_out_low, attend_low)
    three_s[0] = jnp.zeros((DP, DP), f32)
    three_s[0, 0:ROWS, 0:D] = dot(attend_low, output[...], NT)
    grad_heads_low = three_s[0].astype(bf16)
    grad_heads_t = three_s[0].T.astype(bf16)
    grad_k[...] = jnp.zeros_like(grad_k)
    grad_v[...] = jnp.zeros_like(grad_v)
    weighted = [(three_s[2, 0:ROWS] * mixes[16 + h : 17 + h]).astype(bf16) for h in range(HEADS)]
    grads_soft = dot(jnp.concatenate(weighted, axis=0), grad_heads_t)

    def scores_back(h):
        soft = soft_s[h]
        grad_soft = grads_soft[h * ROWS : (h + 1) * ROWS]
        all_grad[h, 0:ROWS] = (soft * (grad_soft - row_sum(soft * grad_soft))).astype(bf16)

    for h in range(HEADS):
        scores_back(h)
    backs = dot(all_grad[...].reshape(HEADS * DP, DP), queries_low)
    for h in range(HEADS):
        back = backs[h * DP : h * DP + ROWS]
        grad_k[...] += back * mixes[h : h + 1]
        talk_s[h : h + 1, :] = row_sum(back * three_s[1, 0:ROWS])
    backs = dot(all_soft[...].reshape(HEADS * DP, DP), grad_heads_low)
    for h in range(HEADS):
        back = backs[h * DP : h * DP + ROWS]
        grad_v[...] += back * mixes[16 + h : 17 + h]
        talk_s[16 + h : 17 + h, :] = row_sum(back * three_s[2, 0:ROWS])
    grad_q = dot(all_keys[...], all_grad[...].reshape(HEADS * DP, DP)).T[0:ROWS]
    talk_before_grad = dot(talk_s[0:12, :], own_t, precision=HIGHEST) * (head_row * HD ** (-0.5))
    talk_after_grad = dot(own_t, talk_s[16:28, :], ((0,), (1,)), precision=HIGHEST) * head_row
    projected_s[:, :D] = grad_q
    projected_s[:, D : 2 * D] = grad_k[:, :D]
    projected_s[:, 2 * D :] = (grad_v[...] * value_mask)[:, :D]
    grad_projected = projected_s[...].astype(bf16)
    grad_normed_one = dot(grad_projected, qkv[...], NT)
    normed_one_t = (hat_one * norm_gain[...] + norm_bias[...]).T.astype(bf16)
    grad_norm_gain = row_sum(grad_normed_one * hat_one)
    grad_norm_bias = row_sum(grad_normed_one)
    handed_grad = grad_middle + norm_backward(grad_normed_one, hat_one, rs_one, norm_gain[...])
    narrow_into(handed_grad_out, handed_grad)

    talk_s[...] = jnp.zeros_like(talk_s)
    talk_s[0:12, 0:HEADS] = talk_before_grad
    talk_s[16:28, 0:HEADS] = talk_after_grad
    grad_qkv = jnp.concatenate([dot(normed_one_t, grad_projected), jnp.zeros((D, QP - 3 * D), f32)], axis=1)
    for b in range(QB - 1):
        extra = talk_s[8 * b : 8 * b + 8, 0:LANES] if b < 4 else jnp.zeros((8, LANES), f32)
        put_block(tiles_out, QKV + b, block_of(grad_qkv, b), extra)
    talk_s[0:8, :] = jnp.zeros((8, DP), f32)
    talk_s[0:1, :D] = grad_norm_gain
    talk_s[1:2, :D] = grad_norm_bias
    talk_s[2:3, :D] = grad_output_bias
    talk_s[3:4, :D] = grad_mlp_gain
    talk_s[4:5, :D] = grad_mlp_bias
    talk_s[5:6, :D] = grad_return_bias
    leading = lax.axis_index("pipe") == 0
    centred_low = centred_tokens.astype(bf16)
    centred_t = centred_tokens.T.astype(bf16)
    covariance = dot(centred_t, centred_low)
    over = iota((D, D), 0) - iota((D, D), 1)
    over = jnp.where(leading, over, -over)
    talk_s[6:7, :D] = jnp.where(leading, 0.0, row_sum(jnp.where(over == 0, covariance, 0.0)))
    wanted = (over < 0) | ((over == 0) & leading)
    covariance = jnp.concatenate([jnp.where(wanted, covariance, 0.0), jnp.zeros((D, DP - D), f32)], axis=1)
    for b in range(DB):
        put_block(tiles_out, COVARIANCE + b, block_of(covariance, b), jnp.zeros((8, LANES), f32))
    for b in range(DB):
        piece = jnp.concatenate([grad_output, jnp.zeros((D, DP - D), f32)], axis=1)
        extra = talk_s[0:8, :]
        put_block(tiles_out, OUTPUT + b, block_of(piece, b), block_of(extra, b))
    add_tail(tiles_out, QKV_TAIL, block_of(grad_qkv, QB - 1), jnp.zeros((8, LANES), f32))

    back_low = handed_grad.astype(bf16)
    handed_low_out[...] = back_low
    deep_grad[:, E - E % LANES :] = jnp.zeros((ROWS, EP - E + E % LANES), f32)
    deep_grad[:, :E] = dot(back_low, project_t[...])

    excited = wide_e[13:14, :E]
    grad_excited = row_sum(deep_grad[:, :E] * deep_s[:, :E])
    grad_excite_pre = grad_excited * excited * (1.0 - excited)
    grad_squeezed = vector_times(grad_excite_pre, excite[...], NT)
    grad_squeeze_pre = grad_squeezed * (squeeze_gate * (1.0 + squeeze_pre * (1.0 - squeeze_gate)))
    grad_pooled = vector_times(grad_squeeze_pre, squeeze_t[...], ((1,), (0,)))
    factors_out[...] = jnp.zeros_like(factors_out)

    def put_factor(start, row):
        width = row.shape[-1]
        for b in range(-(-width // LANES)):
            end = min(width, (b + 1) * LANES)
            factors_out[start + b : start + b + 1, 0 : end - b * LANES] = row[:, b * LANES : end]

    put_factor(0, wide_e[14:15, :E])
    put_factor(EB, grad_excite_pre)
    put_factor(2 * EB, squeezed)
    put_factor(2 * EB + 3, grad_squeeze_pre)
    wide_e[14:15, :E] = grad_pooled / pixels
    tail_e[...] = jnp.zeros_like(tail_e)
    batch_out[...] = jnp.zeros_like(batch_out)

    def backward_one(c, carry):
        at = pl.ds(c * LANES, LANES)
        grad_deep = (deep_grad[:, at] * wide_e[13:14, at] + wide_e[14:15, at]) * live[...]
        three = sideways(beside.at[c % 3], grad_deep)
        taps = depthwise_kernel_grad(three, active_e[:, at])
        for t in range(8):
            smalls_e[t : t + 1, at] = taps[t] * wide_e[3:4, at]
        flipped = [wide_e[12 - t : 13 - t, at] for t in range(9)]
        grad_normed = depthwise(three, flipped) * slope_e[:, at]
        centred = expanded_s[:, at] - wide_e[0:1, at]
        grad_gain = row_sum(grad_normed * centred) * wide_e[15:16, at]
        grad_bias = row_sum(grad_normed)
        batch_out[pl.ds(c, 1), :] = grad_gain
        batch_out[pl.ds(c + 16, 1), :] = grad_bias
        tail_e[0:1, at] = grad_gain
        tail_e[1:2, at] = grad_bias
        tail_e[2:3, at] = taps[8] * wide_e[3:4, at]
        grad_second = grad_gain * wide_e[15:16, at] * wide_e[1:2, at] * (-1.0 / count)
        tail_e[3:4, at] = jnp.where(leading, grad_second, 0.0)
        tail_e[4:5, at] = jnp.where(leading, 0.0, grad_second)
        expanded_grad_out[:, at] = (grad_normed * wide_e[1:2, at]).astype(bf16)
        return carry

    for c in range(EB):
        backward_one(c, 0)
    grad_project = dot(handed_grad.T.astype(bf16), scaled_s[...])
    for b in range(EB - 1):
        put_block(tiles_out, PROJECT + b, block_of(grad_project, b), smalls_e[:, b * LANES : (b + 1) * LANES])
    add_tail(tiles_out, PROJECT_TAIL, block_of(grad_project, EB - 1), smalls_e[:, EP - LANES :])
    grad_expand = dot(centred_t, expanded_grad_out[...])
    for b in range(EB - 1):
        put_block(tiles_out, EXPAND + b, block_of(grad_expand, b), tail_e[:, b * LANES : (b + 1) * LANES])
    add_tail(tiles_out, EXPAND_TAIL, block_of(grad_expand, EB - 1), tail_e[:, EP - LANES :])
    spare = tiles_out.shape[0] - ALL_TILES
    if spare:
        tiles_out[ALL_TILES:] = jnp.zeros((spare, 16, LANES), bf16)

    half = pieces // 2
    mine = lax.axis_index("pipe")
    base = 0
    for part, order in enumerate(orders):
        size = per_piece[part]
        me = home_of(order) & (half - 1)
        for piece in range(half):
            first = base * 2 + piece * size
            to = pl.ds(base + (piece ^ me) * size, size)
            kept_out[to] = tiles_out[pl.ds(first + mine * half * size, size)]
            sent_out[to] = tiles_out[pl.ds(first + (1 - mine) * half * size, size)]
        base += half * size


RIDE_TILES = 4


def ridden_sum(batch, arrivals):
    total = batch[...].reshape(2, 16, LANES)
    for ref in arrivals:
        end = ref.shape[0]
        total = total + (ref[end - 4 : end - 2].astype(f32) + ref[end - 2 : end].astype(f32))
    return total


def put_ride(ref, total):
    high = total.astype(bf16)
    end = ref.shape[0]
    ref[end - 4 : end - 2] = high
    ref[end - 2 : end] = (total - high.astype(f32)).astype(bf16)


def added(terms, at):
    return functools.reduce(jnp.add, [term[at].astype(f32) for term in terms]).astype(bf16)


def halves_kernel(count, size, rides, *refs):
    if rides:
        own, other, batch, kept, sent, batch_out = refs
        total = ridden_sum(batch, [other] if other.shape[0] > 2 * count * size else [])
        batch_out[...] = total.reshape(batch_out.shape)
        put_ride(sent, total)
    else:
        own, other, kept, sent = refs
    for i in range(count):
        here = slice(i * size, (i + 1) * size)
        there = slice((count + i) * size, (count + i + 1) * size)
        kept[here] = added([own, other], here)
        sent[here] = added([own, other], there)


def pieces_kernel(count, rows, sizes, terms_of, *refs):
    terms = []
    refs = list(refs)
    for number in terms_of:
        terms.append([refs.pop(0) for _ in range(number)])
    batch = refs.pop(0)
    batch_out = refs.pop()
    whole = count * rows * sizes[-1]
    total = ridden_sum(batch, [ref for ref in terms[-1] if ref.shape[0] > whole])
    batch_out[...] = total.reshape(batch_out.shape)
    for j, out in enumerate(refs):
        if j:
            put_ride(out, total)
        for i in range(rows):
            at = i * sum(sizes)
            for part, size in zip(terms, sizes):
                out[at : at + size] = added(part, slice((j * rows + i) * size, (j * rows + i + 1) * size))
                at += size


def finish_kernel(own, *refs):
    *others, batch, factors, held, batch_out = refs
    size = own.shape[0]
    batch_out[...] = ridden_sum(batch, others).reshape(batch_out.shape)
    held[0:size] = added([own, *others], slice(0, size))
    held[size:] = factors[...].astype(bf16).reshape(FACTOR_ROWS // 16, 16, LANES)


def side_by_side_kernel(sizes, *refs):
    outs = refs[len(refs) - len(sizes) :]
    rows = 0
    for ref in refs[: len(refs) - len(sizes)]:
        count = ref.shape[0] // sum(sizes)
        for i in range(count):
            at = i * sum(sizes)
            for out, size in zip(outs, sizes):
                out[rows * size : (rows + 1) * size] = ref[at : at + size]
                at += size
            rows += 1


def last_kernel(
    images_total, codes, sums, total, gain, tokens, handed_low, expanded_grad, expand, grad_out, wide
):
    side = code_of(codes)[0]
    count = images_total * (side * side).astype(f32)
    average, inverse = moments(sums[...], count)
    scale = inverse * gain[...]
    for b in range(EB):
        wide[0:1, b * LANES : (b + 1) * LANES] = total[b : b + 1, :]
        wide[1:2, b * LANES : (b + 1) * LANES] = total[16 + b : 17 + b, :]
    grad_variance = -0.5 * inverse * scale * wide[0:1, :E]
    grad_second = grad_variance / count
    grad_first = (-scale * wide[1:2, :E] - 2.0 * average * grad_variance) / count
    expanded = dot(tokens[...], expand[...])
    grad = (expanded_grad[:, :E].astype(f32) + grad_first + 2.0 * expanded * grad_second).astype(bf16)
    grad_tokens = (handed_low[...].astype(f32) + dot(grad, expand[...], NT)) * grid_mask((ROWS, D), side)
    narrow_into(grad_out, grad_tokens)


def unpack_kernel(pieces, per_piece, orders, merged, *refs):
    expand, *refs = refs
    single = (len(refs) - UNPACKED - merged) // PARTS
    inputs = refs[: merged + PARTS * single]
    (
        expand_out,
        gain_out,
        bias_out,
        depth_one_out,
        squeeze_out,
        squeeze_bias_out,
        excite_out,
        excite_bias_out,
        project_out,
        norm_gain_out,
        norm_bias_out,
        qkv_out,
        talk_before_out,
        talk_after_out,
        output_out,
        output_bias_out,
        mlp_gain_out,
        mlp_bias_out,
        hidden_out,
        hidden_bias_out,
        depth_two_out,
        return_out,
        return_bias_out,
        tiles,
        factors,
        wide,
    ) = refs[merged + PARTS * single :]
    for part, order in enumerate(orders):
        me = home_of(order)
        size = per_piece[part]
        base = sum(per_piece[:part])
        at = 0
        riding = FACTOR_ROWS // 16
        own = inputs[merged + part * single : merged + (part + 1) * single]
        for number, ref in enumerate(inputs[:merged] + own):
            width = sum(per_piece) + riding if number < merged else size + riding * (part == RIDDEN)
            skipped = base if number < merged else 0
            for inner in range(ref.shape[0] // width):
                home = at ^ me
                start = inner * width + skipped
                tiles[pl.ds(base * pieces + home * size, size)] = ref[start : start + size]
                if part == RIDDEN:
                    factor = ref[start + size : start + size + riding]
                    factors[home] = factor.reshape(FACTOR_ROWS, LANES).astype(f32)
                at += 1

    def block(b):
        return tiles[b * TILES : (b + 1) * TILES].reshape(ROWS, LANES).astype(f32)

    def spread(first, count, width, out, take, tail=None):
        for b in range(count):
            value = block(first + b) if b < count - 1 or tail is None else pltpu.roll(block(tail), LANES - TAIL_LANE, 1)
            start, stop = b * LANES, min(width, (b + 1) * LANES)
            out[:, start:stop] = value[0:D, 0 : stop - start]
            for ref, top, row, rows in take:
                if len(ref.shape) == 1:
                    ref[start:stop] = value[D + row, 0 : stop - start]
                else:
                    ref[top : top + rows, start:stop] = value[D + row : D + row + rows, 0 : stop - start]

    spread(PROJECT, EB, E, project_out, [(depth_one_out, 0, 0, 8)], PROJECT_TAIL)
    spread(HIDDEN, FB, F, hidden_out, [(depth_two_out, 0, 0, 8)])
    spread(RETURN, FB, F, return_out, [(depth_two_out, 8, 0, 1), (hidden_bias_out, 0, 1, 1)])
    spread(QKV, QB, 3 * D, qkv_out, [], QKV_TAIL)

    def gathered(start, width):
        columns = [factors[:, start + b, :] for b in range(-(-width // LANES))]
        return jnp.concatenate(columns, axis=1)[:, 0:width]

    pooled = gathered(0, E)
    grad_excite_pre = gathered(EB, E)
    squeezed = gathered(2 * EB, SQ)
    grad_squeeze_pre = gathered(2 * EB + 3, SQ)
    squeeze_out[...] = dot(grad_squeeze_pre.T.astype(bf16), pooled.astype(bf16))
    excite_out[...] = dot(squeezed.T.astype(bf16), grad_excite_pre.astype(bf16))
    squeeze_bias_out[...] = jnp.sum(grad_squeeze_pre, axis=0)
    excite_bias_out[...] = jnp.sum(grad_excite_pre, axis=0)

    tail = pltpu.roll(block(EXPAND_TAIL), LANES - TAIL_LANE, 1)
    for b in range(EB):
        value = block(EXPAND + b) if b < EB - 1 else tail
        wide[:, b * LANES : (b + 1) * LANES] = value
    gain_out[...] = wide[D, 0:E]
    bias_out[...] = wide[D + 1, 0:E]
    depth_one_out[8:9, :] = wide[D + 2 : D + 3, 0:E]
    both = jnp.concatenate([block(COVARIANCE), block(COVARIANCE + 1)], axis=1)[0:D, 0:D]
    turned = both.T
    over = iota((D, D), 0) - iota((D, D), 1)
    diagonal = jnp.concatenate([block(OUTPUT)[D + 6 : D + 7], block(OUTPUT + 1)[D + 6 : D + 7]], axis=1)[:, 0:D]
    first = jnp.where(over <= 0, both, turned).astype(bf16)
    second = jnp.where(over > 0, both, jnp.where(over < 0, turned, diagonal)).astype(bf16)
    added = dot(first, expand[...]) * wide[D + 3 : D + 4, 0:E] + dot(second, expand[...]) * wide[D + 4 : D + 5, 0:E]
    expand_out[...] = wide[0:D, 0:E] + added
    vectors = (norm_gain_out, norm_bias_out, output_bias_out, mlp_gain_out, mlp_bias_out, return_bias_out)
    spread(OUTPUT, DB, D, output_out, [(ref, 0, row, 1) for row, ref in enumerate(vectors)])
    talk_before_out[0:8] = block(QKV)[D : D + 8, 0:HEADS]
    talk_before_out[8:12] = block(QKV + 1)[D : D + 4, 0:HEADS]
    talk_after_out[0:8] = block(QKV + 2)[D : D + 8, 0:HEADS]
    talk_after_out[8:12] = block(QKV + 3)[D : D + 4, 0:HEADS]

def kernel_call(body, name, shapes, scratch, operands, fetched, limit, flops):
    in_specs = [pl.BlockSpec(memory_space=pltpu.VMEM)] * len(operands)
    if fetched is not None:
        in_specs[0] = pl.BlockSpec(memory_space=pltpu.SMEM)
        in_specs += [pl.BlockSpec(memory_space=pltpu.HBM)] * len(fetched)
    return pl.pallas_call(
        body,
        out_shape=[jax.ShapeDtypeStruct(shape, kind) for shape, kind in shapes],
        in_specs=in_specs,
        out_specs=[pl.BlockSpec(memory_space=pltpu.VMEM)] * len(shapes),
        scratch_shapes=scratch,
        compiler_params=pltpu.CompilerParams(vmem_limit_bytes=limit * MIB),
        cost_estimate=pl.CostEstimate(flops=flops, bytes_accessed=8 * MIB, transcendentals=0),
        name=name,
    )(*operands, *(fetched or ()))


def swapped(value, axis, mask):
    size = lax.axis_size(axis)
    return lax.ppermute(value, axis, [(i, i ^ mask) for i in range(size)])


def summed_over_dp(value, bits):
    for first in range(0, bits, 2):
        here = [1 << b for b in range(first, min(first + 2, bits))]
        masks = here + ([here[0] | here[1]] if len(here) == 2 else [])
        others = [swapped(value, "dp", mask) for mask in masks]
        value = value + functools.reduce(jnp.add, others)
    return value


def on_device(
    images,
    codes,
    cotangent,
    expand_weight,
    batch_gain,
    batch_bias,
    depth_one,
    squeeze_weight,
    squeeze_bias,
    excite_weight,
    excite_bias,
    project_weight,
    norm_gain,
    norm_bias,
    qkv_weight,
    talk_before,
    talk_after,
    output_weight,
    output_bias,
    mlp_gain,
    mlp_bias,
    hidden_weight,
    hidden_bias,
    depth_two,
    return_weight,
    return_bias,
):
    devices_dp = lax.axis_size("dp")
    bits = devices_dp.bit_length() - 1
    pieces = 2 * devices_dp
    half = pieces // 2
    images_total = float(images.shape[1] * devices_dp)
    per_piece = -(-ALL_TILES // pieces)
    per_piece = [per_piece - per_piece // 2, per_piece // 2]
    factor_tiles = FACTOR_ROWS // 16
    pipe = lax.axis_index("pipe")

    rest = list(range(2, bits))
    groups = [rest[g : g + 2] for g in range(0, len(rest), 2)]
    orders = [[1, 0] + rest, [0, 1] + rest]
    image = lax.dynamic_index_in_dim(images, pipe, 0, keepdims=False)[0]
    upstream = lax.dynamic_index_in_dim(cotangent, pipe, 0, keepdims=False)[0]

    def row(vector):
        return vector.reshape(1, -1)

    def buffers(arrays):
        return [pltpu.VMEM(a.shape, a.dtype) for a in arrays]

    squeeze_t = squeeze_weight.T
    project_t = project_weight.T
    return_t = return_weight.T
    gain = row(batch_gain)

    (sums,) = kernel_call(
        sums_kernel,
        "sums",
        [((3, E), f32)],
        buffers([expand_weight]) + [pltpu.SemaphoreType.DMA((1,))],
        (codes, image),
        (expand_weight,),
        16,
        1 << 33,
    )
    sums = summed_over_dp(sums, bits)

    operands = (
        codes,
        image,
        upstream,
        sums,
        gain,
        row(batch_bias),
        row(squeeze_bias),
        row(excite_bias),
        row(hidden_bias),
        expand_weight,
        depth_one,
        squeeze_t,
        excite_weight,
        project_t,
        row(norm_gain),
        row(norm_bias),
        qkv_weight,
        talk_before,
        talk_after,
        output_weight,
        row(output_bias),
        row(mlp_gain),
        row(mlp_bias),
        hidden_weight,
        depth_two,
        return_t,
        row(return_bias),
    )
    shapes = [
        ((PIX, D), bf16),
        ((PIX, D), bf16),
        ((PIX, D), f32),
        ((ROWS, D), bf16),
        ((ROWS, D), bf16),
        ((ROWS, EP), bf16),
        ((32, LANES), f32),
        ((sum(per_piece) * half, 16, LANES), bf16),
        ((sum(per_piece) * half, 16, LANES), bf16),
        ((FACTOR_ROWS, LANES), f32),
    ]
    scratch = [
        pltpu.VMEM((sum(per_piece) * pieces, 16, LANES), bf16),
        pltpu.VMEM((16, EP), f32),
        pltpu.VMEM((16, FP), f32),
        pltpu.VMEM((ROWS, LANES), f32),
        pltpu.VMEM((ROWS, LANES), f32),
        pltpu.VMEM((3, ROWS + 16, LANES), f32),
        pltpu.VMEM((8, EP), f32),
        pltpu.VMEM((ROWS, EP), f32),
        pltpu.VMEM((ROWS, EP), f32),
        pltpu.VMEM((ROWS, EP), f32),
        pltpu.VMEM((ROWS, EP), f32),
        pltpu.VMEM((ROWS, EP), f32),
        pltpu.VMEM((ROWS, EP), bf16),
        pltpu.VMEM((32, DP), f32),
        pltpu.VMEM((3, DP, DP), f32),
        pltpu.VMEM((ROWS, DP), f32),
        pltpu.VMEM((HEADS, ROWS, DP), f32),
        pltpu.VMEM((HEADS, DP, DP), bf16),
        pltpu.VMEM((HEADS, DP, DP), bf16),
        pltpu.VMEM((D, HEADS * DP), bf16),
        pltpu.VMEM((D, HEADS * DP), bf16),
        pltpu.VMEM((ROWS, FP), f32),
        pltpu.VMEM((ROWS, FP), f32),
        pltpu.VMEM((ROWS, FP), bf16),
        pltpu.VMEM((ROWS, FP), bf16),
        pltpu.VMEM((ROWS, FP), f32),
        pltpu.VMEM((8, EP), f32),
        pltpu.VMEM((8, EP), f32),
        pltpu.VMEM((16, FP), f32),
        pltpu.VMEM((ROWS, DP), f32),
        pltpu.VMEM((ROWS, DP), f32),
        pltpu.VMEM((32, DP), f32),
        pltpu.VMEM((ROWS, 3 * D), f32),
    ]
    first, second, handed_grad, handed_low, tokens, expanded_grad, batch, kept, sent, factors = kernel_call(
        functools.partial(middle_kernel, images_total, pieces, per_piece, orders),
        "middle",
        shapes,
        scratch,
        operands,
        (),
        40,
        1 << 32,
    )

    def masks_of(group):
        return [sum(1 << b for i, b in enumerate(group) if (j >> (len(group) - 1 - i)) & 1) for j in range(1 << len(group))]

    def tiles_of(count):
        return ((count, 16, LANES), bf16)

    def small_kernel(body, name, shapes, operands):
        return kernel_call(body, name, shapes, [], operands, None, 2, 1 << 20)

    arrived = swapped(sent, "pipe", 1)
    cuts = [0, half * per_piece[0], half * sum(per_piece)]
    terms = [[value[cuts[part] : cuts[part + 1]] for value in (kept, arrived)] for part in range(PARTS)]
    held = [None] * PARTS
    count = half
    for step in range(2):
        count //= 2
        for part, order in enumerate(orders):
            size = per_piece[part]
            rides = part == RIDDEN
            body = functools.partial(halves_kernel, count, size, rides)
            shapes = [tiles_of(count * size), tiles_of(count * size + RIDE_TILES * rides)]
            if rides:
                mine, going, batch = small_kernel(body, "halves", shapes + [((32, LANES), f32)], (*terms[part], batch))
            else:
                mine, going = small_kernel(body, "halves", shapes, terms[part])
            held[part] = (mine, swapped(going, "dp", 1 << order[step]))
        terms = [list(pair) for pair in held]
    sizes = per_piece
    for group in groups:
        masks = masks_of(group)
        count //= len(masks)
        body = functools.partial(pieces_kernel, len(masks), count, sizes, [len(part) for part in terms])
        shapes = [tiles_of(count * sum(sizes) + (RIDE_TILES if j else 0)) for j in range(len(masks))]
        *going, batch = small_kernel(
            body, "pieces", shapes + [((32, LANES), f32)], (*[term for part in terms for term in part], batch)
        )
        sizes = [sum(sizes)]
        terms = [[going[0]] + [swapped(value, "dp", mask) for value, mask in zip(going[1:], masks[1:])]]
    held, batch = small_kernel(
        finish_kernel, "finish", [tiles_of(sum(sizes) + factor_tiles), ((32, LANES), f32)], (*terms[0], batch, factors)
    )
    (images_grad,) = kernel_call(
        functools.partial(last_kernel, images_total),
        "last",
        [((PIX, D), f32)],
        [pltpu.VMEM((2, EP), f32)],
        (codes, sums, batch, gain, tokens, handed_low, expanded_grad, expand_weight),
        (),
        16,
        1 << 31,
    )

    sizes = [per_piece[0], per_piece[1] + factor_tiles]
    merged = [held]
    for number, group in enumerate(reversed(groups)):
        merged += [swapped(held, "dp", mask) for mask in masks_of(group)[1:]]
        count *= 1 << len(group)
        if number < len(groups) - 1:
            (held,) = small_kernel(
                functools.partial(side_by_side_kernel, [sum(sizes)]), "together", [tiles_of(count * sum(sizes))], merged
            )
    held = list(
        small_kernel(
            functools.partial(side_by_side_kernel, sizes), "apart", [tiles_of(count * size) for size in sizes], merged
        )
    )
    held, images_grad = lax.optimization_barrier((held, images_grad))
    held = list(held)

    leading = pipe == 0

    def both_layers(one, two):
        other = swapped(jnp.where(leading, two, one), "pipe", 1)
        return jnp.where(leading, jnp.stack([one, other]), jnp.stack([other, two]))[None, :, None]

    activations = both_layers(first, second)
    input_grads = both_layers(images_grad, handed_grad)
    collected = [[], []]
    for step in (1, 0):
        arrived = [swapped(value, "dp", 1 << order[step]) for value, order in zip(held[::-1], orders[::-1])][::-1]
        count *= 2
        for part, size in enumerate(sizes):
            collected[part].append(arrived[part])
            (held[part],) = small_kernel(
                functools.partial(side_by_side_kernel, [size]),
                "together",
                [tiles_of(count * size)],
                (held[part], arrived[part]),
            )
    held, activations, input_grads = lax.optimization_barrier((held, activations, input_grads))
    for part in range(PARTS):
        collected[part].append(swapped(held[part], "pipe", 1))
    grads = kernel_call(
        functools.partial(unpack_kernel, pieces, per_piece, orders, len(merged)),
        "unpack",
        [
            ((D, E), f32),
            ((E,), f32),
            ((E,), f32),
            ((9, E), f32),
            ((SQ, E), f32),
            ((SQ,), f32),
            ((SQ, E), f32),
            ((E,), f32),
            ((D, E), f32),
            ((D,), f32),
            ((D,), f32),
            ((D, 3 * D), f32),
            ((HEADS, HEADS), f32),
            ((HEADS, HEADS), f32),
            ((D, D), f32),
            ((D,), f32),
            ((D,), f32),
            ((D,), f32),
            ((D, F), f32),
            ((F,), f32),
            ((9, F), f32),
            ((D, F), f32),
            ((D,), f32),
        ],
        [
            pltpu.VMEM((sum(per_piece) * pieces, 16, LANES), bf16),
            pltpu.VMEM((pieces, FACTOR_ROWS, LANES), f32),
            pltpu.VMEM((ROWS, EP), f32),
        ],
        (expand_weight, *merged, *collected[0], *collected[1]),
        None,
        40,
        1 << 26,
    )
    grads = list(grads)
    for transposed in (4, 8, 21):
        grads[transposed] = grads[transposed].T

    return (activations, input_grads, *grads)


def solution(mesh):
    in_specs = (P(None, "dp", None, None), P(), P(None, "dp", None, None)) + (P(),) * 23
    out_specs = (P("pipe", None, "dp", None, None), P("pipe", None, "dp", None, None)) + (P(),) * 23
    return jax.shard_map(on_device, mesh=mesh, in_specs=in_specs, out_specs=out_specs, check_vma=False)
```

time: 112 us -> 99.6 us (0.89)
  Pallas kernels: 29.8 us -> 24.9 us
  starting transfers between devices: 30.5 us -> 27.2 us
  other arithmetic: 2.47 us -> 0.19 us
  local copies, waits for them, and re-layouts: 7.48 us -> 5.71 us
    pallas_call x4 -> x15, Pallas kernels: 29.8 us -> 24.9 us  [kernel_call(): pl.pallas_call(body, out_shape=[jax.ShapeDtypeStruct(shape, kind) for sha...]
    ppermute x25, starting transfers between devices: 30.5 us -> 27.2 us  [swapped(): return lax.ppermute(value, axis, [(i, i ^ mask) for i in range(size)])]
    convert_element_type x11 -> x0, other arithmetic: 1.8 us -> none  [the longest x5 1.78 us: plus(): functools.reduce(jnp.add, [v.astype(f32) for v in (value, *others)])]
    unnamed x62 -> x60, local copies, waits for them, and re-layouts: 5.89 us -> 4.83 us
  transfers between devices with their start and end apart: 25 -> 25, of which waited for: 18 -> 18; matrix products, arithmetic and copies ran while one was open for 3% -> 3% of each run, Pallas kernels for 1% -> 2%
where the time goes in v2:
time: 99.6 us; the launch traced here: 99.4 us
  waiting for transfers between devices  40 us (40%)
  starting transfers between devices  27.2 us (27%)
  Pallas kernels  24.9 us (25%)
  local copies, waits for them, and re-layouts  5.71 us (6%)
  between operations  1.36 us (1%)
    ppermute x25, waiting for transfers between devices, swapped(): return lax.ppermute(value, axis, [(i, i ^ mask) for i in range(size)])  40 us
    ppermute x25, starting transfers between devices, swapped(): return lax.ppermute(value, axis, [(i, i ^ mask) for i in range(size)])  27.2 us
    pallas_call x15, Pallas kernels, kernel_call(): pl.pallas_call(body, out_shape=[jax.ShapeDtypeStruct(shape, kind) for sha...  24.9 us
    unnamed x60, local copies, waits for them, and re-layouts  4.83 us
  transfers between devices with their start and end apart: 25, of which 18 were waited for; matrix products, arithmetic and copies ran while one was open for 3% of the time, Pallas kernels for 2%

profile of v2, /device:TPU:0, one launch (start us, length us, event | category | flops | bytes accessed | tf_op | source)
XLA Modules:
  0.0 99.4 jit_solution(16033204805562757811)
XLA Ops:
  5.1 4.0 %collective-permute-start.2 = (f32[3,1296]{1,0:T(4,128)S(1)}, f32[3,1296]{1,0:T(4,128)S(1)}, u32[]{:S(2)}, u32[]{:S(2)}) collective-permute-start(f32[3,1296]{1,0:T(4,128)S(1)} %sums.1), channel_id=1, source_target_pairs={{0,3},{1,2},{2,1},{3,0},{4,7},{5,6},{6,5},{7,4},{8,11},{9,10},{10,... | collective-permute-start | bytes 46664 | tf_op jit(solution)/shard_map/ppermute | solution.py:843
  10.8 2.0 %collective-permute-done.1 = f32[3,1296]{1,0:T(4,128)S(1)} collective-permute-done((f32[3,1296]{1,0:T(4,128)S(1)}, f32[3,1296]{1,0:T(4,128)S(1)}, u32[]{:S(2)}, u32[]{:S(2)}) %collective-permute-start.1) | collective-permute-done | bytes 15584 | tf_op jit(solution)/shard_map/ppermute | solution.py:843
  13.4 3.7 %collective-permute-start.5 = (f32[3,1296]{1,0:T(4,128)S(1)}, f32[3,1296]{1,0:T(4,128)S(1)}, u32[]{:S(2)}, u32[]{:S(2)}) collective-permute-start(f32[3,1296]{1,0:T(4,128)S(1)} %add_add_fusion.1), channel_id=1, source_target_pairs={{0,12},{1,13},{2,14},{3,15},{4,8},{5,9},{6,10},{7,11},{8,4},{9,5},... | collective-permute-start | bytes 46664 | tf_op jit(solution)/shard_map/ppermute | solution.py:843
  19.1 2.7 %collective-permute-done.4 = f32[3,1296]{1,0:T(4,128)S(1)} collective-permute-done((f32[3,1296]{1,0:T(4,128)S(1)}, f32[3,1296]{1,0:T(4,128)S(1)}, u32[]{:S(2)}, u32[]{:S(2)}) %collective-permute-start.4) | collective-permute-done | bytes 15584 | tf_op jit(solution)/shard_map/ppermute | solution.py:843
  22.0 16.9 %middle.1 = (bf16[196,216]{1,0:T(8,128)(2,1)S(1)}, bf16[196,216]{1,0:T(8,128)(2,1)S(1)}, f32[196,216]{1,0:T(8,128)S(1)}, bf16[224,216]{1,0:T(8,128)(2,1)S(1)}, b...) custom-call(s32[2,4]{1,0:T(2,128)S(1)} %copy-done.21, ...), custom_call_target="tpu_custom_call" | custom-call | flops 4294967296 | bytes 8388608 | tf_op jit(solution)/shard_map/middle/pallas_call | solution.py:829
  39.1 2.8 %collective-permute-done.6 = bf16[304,16,128]{2,1,0:T(8,128)(2,1)S(1)} collective-permute-done((bf16[304,16,128]{2,1,0:T(8,128)(2,1)S(1)}, bf16[304,16,128]{2,1,0:T(8,128)(2,1)S(1)}, u32[]{:S(2)}, u32[]{:S(2)}) %collective-permute-start.6) | collective-permute-done | bytes 1245216 | tf_op jit(solution)/shard_map/ppermute | solution.py:843
  42.2 1.6 %collective-permute-start.7 = (bf16[80,16,128]{2,1,0:T(8,128)(2,1)S(1)}, bf16[80,16,128]{2,1,0:T(8,128)(2,1)S(1)}, u32[]{:S(2)}, u32[]{:S(2)}) collective-permute-start(bf16[80,16,128]{2,1,0:T(8,128)(2,1)S(1)} %get-tuple-element.87), channel_id=1, source_target_pairs={{0,2},{1,3},{2,0},{3,1},{4,6},{5,7},{6,4},{7,5},{8,10},{9,11},{10,... | collective-permute-start | bytes 983048 | tf_op jit(solution)/shard_map/ppermute | solution.py:843
  44.7 8.6 %collective-permute-done.9.refs_1_ = bf16[76,16,128]{2,1,0:T(8,128)(2,1)S(1)} collective-permute-done((bf16[76,16,128]{2,1,0:T(8,128)(2,1)S(1)}, bf16[76,16,128]{2,1,0:T(8,128)(2,1)S(1)}, u32[]{:S(2)}, u32[]{:S(2)}) %collective-permute-start.9) | collective-permute-done | bytes 311328 | tf_op jit(solution)/shard_map/ppermute | solution.py:843
  54.7 4.1 %collective-permute-done.10.refs_3_ = bf16[40,16,128]{2,1,0:T(8,128)(2,1)S(1)} collective-permute-done((bf16[40,16,128]{2,1,0:T(8,128)(2,1)S(1)}, bf16[40,16,128]{2,1,0:T(8,128)(2,1)S(1)}, u32[]{:S(2)}, u32[]{:S(2)}) %collective-permute-start.10) | collective-permute-done | bytes 163872 | tf_op jit(solution)/shard_map/ppermute | solution.py:843
  59.5 2.1 %collective-permute-start.11 = (bf16[23,16,128]{2,1,0:T(8,128)(2,1)S(1)}, bf16[23,16,128]{2,1,0:T(8,128)(2,1)S(1)}, u32[]{:S(2)}, u32[]{:S(2)}) collective-permute-start(bf16[23,16,128]{2,1,0:T(8,128)(2,1)S(1)} %get-tuple-element.98), channel_id=1, source_target_pairs={{0,8},{1,9},{2,10},{3,11},{4,12},{5,13},{6,14},{7,15},{8,0},{9,1},... | collective-permute-start | bytes 282632 | tf_op jit(solution)/shard_map/ppermute | solution.py:843
  61.6 2.4 %collective-permute-start.13 = (bf16[23,16,128]{2,1,0:T(8,128)(2,1)S(1)}, bf16[23,16,128]{2,1,0:T(8,128)(2,1)S(1)}, u32[]{:S(2)}, u32[]{:S(2)}) collective-permute-start(bf16[23,16,128]{2,1,0:T(8,128)(2,1)S(1)} %get-tuple-element.100), channel_id=1, source_target_pairs={{0,12},{1,13},{2,14},{3,15},{4,8},{5,9},{6,10},{7,11},{8,4},{9,5},... | collective-permute-start | bytes 282632 | tf_op jit(solution)/shard_map/ppermute | solution.py:843
  64.0 3.1 %collective-permute-done.11.refs_0_ = bf16[23,16,128]{2,1,0:T(8,128)(2,1)S(1)} collective-permute-done((bf16[23,16,128]{2,1,0:T(8,128)(2,1)S(1)}, bf16[23,16,128]{2,1,0:T(8,128)(2,1)S(1)}, u32[]{:S(2)}, u32[]{:S(2)}) %collective-permute-start.11) | collective-permute-done | bytes 94240 | tf_op jit(solution)/shard_map/ppermute | solution.py:843
  67.1 1.4 %collective-permute-done.12.refs_1_ = bf16[23,16,128]{2,1,0:T(8,128)(2,1)S(1)} collective-permute-done((bf16[23,16,128]{2,1,0:T(8,128)(2,1)S(1)}, bf16[23,16,128]{2,1,0:T(8,128)(2,1)S(1)}, u32[]{:S(2)}, u32[]{:S(2)}) %collective-permute-start.12) | collective-permute-done | bytes 94240 | tf_op jit(solution)/shard_map/ppermute | solution.py:843
  68.5 2.1 %collective-permute-start.16 = (bf16[21,16,128]{2,1,0:T(8,128)(2,1)S(1)}, bf16[21,16,128]{2,1,0:T(8,128)(2,1)S(1)}, u32[]{:S(2)}, u32[]{:S(2)}) collective-permute-start(bf16[21,16,128]{2,1,0:T(8,128)(2,1)S(1)} %get-tuple-element.103.refs_0_.refs_1_), channel_id=1, source_target_pairs={{0,12},{1,13},{2,14},{3,15},{4,8},{5,9},{6,10},{7,11},{8,4},{9,5},... | collective-permute-start | bytes 258056 | tf_op jit(solution)/shard_map/ppermute | solution.py:843
  70.7 2.3 %collective-permute-start.14 = (bf16[21,16,128]{2,1,0:T(8,128)(2,1)S(1)}, bf16[21,16,128]{2,1,0:T(8,128)(2,1)S(1)}, u32[]{:S(2)}, u32[]{:S(2)}) collective-permute-start(bf16[21,16,128]{2,1,0:T(8,128)(2,1)S(1)} %get-tuple-element.103.refs_0_.refs_1_), channel_id=1, source_target_pairs={{0,8},{1,9},{2,10},{3,11},{4,12},{5,13},{6,14},{7,15},{8,0},{9,1},... | collective-permute-start | bytes 258056 | tf_op jit(solution)/shard_map/ppermute | solution.py:843
  75.0 1.8 %collective-permute-done.15.refs_2_.refs_3_ = bf16[21,16,128]{2,1,0:T(8,128)(2,1)S(1)} collective-permute-done((bf16[21,16,128]{2,1,0:T(8,128)(2,1)S(1)}, bf16[21,16,128]{2,1,0:T(8,128)(2,1)S(1)}, u32[]{:S(2)}, u32[]{:S(2)}) %collective-permute-start.15) | collective-permute-done | bytes 86048 | tf_op jit(solution)/shard_map/ppermute | solution.py:843
  77.4 1.5 %collective-permute-start.19 = (bf16[44,16,128]{2,1,0:T(8,128)(2,1)S(1)}, bf16[44,16,128]{2,1,0:T(8,128)(2,1)S(1)}, u32[]{:S(2)}, u32[]{:S(2)}) collective-permute-start(bf16[44,16,128]{2,1,0:T(8,128)(2,1)S(1)} %get-tuple-element.111.refs_0_), channel_id=1, source_target_pairs={{0,2},{1,3},{2,0},{3,1},{4,6},{5,7},{6,4},{7,5},{8,10},{9,11},{10,... | collective-permute-start | bytes 540680 | tf_op jit(solution)/shard_map/ppermute | solution.py:843
  79.0 3.2 %collective-permute-done.17.refs_1_.refs_5_ = bf16[40,16,128]{2,1,0:T(8,128)(2,1)S(1)} collective-permute-done((bf16[40,16,128]{2,1,0:T(8,128)(2,1)S(1)}, bf16[40,16,128]{2,1,0:T(8,128)(2,1)S(1)}, u32[]{:S(2)}, u32[]{:S(2)}) %collective-permute-start.17) | collective-permute-done | bytes 163872 | tf_op jit(solution)/shard_map/ppermute | solution.py:843
  82.2 1.6 %collective-permute-start.18 = (bf16[80,16,128]{2,1,0:T(8,128)(2,1)S(1)}, bf16[80,16,128]{2,1,0:T(8,128)(2,1)S(1)}, u32[]{:S(2)}, u32[]{:S(2)}) collective-permute-start(bf16[80,16,128]{2,1,0:T(8,128)(2,1)S(1)} %together.4.refs_0_), channel_id=1, source_target_pairs={{0,2},{1,3},{2,0},{3,1},{4,6},{5,7},{6,4},{7,5},{8,10},{9,11},{10,... | collective-permute-start | bytes 983048 | tf_op jit(solution)/shard_map/ppermute | solution.py:843
  83.8 1.4 %collective-permute-start.20 = (bf16[88,16,128]{2,1,0:T(8,128)(2,1)S(1)}, bf16[88,16,128]{2,1,0:T(8,128)(2,1)S(1)}, u32[]{:S(2)}, u32[]{:S(2)}) collective-permute-start(bf16[88,16,128]{2,1,0:T(8,128)(2,1)S(1)} %together.6.refs_0_), channel_id=1, source_target_pairs={{0,1},{1,0},{2,3},{3,2},{4,5},{5,4},{6,7},{7,6},{8,9},{9,8},{10,11... | collective-permute-start | bytes 1081352 | tf_op jit(solution)/shard_map/ppermute | solution.py:843
  85.4 1.4 %collective-permute-done.22 = f32[196,216]{1,0:T(8,128)S(1)} collective-permute-done((f32[196,216]{1,0:T(8,128)S(1)}, f32[196,216]{1,0:T(8,128)S(1)}, u32[]{:S(2)}, u32[]{:S(2)}) %collective-permute-start.22) | collective-permute-done | bytes 169376 | tf_op jit(solution)/shard_map/ppermute | solution.py:843
  86.8 3.1 %collective-permute-done.18.refs_1_.refs_6_ = bf16[80,16,128]{2,1,0:T(8,128)(2,1)S(1)} collective-permute-done((bf16[80,16,128]{2,1,0:T(8,128)(2,1)S(1)}, bf16[80,16,128]{2,1,0:T(8,128)(2,1)S(1)}, u32[]{:S(2)}, u32[]{:S(2)}) %collective-permute-start.18) | collective-permute-done | bytes 327712 | tf_op jit(solution)/shard_map/ppermute | solution.py:843
  89.9 1.3 %collective-permute-done.20.refs_1_.refs_9_ = bf16[88,16,128]{2,1,0:T(8,128)(2,1)S(1)} collective-permute-done((bf16[88,16,128]{2,1,0:T(8,128)(2,1)S(1)}, bf16[88,16,128]{2,1,0:T(8,128)(2,1)S(1)}, u32[]{:S(2)}, u32[]{:S(2)}) %collective-permute-start.20) | collective-permute-done | bytes 360480 | tf_op jit(solution)/shard_map/ppermute | solution.py:843
  94.5 4.8 %unpack.1 = (f32[216,1296]{1,0:T(8,128)}, f32[1296]{0:T(1024)}, f32[1296]{0:T(1024)}, f32[9,1296]{1,0:T(8,128)}, f32[324,1296]{1,0:T(8,128)}, /*index=5*/f32[324...) custom-call(bf16[216,1296]{1,0:T(8,128)(2,1)S(1)} %copy-done.2, ...), custom_call_target="tpu_custom_call" | custom-call | flops 67108864 | bytes 8388608 | tf_op jit(solution)/shard_map/unpack/pallas_call | solution.py:829
  (118 shorter events, 18.4 us)
Async XLA Ops:
  5.1 5.7 %collective-permute-start.2 = (f32[3,1296]{1,0:T(4,128)S(1)}, f32[3,1296]{1,0:T(4,128)S(1)}, u32[]{:S(2)}, u32[]{:S(2)}) collective-permute-start(f32[3,1296]{1,0:T(4,128)S(1)} %sums.1), channel_id=1, source_target_pairs={{0,3},{1,2},{2,1},{3,0},{4,7},{5,6},{6,5},{7,4},{8,11},{9,10},{10,... | collective-permute-start | bytes 46664 | tf_op jit(solution)/shard_map/ppermute | solution.py:843
  9.1 3.8 %collective-permute-start.1 = (f32[3,1296]{1,0:T(4,128)S(1)}, f32[3,1296]{1,0:T(4,128)S(1)}, u32[]{:S(2)}, u32[]{:S(2)}) collective-permute-start(f32[3,1296]{1,0:T(4,128)S(1)} %sums.1), channel_id=1, source_target_pairs={{0,2},{1,3},{2,0},{3,1},{4,6},{5,7},{6,4},{7,5},{8,10},{9,11},{10,... | collective-permute-start | bytes 46664 | tf_op jit(solution)/shard_map/ppermute | solution.py:843
  9.6 3.8 %collective-permute-start = (f32[3,1296]{1,0:T(4,128)S(1)}, f32[3,1296]{1,0:T(4,128)S(1)}, u32[]{:S(2)}, u32[]{:S(2)}) collective-permute-start(f32[3,1296]{1,0:T(4,128)S(1)} %sums.1), channel_id=1, source_target_pairs={{0,1},{1,0},{2,3},{3,2},{4,5},{5,4},{6,7},{7,6},{8,9},{9,8},{10,11... | collective-permute-start | bytes 46664 | tf_op jit(solution)/shard_map/ppermute | solution.py:843
  13.4 5.7 %collective-permute-start.5 = (f32[3,1296]{1,0:T(4,128)S(1)}, f32[3,1296]{1,0:T(4,128)S(1)}, u32[]{:S(2)}, u32[]{:S(2)}) collective-permute-start(f32[3,1296]{1,0:T(4,128)S(1)} %add_add_fusion.1), channel_id=1, source_target_pairs={{0,12},{1,13},{2,14},{3,15},{4,8},{5,9},{6,10},{7,11},{8,4},{9,5},... | collective-permute-start | bytes 46664 | tf_op jit(solution)/shard_map/ppermute | solution.py:843
  17.1 4.7 %collective-permute-start.4 = (f32[3,1296]{1,0:T(4,128)S(1)}, f32[3,1296]{1,0:T(4,128)S(1)}, u32[]{:S(2)}, u32[]{:S(2)}) collective-permute-start(f32[3,1296]{1,0:T(4,128)S(1)} %add_add_fusion.1), channel_id=1, source_target_pairs={{0,8},{1,9},{2,10},{3,11},{4,12},{5,13},{6,14},{7,15},{8,0},{9,1},... | collective-permute-start | bytes 46664 | tf_op jit(solution)/shard_map/ppermute | solution.py:843
  17.1 4.7 %collective-permute-start.3 = (f32[3,1296]{1,0:T(4,128)S(1)}, f32[3,1296]{1,0:T(4,128)S(1)}, u32[]{:S(2)}, u32[]{:S(2)}) collective-permute-start(f32[3,1296]{1,0:T(4,128)S(1)} %add_add_fusion.1), channel_id=1, source_target_pairs={{0,4},{1,5},{2,6},{3,7},{4,0},{5,1},{6,2},{7,3},{8,12},{9,13},{10,... | collective-permute-start | bytes 46664 | tf_op jit(solution)/shard_map/ppermute | solution.py:843
  38.9 3.0 %collective-permute-start.6 = (bf16[304,16,128]{2,1,0:T(8,128)(2,1)S(1)}, bf16[304,16,128]{2,1,0:T(8,128)(2,1)S(1)}, u32[]{:S(2)}, u32[]{:S(2)}) collective-permute-start(bf16[304,16,128]{2,1,0:T(8,128)(2,1)S(1)} %get-tuple-element.85), channel_id=1, source_target_pairs={{0,16},{16,0},{1,17},{17,1},{2,18},{18,2},{3,19},{19,3},{4,20},{20... | collective-permute-start | bytes 3735560 | tf_op jit(solution)/shard_map/ppermute | solution.py:843
  42.2 11.8 %collective-permute-start.7 = (bf16[80,16,128]{2,1,0:T(8,128)(2,1)S(1)}, bf16[80,16,128]{2,1,0:T(8,128)(2,1)S(1)}, u32[]{:S(2)}, u32[]{:S(2)}) collective-permute-start(bf16[80,16,128]{2,1,0:T(8,128)(2,1)S(1)} %get-tuple-element.87), channel_id=1, source_target_pairs={{0,2},{1,3},{2,0},{3,1},{4,6},{5,7},{6,4},{7,5},{8,10},{9,11},{10,... | collective-permute-start | bytes 983048 | tf_op jit(solution)/shard_map/ppermute | solution.py:843
  44.1 9.2 %collective-permute-start.9 = (bf16[76,16,128]{2,1,0:T(8,128)(2,1)S(1)}, bf16[76,16,128]{2,1,0:T(8,128)(2,1)S(1)}, u32[]{:S(2)}, u32[]{:S(2)}) collective-permute-start(bf16[76,16,128]{2,1,0:T(8,128)(2,1)S(1)} %get-tuple-element.92), channel_id=1, source_target_pairs={{0,1},{1,0},{2,3},{3,2},{4,5},{5,4},{6,7},{7,6},{8,9},{9,8},{10,11... | collective-permute-start | bytes 933896 | tf_op jit(solution)/shard_map/ppermute | solution.py:843
  53.4 5.4 %collective-permute-start.10 = (bf16[40,16,128]{2,1,0:T(8,128)(2,1)S(1)}, bf16[40,16,128]{2,1,0:T(8,128)(2,1)S(1)}, u32[]{:S(2)}, u32[]{:S(2)}) collective-permute-start(bf16[40,16,128]{2,1,0:T(8,128)(2,1)S(1)} %get-tuple-element.95), channel_id=1, source_target_pairs={{0,2},{1,3},{2,0},{3,1},{4,6},{5,7},{6,4},{7,5},{8,10},{9,11},{10,... | collective-permute-start | bytes 491528 | tf_op jit(solution)/shard_map/ppermute | solution.py:843
  54.1 5.4 %collective-permute-start.8 = (bf16[40,16,128]{2,1,0:T(8,128)(2,1)S(1)}, bf16[40,16,128]{2,1,0:T(8,128)(2,1)S(1)}, u32[]{:S(2)}, u32[]{:S(2)}) collective-permute-start(bf16[40,16,128]{2,1,0:T(8,128)(2,1)S(1)} %get-tuple-element.89), channel_id=1, source_target_pairs={{0,1},{1,0},{2,3},{3,2},{4,5},{5,4},{6,7},{7,6},{8,9},{9,8},{10,11... | collective-permute-start | bytes 491528 | tf_op jit(solution)/shard_map/ppermute | solution.py:843
  59.5 7.5 %collective-permute-start.11 = (bf16[23,16,128]{2,1,0:T(8,128)(2,1)S(1)}, bf16[23,16,128]{2,1,0:T(8,128)(2,1)S(1)}, u32[]{:S(2)}, u32[]{:S(2)}) collective-permute-start(bf16[23,16,128]{2,1,0:T(8,128)(2,1)S(1)} %get-tuple-element.98), channel_id=1, source_target_pairs={{0,8},{1,9},{2,10},{3,11},{4,12},{5,13},{6,14},{7,15},{8,0},{9,1},... | collective-permute-start | bytes 282632 | tf_op jit(solution)/shard_map/ppermute | solution.py:843
  61.6 6.9 %collective-permute-start.12 = (bf16[23,16,128]{2,1,0:T(8,128)(2,1)S(1)}, bf16[23,16,128]{2,1,0:T(8,128)(2,1)S(1)}, u32[]{:S(2)}, u32[]{:S(2)}) collective-permute-start(bf16[23,16,128]{2,1,0:T(8,128)(2,1)S(1)} %get-tuple-element.99), channel_id=1, source_target_pairs={{0,4},{1,5},{2,6},{3,7},{4,0},{5,1},{6,2},{7,3},{8,12},{9,13},{10,... | collective-permute-start | bytes 282632 | tf_op jit(solution)/shard_map/ppermute | solution.py:843
  61.6 6.9 %collective-permute-start.13 = (bf16[23,16,128]{2,1,0:T(8,128)(2,1)S(1)}, bf16[23,16,128]{2,1,0:T(8,128)(2,1)S(1)}, u32[]{:S(2)}, u32[]{:S(2)}) collective-permute-start(bf16[23,16,128]{2,1,0:T(8,128)(2,1)S(1)} %get-tuple-element.100), channel_id=1, source_target_pairs={{0,12},{1,13},{2,14},{3,15},{4,8},{5,9},{6,10},{7,11},{8,4},{9,5},... | collective-permute-start | bytes 282632 | tf_op jit(solution)/shard_map/ppermute | solution.py:843
  68.5 6.4 %collective-permute-start.16 = (bf16[21,16,128]{2,1,0:T(8,128)(2,1)S(1)}, bf16[21,16,128]{2,1,0:T(8,128)(2,1)S(1)}, u32[]{:S(2)}, u32[]{:S(2)}) collective-permute-start(bf16[21,16,128]{2,1,0:T(8,128)(2,1)S(1)} %get-tuple-element.103.refs_0_.refs_1_), channel_id=1, source_target_pairs={{0,12},{1,13},{2,14},{3,15},{4,8},{5,9},{6,10},{7,11},{8,4},{9,5},... | collective-permute-start | bytes 258056 | tf_op jit(solution)/shard_map/ppermute | solution.py:843
  70.6 6.1 %collective-permute-start.15 = (bf16[21,16,128]{2,1,0:T(8,128)(2,1)S(1)}, bf16[21,16,128]{2,1,0:T(8,128)(2,1)S(1)}, u32[]{:S(2)}, u32[]{:S(2)}) collective-permute-start(bf16[21,16,128]{2,1,0:T(8,128)(2,1)S(1)} %get-tuple-element.103.refs_0_.refs_1_), channel_id=1, source_target_pairs={{0,4},{1,5},{2,6},{3,7},{4,0},{5,1},{6,2},{7,3},{8,12},{9,13},{10,... | collective-permute-start | bytes 258056 | tf_op jit(solution)/shard_map/ppermute | solution.py:843
  70.7 6.0 %collective-permute-start.14 = (bf16[21,16,128]{2,1,0:T(8,128)(2,1)S(1)}, bf16[21,16,128]{2,1,0:T(8,128)(2,1)S(1)}, u32[]{:S(2)}, u32[]{:S(2)}) collective-permute-start(bf16[21,16,128]{2,1,0:T(8,128)(2,1)S(1)} %get-tuple-element.103.refs_0_.refs_1_), channel_id=1, source_target_pairs={{0,8},{1,9},{2,10},{3,11},{4,12},{5,13},{6,14},{7,15},{8,0},{9,1},... | collective-permute-start | bytes 258056 | tf_op jit(solution)/shard_map/ppermute | solution.py:843
  76.8 5.4 %collective-permute-start.17 = (bf16[40,16,128]{2,1,0:T(8,128)(2,1)S(1)}, bf16[40,16,128]{2,1,0:T(8,128)(2,1)S(1)}, u32[]{:S(2)}, u32[]{:S(2)}) collective-permute-start(bf16[40,16,128]{2,1,0:T(8,128)(2,1)S(1)} %get-tuple-element.110.refs_0_), channel_id=1, source_target_pairs={{0,1},{1,0},{2,3},{3,2},{4,5},{5,4},{6,7},{7,6},{8,9},{9,8},{10,11... | collective-permute-start | bytes 491528 | tf_op jit(solution)/shard_map/ppermute | solution.py:843
  77.4 6.4 %collective-permute-start.19 = (bf16[44,16,128]{2,1,0:T(8,128)(2,1)S(1)}, bf16[44,16,128]{2,1,0:T(8,128)(2,1)S(1)}, u32[]{:S(2)}, u32[]{:S(2)}) collective-permute-start(bf16[44,16,128]{2,1,0:T(8,128)(2,1)S(1)} %get-tuple-element.111.refs_0_), channel_id=1, source_target_pairs={{0,2},{1,3},{2,0},{3,1},{4,6},{5,7},{6,4},{7,5},{8,10},{9,11},{10,... | collective-permute-start | bytes 540680 | tf_op jit(solution)/shard_map/ppermute | solution.py:843
  78.9 6.4 %collective-permute-start.21 = (bf16[196,216]{1,0:T(8,128)(2,1)S(1)}, bf16[196,216]{1,0:T(8,128)(2,1)S(1)}, u32[]{:S(2)}, u32[]{:S(2)}) collective-permute-start(bf16[196,216]{1,0:T(8,128)(2,1)S(1)} %broadcast_select_fusion.1), channel_id=1, source_target_pairs={{0,16},{16,0},{1,17},{17,1},{2,18},{18,2},{3,19},{19,3},{4,20},{20... | collective-permute-start | bytes 254024 | tf_op jit(solution)/shard_map/ppermute | solution.py:843
  82.2 7.7 %collective-permute-start.18 = (bf16[80,16,128]{2,1,0:T(8,128)(2,1)S(1)}, bf16[80,16,128]{2,1,0:T(8,128)(2,1)S(1)}, u32[]{:S(2)}, u32[]{:S(2)}) collective-permute-start(bf16[80,16,128]{2,1,0:T(8,128)(2,1)S(1)} %together.4.refs_0_), channel_id=1, source_target_pairs={{0,2},{1,3},{2,0},{3,1},{4,6},{5,7},{6,4},{7,5},{8,10},{9,11},{10,... | collective-permute-start | bytes 983048 | tf_op jit(solution)/shard_map/ppermute | solution.py:843
  83.8 7.5 %collective-permute-start.20 = (bf16[88,16,128]{2,1,0:T(8,128)(2,1)S(1)}, bf16[88,16,128]{2,1,0:T(8,128)(2,1)S(1)}, u32[]{:S(2)}, u32[]{:S(2)}) collective-permute-start(bf16[88,16,128]{2,1,0:T(8,128)(2,1)S(1)} %together.6.refs_0_), channel_id=1, source_target_pairs={{0,1},{1,0},{2,3},{3,2},{4,5},{5,4},{6,7},{7,6},{8,9},{9,8},{10,11... | collective-permute-start | bytes 1081352 | tf_op jit(solution)/shard_map/ppermute | solution.py:843
  91.3 3.2 %collective-permute-start.24 = (bf16[176,16,128]{2,1,0:T(8,128)(2,1)S(1)}, bf16[176,16,128]{2,1,0:T(8,128)(2,1)S(1)}, u32[]{:S(2)}, u32[]{:S(2)}) collective-permute-start(bf16[176,16,128]{2,1,0:T(8,128)(2,1)S(1)} %together.7), channel_id=1, source_target_pairs={{0,16},{16,0},{1,17},{17,1},{2,18},{18,2},{3,19},{19,3},{4,20},{20... | collective-permute-start | bytes 2162696 | tf_op jit(solution)/shard_map/ppermute | solution.py:843
  91.4 3.1 %collective-permute-start.23 = (bf16[160,16,128]{2,1,0:T(8,128)(2,1)S(1)}, bf16[160,16,128]{2,1,0:T(8,128)(2,1)S(1)}, u32[]{:S(2)}, u32[]{:S(2)}) collective-permute-start(bf16[160,16,128]{2,1,0:T(8,128)(2,1)S(1)} %together.5), channel_id=1, source_target_pairs={{0,16},{16,0},{1,17},{17,1},{2,18},{18,2},{3,19},{19,3},{4,20},{20... | collective-permute-start | bytes 1966088 | tf_op jit(solution)/shard_map/ppermute | solution.py:843
  (29 other events, 435.5 us)

commit v3 on v2

--- a/solution.py
+++ b/solution.py
@@ -5,6 +5,7 @@
 import jax.numpy as jnp
 from jax import lax
 from jax.experimental import pallas as pl
+from jax.experimental.layout import Layout, with_layout_constraint
 from jax.experimental.pallas import tpu as pltpu
 from jax.sharding import PartitionSpec as P
 
@@ -48,7 +49,7 @@
 PARTS = 2
 RIDDEN = 1
 FACTOR_ROWS = 32
-WEIGHTS = 18
+WEIGHTS = 17
 UNPACKED = 26
 
 f32 = jnp.float32
@@ -124,19 +125,22 @@
 
 
 def depthwise_kernel_grad(three, v):
-    v3 = grid(v)
-    taps = []
+    v3 = grid(v.astype(bf16))
+    sides = [grid(side.astype(bf16)) for side in three]
+    row = jnp.zeros((1, WIDE, LANES), bf16)
+    products = []
     for a in (-1, 0, 1):
         for b in (-1, 0, 1):
-            g3 = grid(three[1 - b])
+            g3 = sides[1 - b]
             if a < 0:
-                product = v3[:-1] * g3[1:]
+                product = jnp.concatenate([v3[:-1] * g3[1:], row], axis=0)
             elif a > 0:
-                product = v3[1:] * g3[:-1]
+                product = jnp.concatenate([v3[1:] * g3[:-1], row], axis=0)
             else:
                 product = v3 * g3
-            taps.append(jnp.sum(jnp.sum(product, axis=0), axis=0, keepdims=True))
-    return taps
+            products.append(flat(product))
+    sums = dot(jnp.ones((16, ROWS), bf16), jnp.concatenate(products, axis=1))
+    return [sums[0:1, t * LANES : (t + 1) * LANES] for t in range(9)]
 
 
 def norm_forward(v):
@@ -209,16 +213,22 @@
     return copies
 
 
-def sums_kernel(codes, image, expand_hbm, sums_out, expand, sems):
-    (expand_copy,) = fetch([expand_hbm], [expand], sems)
-    side = code_of(codes)[0]
-    tokens = widen(image[...], side).astype(bf16)
+def sums_kernel(image, expand_hbm, codes_hbm, sums_out, tokens_out, expanded_out, expand, codes, sems):
+    expand_copy, codes_copy = fetch([expand_hbm, codes_hbm], [expand, codes], sems)
+    tokens = widen(image[...], SIDE).astype(bf16)
     expand_copy.wait()
     expanded = dot(tokens, expand[...])
+    codes_copy.wait()
+    live = grid_mask((ROWS, 1), code_of(codes)[0])
+    tokens = tokens.astype(f32) * live
+    expanded = expanded * live
+    tokens_out[...] = tokens.astype(bf16)
+    expanded_out[:, E - E % LANES :] = jnp.zeros((ROWS, EP - E + E % LANES), f32)
+    expanded_out[:, :E] = expanded
     sums_out[0:1, :] = row_sum(expanded)
     sums_out[1:2, :] = row_sum(expanded * expanded)
     sums_out[2:3, :] = jnp.zeros((1, E), f32)
-    sums_out[2:3, :D] = row_sum(tokens.astype(f32))
+    sums_out[2:3, :D] = row_sum(tokens)
 
 
 def middle_kernel(
@@ -227,7 +237,8 @@
     per_piece,
     orders,
     codes,
-    image,
+    tokens_in,
+    expanded_s,
     cotangent,
     sums,
     gain,
@@ -242,11 +253,12 @@
         second_out,
         handed_grad_out,
         handed_low_out,
-        tokens_out,
         expanded_grad_out,
         batch_out,
-        kept_out,
-        sent_out,
+        kept_low,
+        kept_high,
+        sent_low,
+        sent_high,
         factors_out,
         tiles_out,
         wide_e,
@@ -255,7 +267,6 @@
         half_live,
         beside,
         half_scale,
-        expanded_s,
         deep_grad,
         active_e,
         slope_e,
@@ -283,7 +294,6 @@
         projected_s,
     ) = refs[WEIGHTS:]
     (
-        expand,
         depth_one,
         squeeze_t,
         excite,
@@ -318,12 +328,9 @@
     wide_e[3:4, :E] = channel_mask
     wide_e[4:13, :E] = depth_one[...] * channel_mask
     wide_e[15:16, :E] = inverse
-    tokens = widen(image[...], side).astype(bf16)
-    tokens_out[...] = tokens
+    tokens = tokens_in[...]
     token_mean = sums[2:3, :D] / count
     centred_tokens = (tokens.astype(f32) - token_mean) * live_d
-    expanded_s[:, E - E % LANES :] = jnp.zeros((ROWS, EP - E + E % LANES), f32)
-    expanded_s[:, :E] = dot(tokens, expand[...])
 
     beside[...] = jnp.zeros_like(beside)
     half_scale[0:1, :] = 0.5 * wide_e[1:2, :]
@@ -580,8 +587,8 @@
         centred = expanded_s[:, at] - wide_e[0:1, at]
         grad_gain = row_sum(grad_normed * centred) * wide_e[15:16, at]
         grad_bias = row_sum(grad_normed)
-        batch_out[pl.ds(c, 1), :] = grad_gain
-        batch_out[pl.ds(c + 16, 1), :] = grad_bias
+        batch_out[c : c + 1, :] = grad_gain
+        batch_out[EB + c : EB + c + 1, :] = grad_bias
         tail_e[0:1, at] = grad_gain
         tail_e[1:2, at] = grad_bias
         tail_e[2:3, at] = taps[8] * wide_e[3:4, at]
@@ -606,39 +613,56 @@
         tiles_out[ALL_TILES:] = jnp.zeros((spare, 16, LANES), bf16)
 
     half = pieces // 2
+    fourth = half // 2
     mine = lax.axis_index("pipe")
     base = 0
     for part, order in enumerate(orders):
         size = per_piece[part]
         me = home_of(order) & (half - 1)
-        for piece in range(half):
-            first = base * 2 + piece * size
-            to = pl.ds(base + (piece ^ me) * size, size)
-            kept_out[to] = tiles_out[pl.ds(first + mine * half * size, size)]
-            sent_out[to] = tiles_out[pl.ds(first + (1 - mine) * half * size, size)]
+        for place in range(half):
+            first = 2 * base + (place ^ me) * size
+            start = base // 2 + (place % fourth) * size
+            to = slice(start, start + size)
+            kept = kept_low if place < fourth else kept_high
+            sent = sent_low if place < fourth else sent_high
+            kept[to] = tiles_out[pl.ds(first + mine * half * size, size)]
+            sent[to] = tiles_out[pl.ds(first + (1 - mine) * half * size, size)]
         base += half * size
 
 
-RIDE_TILES = 4
+RIDE_ROWS = 24
+RIDE_TILES = 2 * RIDE_ROWS // 16
 
 
 def ridden_sum(batch, arrivals):
-    total = batch[...].reshape(2, 16, LANES)
+    total = batch[...]
     for ref in arrivals:
         end = ref.shape[0]
-        total = total + (ref[end - 4 : end - 2].astype(f32) + ref[end - 2 : end].astype(f32))
+        both = ref[end - RIDE_TILES : end].reshape(2 * RIDE_ROWS, LANES).astype(f32)
+        total = total + (both[:RIDE_ROWS] + both[RIDE_ROWS:])
     return total
 
 
 def put_ride(ref, total):
-    high = total.astype(bf16)
+    high = total.astype(bf16).astype(f32)
+    both = jnp.concatenate([high, total - high], axis=0)
     end = ref.shape[0]
-    ref[end - 4 : end - 2] = high
-    ref[end - 2 : end] = (total - high.astype(f32)).astype(bf16)
+    ref[end - RIDE_TILES : end] = both.astype(bf16).reshape(RIDE_TILES, 16, LANES)
 
 
 def added(terms, at):
     return functools.reduce(jnp.add, [term[at].astype(f32) for term in terms]).astype(bf16)
+
+
+def slices_kernel(lengths, rides, *refs):
+    own, other, *refs = refs
+    if rides:
+        batch, *refs = refs
+        put_ride(refs[RIDDEN], batch[...])
+    start = 0
+    for length, out in zip(lengths, refs):
+        out[0:length] = added([own, other], slice(start, start + length))
+        start += length
 
 
 def halves_kernel(count, size, rides, *refs):
@@ -706,7 +730,7 @@
     scale = inverse * gain[...]
     for b in range(EB):
         wide[0:1, b * LANES : (b + 1) * LANES] = total[b : b + 1, :]
-        wide[1:2, b * LANES : (b + 1) * LANES] = total[16 + b : 17 + b, :]
+        wide[1:2, b * LANES : (b + 1) * LANES] = total[EB + b : EB + b + 1, :]
     grad_variance = -0.5 * inverse * scale * wide[0:1, :E]
     grad_second = grad_variance / count
     grad_first = (-scale * wide[1:2, :E] - 2.0 * average * grad_variance) / count
@@ -824,7 +848,8 @@
 def kernel_call(body, name, shapes, scratch, operands, fetched, limit, flops):
     in_specs = [pl.BlockSpec(memory_space=pltpu.VMEM)] * len(operands)
     if fetched is not None:
-        in_specs[0] = pl.BlockSpec(memory_space=pltpu.SMEM)
+        if operands[0].dtype == jnp.int32:
+            in_specs[0] = pl.BlockSpec(memory_space=pltpu.SMEM)
         in_specs += [pl.BlockSpec(memory_space=pltpu.HBM)] * len(fetched)
     return pl.pallas_call(
         body,
@@ -907,13 +932,13 @@
     return_t = return_weight.T
     gain = row(batch_gain)
 
-    (sums,) = kernel_call(
+    sums, tokens, expanded = kernel_call(
         sums_kernel,
         "sums",
-        [((3, E), f32)],
-        buffers([expand_weight]) + [pltpu.SemaphoreType.DMA((1,))],
-        (codes, image),
-        (expand_weight,),
+        [((3, E), f32), ((ROWS, D), bf16), ((ROWS, EP), f32)],
+        buffers([expand_weight]) + [pltpu.SMEM(codes.shape, codes.dtype), pltpu.SemaphoreType.DMA((2,))],
+        (image,),
+        (expand_weight, codes),
         16,
         1 << 33,
     )
@@ -921,7 +946,8 @@
 
     operands = (
         codes,
-        image,
+        tokens,
+        expanded,
         upstream,
         sums,
         gain,
@@ -929,7 +955,6 @@
         row(squeeze_bias),
         row(excite_bias),
         row(hidden_bias),
-        expand_weight,
         depth_one,
         squeeze_t,
         excite_weight,
@@ -953,11 +978,9 @@
         ((PIX, D), bf16),
         ((PIX, D), f32),
         ((ROWS, D), bf16),
-        ((ROWS, D), bf16),
         ((ROWS, EP), bf16),
-        ((32, LANES), f32),
-        ((sum(per_piece) * half, 16, LANES), bf16),
-        ((sum(per_piece) * half, 16, LANES), bf16),
+        ((RIDE_ROWS, LANES), f32),
+        *[((sum(per_piece) * half // 2, 16, LANES), bf16)] * 4,
         ((FACTOR_ROWS, LANES), f32),
     ]
     scratch = [
@@ -968,7 +991,6 @@
         pltpu.VMEM((ROWS, LANES), f32),
         pltpu.VMEM((3, ROWS + 16, LANES), f32),
         pltpu.VMEM((8, EP), f32),
-        pltpu.VMEM((ROWS, EP), f32),
         pltpu.VMEM((ROWS, EP), f32),
         pltpu.VMEM((ROWS, EP), f32),
         pltpu.VMEM((ROWS, EP), f32),
@@ -995,7 +1017,7 @@
         pltpu.VMEM((32, DP), f32),
         pltpu.VMEM((ROWS, 3 * D), f32),
     ]
-    first, second, handed_grad, handed_low, tokens, expanded_grad, batch, kept, sent, factors = kernel_call(
+    first, second, handed_grad, handed_low, expanded_grad, batch, *packed, factors = kernel_call(
         functools.partial(middle_kernel, images_total, pieces, per_piece, orders),
         "middle",
         shapes,
@@ -1015,24 +1037,39 @@
     def small_kernel(body, name, shapes, operands):
         return kernel_call(body, name, shapes, [], operands, None, 2, 1 << 20)
 
-    arrived = swapped(sent, "pipe", 1)
-    cuts = [0, half * per_piece[0], half * sum(per_piece)]
-    terms = [[value[cuts[part] : cuts[part + 1]] for value in (kept, arrived)] for part in range(PARTS)]
+    kept_low, kept_high, sent_low, sent_high = packed
+    arrived_high = swapped(sent_high, "pipe", 1)
+    arrived_low = swapped(sent_low, "pipe", 1)
+    count = half // 2
+    lengths = [count * size for size in per_piece]
+    riding = [length + RIDE_TILES * (part == RIDDEN) for part, length in enumerate(lengths)]
+    going = small_kernel(
+        functools.partial(slices_kernel, lengths, True),
+        "firsts",
+        [tiles_of(length) for length in riding],
+        (kept_high, arrived_high, batch),
+    )
+    arrived = [swapped(value, "dp", 1 << order[0]) for value, order in zip(going, orders)]
+    mine = small_kernel(
+        functools.partial(slices_kernel, lengths, False),
+        "keeps",
+        [tiles_of(length) for length in lengths],
+        (kept_low, arrived_low),
+    )
+    terms = [list(pair) for pair in zip(mine, arrived)]
     held = [None] * PARTS
-    count = half
-    for step in range(2):
-        count //= 2
-        for part, order in enumerate(orders):
-            size = per_piece[part]
-            rides = part == RIDDEN
-            body = functools.partial(halves_kernel, count, size, rides)
-            shapes = [tiles_of(count * size), tiles_of(count * size + RIDE_TILES * rides)]
-            if rides:
-                mine, going, batch = small_kernel(body, "halves", shapes + [((32, LANES), f32)], (*terms[part], batch))
-            else:
-                mine, going = small_kernel(body, "halves", shapes, terms[part])
-            held[part] = (mine, swapped(going, "dp", 1 << order[step]))
-        terms = [list(pair) for pair in held]
+    count //= 2
+    for part, order in enumerate(orders):
+        size = per_piece[part]
+        rides = part == RIDDEN
+        body = functools.partial(halves_kernel, count, size, rides)
+        shapes = [tiles_of(count * size), tiles_of(count * size + RIDE_TILES * rides)]
+        if rides:
+            mine, going, batch = small_kernel(body, "halves", shapes + [((RIDE_ROWS, LANES), f32)], (*terms[part], batch))
+        else:
+            mine, going = small_kernel(body, "halves", shapes, terms[part])
+        held[part] = (mine, swapped(going, "dp", 1 << order[1]))
+    terms = [list(pair) for pair in held]
     sizes = per_piece
     for group in groups:
         masks = masks_of(group)
@@ -1040,12 +1077,12 @@
         body = functools.partial(pieces_kernel, len(masks), count, sizes, [len(part) for part in terms])
         shapes = [tiles_of(count * sum(sizes) + (RIDE_TILES if j else 0)) for j in range(len(masks))]
         *going, batch = small_kernel(
-            body, "pieces", shapes + [((32, LANES), f32)], (*[term for part in terms for term in part], batch)
+            body, "pieces", shapes + [((RIDE_ROWS, LANES), f32)], (*[term for part in terms for term in part], batch)
         )
         sizes = [sum(sizes)]
         terms = [[going[0]] + [swapped(value, "dp", mask) for value, mask in zip(going[1:], masks[1:])]]
     held, batch = small_kernel(
-        finish_kernel, "finish", [tiles_of(sum(sizes) + factor_tiles), ((32, LANES), f32)], (*terms[0], batch, factors)
+        finish_kernel, "finish", [tiles_of(sum(sizes) + factor_tiles), ((RIDE_ROWS, LANES), f32)], (*terms[0], batch, factors)
     )
     (images_grad,) = kernel_call(
         functools.partial(last_kernel, images_total),
@@ -1081,23 +1118,29 @@
         other = swapped(jnp.where(leading, two, one), "pipe", 1)
         return jnp.where(leading, jnp.stack([one, other]), jnp.stack([other, two]))[None, :, None]
 
-    activations = both_layers(first, second)
-    input_grads = both_layers(images_grad, handed_grad)
+    activations = with_layout_constraint(both_layers(first, second), Layout(major_to_minor=(0, 2, 3, 1, 4)))
+    input_grads = with_layout_constraint(
+        both_layers(images_grad, handed_grad), Layout(major_to_minor=(0, 1, 3, 2, 4))
+    )
     collected = [[], []]
+    across = [[], []]
     for step in (1, 0):
         arrived = [swapped(value, "dp", 1 << order[step]) for value, order in zip(held[::-1], orders[::-1])][::-1]
-        count *= 2
         for part, size in enumerate(sizes):
             collected[part].append(arrived[part])
-            (held[part],) = small_kernel(
-                functools.partial(side_by_side_kernel, [size]),
-                "together",
-                [tiles_of(count * size)],
-                (held[part], arrived[part]),
-            )
-    held, activations, input_grads = lax.optimization_barrier((held, activations, input_grads))
-    for part in range(PARTS):
-        collected[part].append(swapped(held[part], "pipe", 1))
+            if step:
+                (held[part],) = small_kernel(
+                    functools.partial(side_by_side_kernel, [size]),
+                    "together",
+                    [tiles_of(2 * count * size)],
+                    (held[part], arrived[part]),
+                )
+        if step:
+            across = [[swapped(value, "pipe", 1)] for value in held]
+        else:
+            arrived, activations, input_grads = lax.optimization_barrier((arrived, activations, input_grads))
+            across = [early + [swapped(value, "pipe", 1)] for early, value in zip(across, arrived)]
+    collected = [own + other for own, other in zip(collected, across)]
     grads = kernel_call(
         functools.partial(unpack_kernel, pieces, per_piece, orders, len(merged)),
         "unpack",

time: 99.6 us -> 96.2 us (0.966)
  waiting for transfers between devices: 40 us -> 36.2 us
  starting transfers between devices: 27.2 us -> 28.8 us
  Pallas kernels: 24.9 us -> 23.6 us
  other arithmetic: 0.19 us -> 1.44 us
  local copies, waits for them, and re-layouts: 5.71 us -> 4.54 us
    ppermute x25 -> x28, waiting for transfers between devices: 40 us -> 36.2 us  [swapped(): return lax.ppermute(value, axis, [(i, i ^ mask) for i in range(size)])]
    unnamed x60 -> x58, local copies, waits for them, and re-layouts: 4.83 us -> 2.84 us
    ppermute x25 -> x28, starting transfers between devices: 27.2 us -> 28.8 us  [swapped(): return lax.ppermute(value, axis, [(i, i ^ mask) for i in range(size)])]
    pallas_call x15 -> x13, Pallas kernels: 24.9 us -> 23.6 us  [kernel_call(): pl.pallas_call(body, out_shape=[jax.ShapeDtypeStruct(shape, kind) for sha...]
    select_n x2, other arithmetic: 0.12 us -> 1.36 us  [both_layers(): jnp.where(leading, jnp.stack([one, other]), jnp.stack([other, two]))]
  transfers between devices with their start and end apart: 25 -> 28, of which waited for: 18 -> 20; matrix products, arithmetic and copies ran while one was open for 3% -> 3% of each run, Pallas kernels for 2% -> 2%
where the time goes in v3:
time: 96.2 us; the launch traced here: 95.9 us
  waiting for transfers between devices  36.2 us (38%)
  starting transfers between devices  28.8 us (30%)
  Pallas kernels  23.6 us (25%)
  local copies, waits for them, and re-layouts  4.54 us (5%)
  other arithmetic  1.44 us (1%)
  between operations  1.32 us (1%)
    ppermute x28, waiting for transfers between devices, swapped(): return lax.ppermute(value, axis, [(i, i ^ mask) for i in range(size)])  36.2 us
    ppermute x28, starting transfers between devices, swapped(): return lax.ppermute(value, axis, [(i, i ^ mask) for i in range(size)])  28.8 us
    pallas_call x13, Pallas kernels, kernel_call(): pl.pallas_call(body, out_shape=[jax.ShapeDtypeStruct(shape, kind) for sha...  23.6 us
    unnamed x58, local copies, waits for them, and re-layouts  2.84 us
  transfers between devices with their start and end apart: 28, of which 20 were waited for; matrix products, arithmetic and copies ran while one was open for 3% of the time, Pallas kernels for 2%

profile of v3, /device:TPU:0, one launch (start us, length us, event | category | flops | bytes accessed | tf_op | source)
XLA Modules:
  0.0 95.9 jit_solution(6686817915715578924)
XLA Ops:
  4.8 4.0 %collective-permute-start.2 = (f32[3,1296]{1,0:T(4,128)S(1)}, f32[3,1296]{1,0:T(4,128)S(1)}, u32[]{:S(2)}, u32[]{:S(2)}) collective-permute-start(f32[3,1296]{1,0:T(4,128)S(1)} %get-tuple-element.89), channel_id=1, source_target_pairs={{0,3},{1,2},{2,1},{3,0},{4,7},{5,6},{6,5},{7,4},{8,11},{9,10},{10,... | collective-permute-start | bytes 46664 | tf_op jit(solution)/shard_map/ppermute | solution.py:868
  10.6 2.0 %collective-permute-done.1 = f32[3,1296]{1,0:T(4,128)S(1)} collective-permute-done((f32[3,1296]{1,0:T(4,128)S(1)}, f32[3,1296]{1,0:T(4,128)S(1)}, u32[]{:S(2)}, u32[]{:S(2)}) %collective-permute-start.1) | collective-permute-done | bytes 15584 | tf_op jit(solution)/shard_map/ppermute | solution.py:868
  13.1 3.7 %collective-permute-start.5 = (f32[3,1296]{1,0:T(4,128)S(1)}, f32[3,1296]{1,0:T(4,128)S(1)}, u32[]{:S(2)}, u32[]{:S(2)}) collective-permute-start(f32[3,1296]{1,0:T(4,128)S(1)} %add_add_fusion.1), channel_id=1, source_target_pairs={{0,12},{1,13},{2,14},{3,15},{4,8},{5,9},{6,10},{7,11},{8,4},{9,5},... | collective-permute-start | bytes 46664 | tf_op jit(solution)/shard_map/ppermute | solution.py:868
  18.8 2.7 %collective-permute-done.4 = f32[3,1296]{1,0:T(4,128)S(1)} collective-permute-done((f32[3,1296]{1,0:T(4,128)S(1)}, f32[3,1296]{1,0:T(4,128)S(1)}, u32[]{:S(2)}, u32[]{:S(2)}) %collective-permute-start.4) | collective-permute-done | bytes 15584 | tf_op jit(solution)/shard_map/ppermute | solution.py:868
  21.7 16.0 %middle.1 = (bf16[196,216]{1,0:T(8,128)(2,1)S(1)}, bf16[196,216]{1,0:T(8,128)(2,1)S(1)}, f32[196,216]{1,0:T(8,128)S(1)}, bf16[224,216]{1,0:T(8,128)(2,1)S(1)}, b...) custom-call(s32[2,4]{1,0:T(2,128)S(1)} %copy-done.21, ...), custom_call_target="tpu_custom_call" | custom-call | flops 4294967296 | bytes 8388608 | tf_op jit(solution)/shard_map/middle/pallas_call | solution.py:854
  38.3 1.5 %collective-permute-done.7.refs_1_ = bf16[152,16,128]{2,1,0:T(8,128)(2,1)S(1)} collective-permute-done((bf16[152,16,128]{2,1,0:T(8,128)(2,1)S(1)}, bf16[152,16,128]{2,1,0:T(8,128)(2,1)S(1)}, u32[]{:S(2)}, u32[]{:S(2)}) %collective-permute-start.7) | collective-permute-done | bytes 622624 | tf_op jit(solution)/shard_map/ppermute | solution.py:868
  40.0 1.6 %collective-permute-start.8 = (bf16[80,16,128]{2,1,0:T(8,128)(2,1)S(1)}, bf16[80,16,128]{2,1,0:T(8,128)(2,1)S(1)}, u32[]{:S(2)}, u32[]{:S(2)}) collective-permute-start(bf16[80,16,128]{2,1,0:T(8,128)(2,1)S(1)} %get-tuple-element.96), channel_id=1, source_target_pairs={{0,2},{1,3},{2,0},{3,1},{4,6},{5,7},{6,4},{7,5},{8,10},{9,11},{10,... | collective-permute-start | bytes 983048 | tf_op jit(solution)/shard_map/ppermute | solution.py:868
  42.3 7.5 %collective-permute-done.8.refs_1_ = bf16[80,16,128]{2,1,0:T(8,128)(2,1)S(1)} collective-permute-done((bf16[80,16,128]{2,1,0:T(8,128)(2,1)S(1)}, bf16[80,16,128]{2,1,0:T(8,128)(2,1)S(1)}, u32[]{:S(2)}, u32[]{:S(2)}) %collective-permute-start.8) | collective-permute-done | bytes 327712 | tf_op jit(solution)/shard_map/ppermute | solution.py:868
  50.7 1.5 %collective-permute-start.11 = (bf16[39,16,128]{2,1,0:T(8,128)(2,1)S(1)}, bf16[39,16,128]{2,1,0:T(8,128)(2,1)S(1)}, u32[]{:S(2)}, u32[]{:S(2)}) collective-permute-start(bf16[39,16,128]{2,1,0:T(8,128)(2,1)S(1)} %get-tuple-element.102), channel_id=1, source_target_pairs={{0,2},{1,3},{2,0},{3,1},{4,6},{5,7},{6,4},{7,5},{8,10},{9,11},{10,... | collective-permute-start | bytes 479240 | tf_op jit(solution)/shard_map/ppermute | solution.py:868
  52.2 3.9 %collective-permute-done.11.refs_3_ = bf16[39,16,128]{2,1,0:T(8,128)(2,1)S(1)} collective-permute-done((bf16[39,16,128]{2,1,0:T(8,128)(2,1)S(1)}, bf16[39,16,128]{2,1,0:T(8,128)(2,1)S(1)}, u32[]{:S(2)}, u32[]{:S(2)}) %collective-permute-start.11) | collective-permute-done | bytes 159776 | tf_op jit(solution)/shard_map/ppermute | solution.py:868
  56.1 2.1 %collective-permute-start.12 = (bf16[22,16,128]{2,1,0:T(8,128)(2,1)S(1)}, bf16[22,16,128]{2,1,0:T(8,128)(2,1)S(1)}, u32[]{:S(2)}, u32[]{:S(2)}) collective-permute-start(bf16[22,16,128]{2,1,0:T(8,128)(2,1)S(1)} %get-tuple-element.105), channel_id=1, source_target_pairs={{0,8},{1,9},{2,10},{3,11},{4,12},{5,13},{6,14},{7,15},{8,0},{9,1},... | collective-permute-start | bytes 270344 | tf_op jit(solution)/shard_map/ppermute | solution.py:868
  58.2 2.4 %collective-permute-start.14 = (bf16[22,16,128]{2,1,0:T(8,128)(2,1)S(1)}, bf16[22,16,128]{2,1,0:T(8,128)(2,1)S(1)}, u32[]{:S(2)}, u32[]{:S(2)}) collective-permute-start(bf16[22,16,128]{2,1,0:T(8,128)(2,1)S(1)} %get-tuple-element.107), channel_id=1, source_target_pairs={{0,12},{1,13},{2,14},{3,15},{4,8},{5,9},{6,10},{7,11},{8,4},{9,5},... | collective-permute-start | bytes 270344 | tf_op jit(solution)/shard_map/ppermute | solution.py:868
  60.6 4.2 %collective-permute-done.12.refs_0_ = bf16[22,16,128]{2,1,0:T(8,128)(2,1)S(1)} collective-permute-done((bf16[22,16,128]{2,1,0:T(8,128)(2,1)S(1)}, bf16[22,16,128]{2,1,0:T(8,128)(2,1)S(1)}, u32[]{:S(2)}, u32[]{:S(2)}) %collective-permute-start.12) | collective-permute-done | bytes 90144 | tf_op jit(solution)/shard_map/ppermute | solution.py:868
  65.0 2.2 %collective-permute-start.17 = (bf16[21,16,128]{2,1,0:T(8,128)(2,1)S(1)}, bf16[21,16,128]{2,1,0:T(8,128)(2,1)S(1)}, u32[]{:S(2)}, u32[]{:S(2)}) collective-permute-start(bf16[21,16,128]{2,1,0:T(8,128)(2,1)S(1)} %get-tuple-element.110.refs_0_.refs_1_), channel_id=1, source_target_pairs={{0,12},{1,13},{2,14},{3,15},{4,8},{5,9},{6,10},{7,11},{8,4},{9,5},... | collective-permute-start | bytes 258056 | tf_op jit(solution)/shard_map/ppermute | solution.py:868
  67.3 2.1 %collective-permute-start.15 = (bf16[21,16,128]{2,1,0:T(8,128)(2,1)S(1)}, bf16[21,16,128]{2,1,0:T(8,128)(2,1)S(1)}, u32[]{:S(2)}, u32[]{:S(2)}) collective-permute-start(bf16[21,16,128]{2,1,0:T(8,128)(2,1)S(1)} %get-tuple-element.110.refs_0_.refs_1_), channel_id=1, source_target_pairs={{0,8},{1,9},{2,10},{3,11},{4,12},{5,13},{6,14},{7,15},{8,0},{9,1},... | collective-permute-start | bytes 258056 | tf_op jit(solution)/shard_map/ppermute | solution.py:868
  71.5 1.8 %collective-permute-done.16.refs_2_.refs_3_ = bf16[21,16,128]{2,1,0:T(8,128)(2,1)S(1)} collective-permute-done((bf16[21,16,128]{2,1,0:T(8,128)(2,1)S(1)}, bf16[21,16,128]{2,1,0:T(8,128)(2,1)S(1)}, u32[]{:S(2)}, u32[]{:S(2)}) %collective-permute-start.16) | collective-permute-done | bytes 86048 | tf_op jit(solution)/shard_map/ppermute | solution.py:868
  73.3 1.4 %collective-permute-start.18 = (bf16[40,16,128]{2,1,0:T(8,128)(2,1)S(1)}, bf16[40,16,128]{2,1,0:T(8,128)(2,1)S(1)}, u32[]{:S(2)}, u32[]{:S(2)}) collective-permute-start(bf16[40,16,128]{2,1,0:T(8,128)(2,1)S(1)} %get-tuple-element.116.refs_0_), channel_id=1, source_target_pairs={{0,1},{1,0},{2,3},{3,2},{4,5},{5,4},{6,7},{7,6},{8,9},{9,8},{10,11... | collective-permute-start | bytes 491528 | tf_op jit(solution)/shard_map/ppermute | solution.py:868
  74.7 1.5 %collective-permute-start.20 = (bf16[44,16,128]{2,1,0:T(8,128)(2,1)S(1)}, bf16[44,16,128]{2,1,0:T(8,128)(2,1)S(1)}, u32[]{:S(2)}, u32[]{:S(2)}) collective-permute-start(bf16[44,16,128]{2,1,0:T(8,128)(2,1)S(1)} %get-tuple-element.117.refs_0_), channel_id=1, source_target_pairs={{0,2},{1,3},{2,0},{3,1},{4,6},{5,7},{6,4},{7,5},{8,10},{9,11},{10,... | collective-permute-start | bytes 540680 | tf_op jit(solution)/shard_map/ppermute | solution.py:868
  76.4 2.3 %collective-permute-done.18.refs_1_.refs_5_ = bf16[40,16,128]{2,1,0:T(8,128)(2,1)S(1)} collective-permute-done((bf16[40,16,128]{2,1,0:T(8,128)(2,1)S(1)}, bf16[40,16,128]{2,1,0:T(8,128)(2,1)S(1)}, u32[]{:S(2)}, u32[]{:S(2)}) %collective-permute-start.18) | collective-permute-done | bytes 163872 | tf_op jit(solution)/shard_map/ppermute | solution.py:868
  78.7 1.5 %collective-permute-start.19 = (bf16[80,16,128]{2,1,0:T(8,128)(2,1)S(1)}, bf16[80,16,128]{2,1,0:T(8,128)(2,1)S(1)}, u32[]{:S(2)}, u32[]{:S(2)}) collective-permute-start(bf16[80,16,128]{2,1,0:T(8,128)(2,1)S(1)} %together.2), channel_id=1, source_target_pairs={{0,2},{1,3},{2,0},{3,1},{4,6},{5,7},{6,4},{7,5},{8,10},{9,11},{10,... | collective-permute-start | bytes 983048 | tf_op jit(solution)/shard_map/ppermute | solution.py:868
  83.5 1.3 %broadcast_select_fusion = f32[1,2,1,196,216]{4,2,3,1,0:T(1,128)} fusion(pred[]{:T(512)S(6)} %eq.3, f32[1,1,1,196,216]{4,2,3,1,0:T(1,128)S(1)} %stack.38, f32[1,1,1,196,216]{4,2,3,1,0:T(1,128)S(1)} %stack.37, f32[1,1,1,196,216]{4,2,3,1,0:T(1,128)S(1)} %stack.40), kind=kLoop, calls=%fused_computation | loop fusion | flops 254016 | bytes 846721 | tf_op jit(solution)/shard_map/jit(_where)/select_n | solution.py:1119
  85.0 2.2 %collective-permute-done.19.refs_6_ = bf16[80,16,128]{2,1,0:T(8,128)(2,1)S(1)} collective-permute-done((bf16[80,16,128]{2,1,0:T(8,128)(2,1)S(1)}, bf16[80,16,128]{2,1,0:T(8,128)(2,1)S(1)}, u32[]{:S(2)}, u32[]{:S(2)}) %collective-permute-start.19) | collective-permute-done | bytes 327712 | tf_op jit(solution)/shard_map/ppermute | solution.py:868
  89.0 1.6 %collective-permute-done.24.refs_7_ = bf16[80,16,128]{2,1,0:T(8,128)(2,1)S(1)} collective-permute-done((bf16[80,16,128]{2,1,0:T(8,128)(2,1)S(1)}, bf16[80,16,128]{2,1,0:T(8,128)(2,1)S(1)}, u32[]{:S(2)}, u32[]{:S(2)}) %collective-permute-start.24) | collective-permute-done | bytes 327712 | tf_op jit(solution)/shard_map/ppermute | solution.py:868
  91.1 4.8 %unpack.1 = (f32[216,1296]{1,0:T(8,128)}, f32[1296]{0:T(1024)}, f32[1296]{0:T(1024)}, f32[9,1296]{1,0:T(8,128)}, f32[324,1296]{1,0:T(8,128)}, /*index=5*/f32[324...) custom-call(bf16[216,1296]{1,0:T(8,128)(2,1)S(1)} %copy-done.2, ...), custom_call_target="tpu_custom_call" | custom-call | flops 67108864 | bytes 8388608 | tf_op jit(solution)/shard_map/unpack/pallas_call | solution.py:854
  (120 shorter events, 18.9 us)
Async XLA Ops:
  4.8 5.7 %collective-permute-start.2 = (f32[3,1296]{1,0:T(4,128)S(1)}, f32[3,1296]{1,0:T(4,128)S(1)}, u32[]{:S(2)}, u32[]{:S(2)}) collective-permute-start(f32[3,1296]{1,0:T(4,128)S(1)} %get-tuple-element.89), channel_id=1, source_target_pairs={{0,3},{1,2},{2,1},{3,0},{4,7},{5,6},{6,5},{7,4},{8,11},{9,10},{10,... | collective-permute-start | bytes 46664 | tf_op jit(solution)/shard_map/ppermute | solution.py:868
  8.8 3.8 %collective-permute-start.1 = (f32[3,1296]{1,0:T(4,128)S(1)}, f32[3,1296]{1,0:T(4,128)S(1)}, u32[]{:S(2)}, u32[]{:S(2)}) collective-permute-start(f32[3,1296]{1,0:T(4,128)S(1)} %get-tuple-element.89), channel_id=1, source_target_pairs={{0,2},{1,3},{2,0},{3,1},{4,6},{5,7},{6,4},{7,5},{8,10},{9,11},{10,... | collective-permute-start | bytes 46664 | tf_op jit(solution)/shard_map/ppermute | solution.py:868
  9.3 3.8 %collective-permute-start = (f32[3,1296]{1,0:T(4,128)S(1)}, f32[3,1296]{1,0:T(4,128)S(1)}, u32[]{:S(2)}, u32[]{:S(2)}) collective-permute-start(f32[3,1296]{1,0:T(4,128)S(1)} %get-tuple-element.89), channel_id=1, source_target_pairs={{0,1},{1,0},{2,3},{3,2},{4,5},{5,4},{6,7},{7,6},{8,9},{9,8},{10,11... | collective-permute-start | bytes 46664 | tf_op jit(solution)/shard_map/ppermute | solution.py:868
  13.1 5.7 %collective-permute-start.5 = (f32[3,1296]{1,0:T(4,128)S(1)}, f32[3,1296]{1,0:T(4,128)S(1)}, u32[]{:S(2)}, u32[]{:S(2)}) collective-permute-start(f32[3,1296]{1,0:T(4,128)S(1)} %add_add_fusion.1), channel_id=1, source_target_pairs={{0,12},{1,13},{2,14},{3,15},{4,8},{5,9},{6,10},{7,11},{8,4},{9,5},... | collective-permute-start | bytes 46664 | tf_op jit(solution)/shard_map/ppermute | solution.py:868
  16.8 4.7 %collective-permute-start.4 = (f32[3,1296]{1,0:T(4,128)S(1)}, f32[3,1296]{1,0:T(4,128)S(1)}, u32[]{:S(2)}, u32[]{:S(2)}) collective-permute-start(f32[3,1296]{1,0:T(4,128)S(1)} %add_add_fusion.1), channel_id=1, source_target_pairs={{0,8},{1,9},{2,10},{3,11},{4,12},{5,13},{6,14},{7,15},{8,0},{9,1},... | collective-permute-start | bytes 46664 | tf_op jit(solution)/shard_map/ppermute | solution.py:868
  16.8 4.7 %collective-permute-start.3 = (f32[3,1296]{1,0:T(4,128)S(1)}, f32[3,1296]{1,0:T(4,128)S(1)}, u32[]{:S(2)}, u32[]{:S(2)}) collective-permute-start(f32[3,1296]{1,0:T(4,128)S(1)} %add_add_fusion.1), channel_id=1, source_target_pairs={{0,4},{1,5},{2,6},{3,7},{4,0},{5,1},{6,2},{7,3},{8,12},{9,13},{10,... | collective-permute-start | bytes 46664 | tf_op jit(solution)/shard_map/ppermute | solution.py:868
  37.8 4.3 %collective-permute-start.6 = (bf16[152,16,128]{2,1,0:T(8,128)(2,1)S(1)}, bf16[152,16,128]{2,1,0:T(8,128)(2,1)S(1)}, u32[]{:S(2)}, u32[]{:S(2)}) collective-permute-start(bf16[152,16,128]{2,1,0:T(8,128)(2,1)S(1)} %get-tuple-element.91), channel_id=1, source_target_pairs={{0,16},{16,0},{1,17},{17,1},{2,18},{18,2},{3,19},{19,3},{4,20},{20... | collective-permute-start | bytes 1867784 | tf_op jit(solution)/shard_map/ppermute | solution.py:868
  40.0 9.8 %collective-permute-start.8 = (bf16[80,16,128]{2,1,0:T(8,128)(2,1)S(1)}, bf16[80,16,128]{2,1,0:T(8,128)(2,1)S(1)}, u32[]{:S(2)}, u32[]{:S(2)}) collective-permute-start(bf16[80,16,128]{2,1,0:T(8,128)(2,1)S(1)} %get-tuple-element.96), channel_id=1, source_target_pairs={{0,2},{1,3},{2,0},{3,1},{4,6},{5,7},{6,4},{7,5},{8,10},{9,11},{10,... | collective-permute-start | bytes 983048 | tf_op jit(solution)/shard_map/ppermute | solution.py:868
  41.6 9.0 %collective-permute-start.10 = (bf16[75,16,128]{2,1,0:T(8,128)(2,1)S(1)}, bf16[75,16,128]{2,1,0:T(8,128)(2,1)S(1)}, u32[]{:S(2)}, u32[]{:S(2)}) collective-permute-start(bf16[75,16,128]{2,1,0:T(8,128)(2,1)S(1)} %get-tuple-element.100), channel_id=1, source_target_pairs={{0,1},{1,0},{2,3},{3,2},{4,5},{5,4},{6,7},{7,6},{8,9},{9,8},{10,11... | collective-permute-start | bytes 921608 | tf_op jit(solution)/shard_map/ppermute | solution.py:868
  49.9 6.1 %collective-permute-start.9 = (bf16[40,16,128]{2,1,0:T(8,128)(2,1)S(1)}, bf16[40,16,128]{2,1,0:T(8,128)(2,1)S(1)}, u32[]{:S(2)}, u32[]{:S(2)}) collective-permute-start(bf16[40,16,128]{2,1,0:T(8,128)(2,1)S(1)} %get-tuple-element.98), channel_id=1, source_target_pairs={{0,1},{1,0},{2,3},{3,2},{4,5},{5,4},{6,7},{7,6},{8,9},{9,8},{10,11... | collective-permute-start | bytes 491528 | tf_op jit(solution)/shard_map/ppermute | solution.py:868
  50.7 5.3 %collective-permute-start.11 = (bf16[39,16,128]{2,1,0:T(8,128)(2,1)S(1)}, bf16[39,16,128]{2,1,0:T(8,128)(2,1)S(1)}, u32[]{:S(2)}, u32[]{:S(2)}) collective-permute-start(bf16[39,16,128]{2,1,0:T(8,128)(2,1)S(1)} %get-tuple-element.102), channel_id=1, source_target_pairs={{0,2},{1,3},{2,0},{3,1},{4,6},{5,7},{6,4},{7,5},{8,10},{9,11},{10,... | collective-permute-start | bytes 479240 | tf_op jit(solution)/shard_map/ppermute | solution.py:868
  56.1 8.6 %collective-permute-start.12 = (bf16[22,16,128]{2,1,0:T(8,128)(2,1)S(1)}, bf16[22,16,128]{2,1,0:T(8,128)(2,1)S(1)}, u32[]{:S(2)}, u32[]{:S(2)}) collective-permute-start(bf16[22,16,128]{2,1,0:T(8,128)(2,1)S(1)} %get-tuple-element.105), channel_id=1, source_target_pairs={{0,8},{1,9},{2,10},{3,11},{4,12},{5,13},{6,14},{7,15},{8,0},{9,1},... | collective-permute-start | bytes 270344 | tf_op jit(solution)/shard_map/ppermute | solution.py:868
  58.2 6.7 %collective-permute-start.13 = (bf16[22,16,128]{2,1,0:T(8,128)(2,1)S(1)}, bf16[22,16,128]{2,1,0:T(8,128)(2,1)S(1)}, u32[]{:S(2)}, u32[]{:S(2)}) collective-permute-start(bf16[22,16,128]{2,1,0:T(8,128)(2,1)S(1)} %get-tuple-element.106), channel_id=1, source_target_pairs={{0,4},{1,5},{2,6},{3,7},{4,0},{5,1},{6,2},{7,3},{8,12},{9,13},{10,... | collective-permute-start | bytes 270344 | tf_op jit(solution)/shard_map/ppermute | solution.py:868
  58.2 6.7 %collective-permute-start.14 = (bf16[22,16,128]{2,1,0:T(8,128)(2,1)S(1)}, bf16[22,16,128]{2,1,0:T(8,128)(2,1)S(1)}, u32[]{:S(2)}, u32[]{:S(2)}) collective-permute-start(bf16[22,16,128]{2,1,0:T(8,128)(2,1)S(1)} %get-tuple-element.107), channel_id=1, source_target_pairs={{0,12},{1,13},{2,14},{3,15},{4,8},{5,9},{6,10},{7,11},{8,4},{9,5},... | collective-permute-start | bytes 270344 | tf_op jit(solution)/shard_map/ppermute | solution.py:868
  65.0 6.5 %collective-permute-start.17 = (bf16[21,16,128]{2,1,0:T(8,128)(2,1)S(1)}, bf16[21,16,128]{2,1,0:T(8,128)(2,1)S(1)}, u32[]{:S(2)}, u32[]{:S(2)}) collective-permute-start(bf16[21,16,128]{2,1,0:T(8,128)(2,1)S(1)} %get-tuple-element.110.refs_0_.refs_1_), channel_id=1, source_target_pairs={{0,12},{1,13},{2,14},{3,15},{4,8},{5,9},{6,10},{7,11},{8,4},{9,5},... | collective-permute-start | bytes 258056 | tf_op jit(solution)/shard_map/ppermute | solution.py:868
  67.1 6.1 %collective-permute-start.16 = (bf16[21,16,128]{2,1,0:T(8,128)(2,1)S(1)}, bf16[21,16,128]{2,1,0:T(8,128)(2,1)S(1)}, u32[]{:S(2)}, u32[]{:S(2)}) collective-permute-start(bf16[21,16,128]{2,1,0:T(8,128)(2,1)S(1)} %get-tuple-element.110.refs_0_.refs_1_), channel_id=1, source_target_pairs={{0,4},{1,5},{2,6},{3,7},{4,0},{5,1},{6,2},{7,3},{8,12},{9,13},{10,... | collective-permute-start | bytes 258056 | tf_op jit(solution)/shard_map/ppermute | solution.py:868
  67.3 6.0 %collective-permute-start.15 = (bf16[21,16,128]{2,1,0:T(8,128)(2,1)S(1)}, bf16[21,16,128]{2,1,0:T(8,128)(2,1)S(1)}, u32[]{:S(2)}, u32[]{:S(2)}) collective-permute-start(bf16[21,16,128]{2,1,0:T(8,128)(2,1)S(1)} %get-tuple-element.110.refs_0_.refs_1_), channel_id=1, source_target_pairs={{0,8},{1,9},{2,10},{3,11},{4,12},{5,13},{6,14},{7,15},{8,0},{9,1},... | collective-permute-start | bytes 258056 | tf_op jit(solution)/shard_map/ppermute | solution.py:868
  73.3 5.4 %collective-permute-start.18 = (bf16[40,16,128]{2,1,0:T(8,128)(2,1)S(1)}, bf16[40,16,128]{2,1,0:T(8,128)(2,1)S(1)}, u32[]{:S(2)}, u32[]{:S(2)}) collective-permute-start(bf16[40,16,128]{2,1,0:T(8,128)(2,1)S(1)} %get-tuple-element.116.refs_0_), channel_id=1, source_target_pairs={{0,1},{1,0},{2,3},{3,2},{4,5},{5,4},{6,7},{7,6},{8,9},{9,8},{10,11... | collective-permute-start | bytes 491528 | tf_op jit(solution)/shard_map/ppermute | solution.py:868
  74.7 6.2 %collective-permute-start.20 = (bf16[44,16,128]{2,1,0:T(8,128)(2,1)S(1)}, bf16[44,16,128]{2,1,0:T(8,128)(2,1)S(1)}, u32[]{:S(2)}, u32[]{:S(2)}) collective-permute-start(bf16[44,16,128]{2,1,0:T(8,128)(2,1)S(1)} %get-tuple-element.117.refs_0_), channel_id=1, source_target_pairs={{0,2},{1,3},{2,0},{3,1},{4,6},{5,7},{6,4},{7,5},{8,10},{9,11},{10,... | collective-permute-start | bytes 540680 | tf_op jit(solution)/shard_map/ppermute | solution.py:868
  76.3 5.8 %collective-permute-start.22 = (bf16[196,216]{1,0:T(8,128)(2,1)S(1)}, bf16[196,216]{1,0:T(8,128)(2,1)S(1)}, u32[]{:S(2)}, u32[]{:S(2)}) collective-permute-start(bf16[196,216]{1,0:T(8,128)(2,1)S(1)} %broadcast_select_fusion.2), channel_id=1, source_target_pairs={{0,16},{16,0},{1,17},{17,1},{2,18},{18,2},{3,19},{19,3},{4,20},{20... | collective-permute-start | bytes 254024 | tf_op jit(solution)/shard_map/ppermute | solution.py:868
  78.7 8.5 %collective-permute-start.19 = (bf16[80,16,128]{2,1,0:T(8,128)(2,1)S(1)}, bf16[80,16,128]{2,1,0:T(8,128)(2,1)S(1)}, u32[]{:S(2)}, u32[]{:S(2)}) collective-permute-start(bf16[80,16,128]{2,1,0:T(8,128)(2,1)S(1)} %together.2), channel_id=1, source_target_pairs={{0,2},{1,3},{2,0},{3,1},{4,6},{5,7},{6,4},{7,5},{8,10},{9,11},{10,... | collective-permute-start | bytes 983048 | tf_op jit(solution)/shard_map/ppermute | solution.py:868
  81.0 7.5 %collective-permute-start.21 = (bf16[88,16,128]{2,1,0:T(8,128)(2,1)S(1)}, bf16[88,16,128]{2,1,0:T(8,128)(2,1)S(1)}, u32[]{:S(2)}, u32[]{:S(2)}) collective-permute-start(bf16[88,16,128]{2,1,0:T(8,128)(2,1)S(1)} %together.3), channel_id=1, source_target_pairs={{0,1},{1,0},{2,3},{3,2},{4,5},{5,4},{6,7},{7,6},{8,9},{9,8},{10,11... | collective-permute-start | bytes 1081352 | tf_op jit(solution)/shard_map/ppermute | solution.py:868
  84.8 5.9 %collective-permute-start.26 = (bf16[88,16,128]{2,1,0:T(8,128)(2,1)S(1)}, bf16[88,16,128]{2,1,0:T(8,128)(2,1)S(1)}, u32[]{:S(2)}, u32[]{:S(2)}) collective-permute-start(bf16[88,16,128]{2,1,0:T(8,128)(2,1)S(1)} %together.3), channel_id=1, source_target_pairs={{0,16},{16,0},{1,17},{17,1},{2,18},{18,2},{3,19},{19,3},{4,20},{20... | collective-permute-start | bytes 1081352 | tf_op jit(solution)/shard_map/ppermute | solution.py:868
  88.5 2.6 %collective-permute-start.27 = (bf16[88,16,128]{2,1,0:T(8,128)(2,1)S(1)}, bf16[88,16,128]{2,1,0:T(8,128)(2,1)S(1)}, u32[]{:S(2)}, u32[]{:S(2)}) collective-permute-start(bf16[88,16,128]{2,1,0:T(8,128)(2,1)S(1)} %collective-permute-done.21.refs_10_), channel_id=1, source_target_pairs={{0,16},{16,0},{1,17},{17,1},{2,18},{18,2},{3,19},{19,3},{4,20},{20... | collective-permute-start | bytes 1081352 | tf_op jit(solution)/shard_map/ppermute | solution.py:868
  (32 other events, 444.5 us)
